TPU v7x, 512 devices: a whole 4x8x8 slice. The times are simulated.
512 devices in a mesh: wide: 128 (over y, z, core), narrow: 4 (over x).
Axes of the slice: x: 4, y: 8, z: 8, core: 2. Of those that a mesh axis runs over, the one named last changes fastest.
Arguments:
- coords: float32 [1536, 3, 512], P(('wide', 'narrow')), may hold values from 0 to 64, as said below
- noise_var: float32 [1536, 512], P(('wide', 'narrow')), may hold values from 1 to 2
- observed: float32 [1536, 512], P(('wide', 'narrow')), may hold values from -16 to 16
- warm_start: float32 [1536, 512], P(('wide', 'narrow')), may hold values from -3 to 3
- leaf_basis: bfloat16 [1536, 512, 64], P(('wide', 'narrow')), may hold values from -0.25 to 0.25
- leaf_transfer: bfloat16 [1536, 64, 64], P(('wide', 'narrow')), may hold values from -0.21875 to 0.21875
- leaf_coupling: bfloat16 [1536, 8, 64, 64], P(('wide', 'narrow')), may hold values from -0.25 to 0.25
- group_coupling: bfloat16 [128, 6, 64, 64], P('wide'), may hold values from -0.3125 to 0.3125
- top_transfer: bfloat16 [128, 64, 64], replicated, may hold values from -0.375 to 0.375
- top_coupling: bfloat16 [16, 4, 64, 64], replicated, may hold values from -0.375 to 0.375
- near_list: int32 [1536, 4], P(('wide', 'narrow')), may hold values from 0 to 1535, as said below
- near_count: int32 [1536], P(('wide', 'narrow')), may hold values from 1 to 4, as said below
- far_list: int32 [1536, 8], P(('wide', 'narrow')), may hold values from 0 to 1535, as said below
- far_count: int32 [1536], P(('wide', 'narrow')), may hold values from 1 to 8, as said below
- group_far: int32 [128, 6], P('wide'), may hold values from 0 to 127, as said below
- parent: int32 [128], replicated, may hold values from 0 to 15, never falling along the last dimension, each value on 1 to 16 neighbouring positions
- top_far: int32 [16, 4], replicated, may hold values from 0 to 15, as said below
Outputs:
- solution_field: float32 [1536, 512], P(('wide', 'narrow'))
- residual: float32 [1536, 512], P(('wide', 'narrow'))
Inputs may be any that keep to these rules, and one draw needn't show every extreme that they name: `coords`: coordinates in box units; leaf b's points lie near the centre of its box on the Morton curve. `near_list`: slots 0 to near_count[b] - 1 of row b are used, later slots are to be ignored; slot 0 is b itself; the entries of a row are distinct and lie in b's level-one box or in the level-one box before or after it. `near_count`: some leaf box of some device uses all 4 slots in every draw. `far_list`: slots 0 to far_count[b] - 1 of row b are used, later slots are to be ignored; the entries of a row are distinct, lie in b's own level-one box and are not in b's near list. `far_count`: some leaf box of some device uses all 8 slots in every draw. `group_far`: the entries of a row g are distinct and differ from g. `parent`: never falls along the level-one boxes; each level-two box has 1 to 16 children. `top_far`: the entries of a row p are distinct and differ from p.
All inputs are finite; a program needn't handle non-finite values.
Results may differ from a plain program's by a relative error of at most 0.0003.
Values may be sent and summed in bfloat16 or wider, within the bound.
No kernel may reach another device: no remote copies, remote signals or barrier semaphores. Data moves between devices by JAX's collectives and lax.ppermute only.
A program may use at most 64 MiB of HBM per device.

v0:
```python
import jax
import jax.numpy as jnp
from jax import lax
from jax.sharding import PartitionSpec as P

ITERS = 2


amplitude = 1.0 / 16.0
length_scale = 1.5
root_three = 1.7320508075688772
highest = lax.Precision.HIGHEST


def padded(array, sides, width):
    for axis, dim in sides:
        devices, length = (lax.axis_size(axis), array.shape[dim])
        up = [(i, (i + 1) % devices) for i in range(devices - 1)]
        down = [(j, i) for i, j in up]
        last = lax.slice_in_dim(array, length - width, length, axis=dim)
        first = lax.slice_in_dim(array, 0, width, axis=dim)
        before = lax.ppermute(last, axis, up)
        after = lax.ppermute(first, axis, down)
        array = jnp.concatenate([before, array, after], axis=dim)
    return array


def kernel_block(target, source):
    squared = jnp.zeros(target.shape[:-2] + (target.shape[-1], source.shape[-1]), jnp.float32)
    for component in range(3):
        between = target[..., component, :, None] - source[..., component, None, :]
        squared = squared + between * between
    scaled = root_three / length_scale * jnp.sqrt(squared)
    return amplitude * (1.0 + scaled) * jnp.exp(-scaled)


def local(
    coords,
    noise_var,
    observed,
    warm_start,
    leaf_basis,
    leaf_transfer,
    leaf_coupling,
    group_coupling,
    top_transfer,
    top_coupling,
    near_list,
    near_count,
    far_list,
    far_count,
    group_far,
    parent,
    top_far,
):
    leaf_count = noise_var.shape[0]
    group_len = leaf_count * lax.axis_size("narrow")
    wide_index = lax.axis_index("wide")
    near_local = near_list - (wide_index - 1) * group_len
    far_local = far_list - wide_index * group_len
    near_most = jnp.max(near_count)
    far_mask = (jnp.arange(far_list.shape[1])[None, :] < far_count[:, None]).astype(jnp.float32)
    basis_float = leaf_basis.astype(jnp.float32)
    transfer_float = leaf_transfer.astype(jnp.float32)
    coupling_float = leaf_coupling.astype(jnp.float32)
    group_float = group_coupling[0].astype(jnp.float32)
    top_float = top_transfer.astype(jnp.float32)
    top_pair_float = top_coupling.astype(jnp.float32)
    parent_table = (parent[:, None] == jnp.arange(top_coupling.shape[0])[None, :]).astype(
        jnp.float32
    )
    parent_row = lax.dynamic_slice_in_dim(parent_table, wide_index, 1, 0)
    own_top_transfer = lax.dynamic_slice_in_dim(top_float, wide_index, 1, 0)[0]
    coord_group = lax.all_gather(coords, "narrow", axis=0, tiled=True)
    coord_window = padded(coord_group, (("wide", 0),), group_len)

    def near_terms(field_window):

        def add_slot(slot_index, totals):
            sources = near_local[:, slot_index]
            source_points = jnp.take(coord_window, sources, axis=0, mode="clip")
            weights_on = (slot_index < near_count).astype(jnp.float32)
            source_values = (
                jnp.take(field_window, sources, axis=0, mode="clip") * weights_on[:, None]
            )
            kernel_tile = kernel_block(coords, source_points)
            return totals + jnp.einsum("bij,bj->bi", kernel_tile, source_values, precision=highest)

        return lax.fori_loop(0, near_most, add_slot, jnp.zeros_like(observed))

    def operator_apply(values):
        coefficients = jnp.einsum("bpr,bp->br", basis_float, values, precision=highest)
        field_group, coef_group = (
            lax.all_gather(values, "narrow", axis=0, tiled=True),
            lax.all_gather(coefficients, "narrow", axis=0, tiled=True),
        )
        field_window = padded(field_group, (("wide", 0),), group_len)
        partial_coef = jnp.einsum("crs,cr->s", transfer_float, coefficients, precision=highest)
        own_coef = lax.psum(partial_coef, "narrow")
        all_coef = lax.all_gather(own_coef[None, :], "wide", axis=0, tiled=True)
        lifted = jnp.einsum("grs,gr->gs", top_float, all_coef, precision=highest)
        top_coef = jnp.dot(parent_table.T, lifted, precision=highest)
        top_in = jnp.einsum(
            "psrt,pst->pr", top_pair_float, jnp.take(top_coef, top_far, axis=0), precision=highest
        )
        down_top = jnp.dot(parent_row, top_in, precision=highest)[0]
        group_in = jnp.einsum(
            "srt,st->r", group_float, jnp.take(all_coef, group_far[0], axis=0), precision=highest
        )
        group_in = group_in + jnp.dot(own_top_transfer, down_top, precision=highest)
        far_coef = jnp.take(coef_group, far_local, axis=0, mode="clip") * far_mask[:, :, None]
        leaf_in = jnp.einsum("bsrt,bst->br", coupling_float, far_coef, precision=highest)
        leaf_in = leaf_in + jnp.einsum("brs,s->br", transfer_float, group_in, precision=highest)
        far_part = jnp.einsum("bpr,br->bp", basis_float, leaf_in, precision=highest)
        return noise_var * values + near_terms(field_window) + far_part

    solution_field = warm_start
    residual = observed - operator_apply(warm_start)

    def squares(vector):
        return lax.psum(jnp.sum(vector * vector), ("wide", "narrow"))

    direction = residual
    norm_now = squares(residual)
    for iteration in range(ITERS):
        mapped = operator_apply(direction)
        step_size = norm_now / lax.psum(jnp.sum(direction * mapped), ("wide", "narrow"))
        solution_field = solution_field + step_size * direction
        residual = residual - step_size * mapped
        norm_next = squares(residual)
        direction = residual + norm_next / norm_now * direction
        norm_now = norm_next
    return (solution_field, residual)


def solution(mesh):
    placed = (
        P(("wide", "narrow"), None, None),
        P(("wide", "narrow"), None),
        P(("wide", "narrow"), None),
        P(("wide", "narrow"), None),
        P(("wide", "narrow"), None, None),
        P(("wide", "narrow"), None, None),
        P(("wide", "narrow"), None, None, None),
        P("wide", None, None, None),
        P(),
        P(),
        P(("wide", "narrow"), None),
        P(("wide", "narrow")),
        P(("wide", "narrow"), None),
        P(("wide", "narrow")),
        P("wide", None),
        P(),
        P(),
    )
    return jax.shard_map(
        local,
        mesh=mesh,
        in_specs=placed,
        out_specs=(P(("wide", "narrow"), None), P(("wide", "narrow"), None)),
        check_vma=False,
    )
```

profile of v0, /device:TPU:1, one launch (start us, length us, event | category | flops | bytes accessed | tf_op | source)
XLA Modules:
  0.0 747.0 jit_solution(17583717452682925119)
XLA Ops:
  0.6 10.5 %all-gather = f32[4,3,512]{2,1,0:T(4,128)S(1)} all-gather(f32[1,3,512]{2,1,0:T(4,128)} %bitcast.352), channel_id=1, replica_groups=mesh['wide'=128,'narrow'=4] {'narrow'}, dimensions={0}, use_global_device_ids=true | all-gather | bytes 30720 | tf_op jit(solution)/shard_map/all_gather | solution.py:94
  11.2 10.5 %collective-permute-start.3 = (f32[12,512]{1,0:T(8,128)S(1)}, f32[12,512]{1,0:T(8,128)}, u32[]{:S(2)}, u32[]{:S(2)}) collective-permute-start(f32[12,512]{1,0:T(8,128)S(1)} %reshape.206), channel_id=1, source_target_pairs={{4,0},{8,4},{12,8},{16,12},{20,16},{24,20},{28,24},{32,28},{36,32}... | collective-permute-start | bytes 73736 | tf_op jit(solution)/shard_map/ppermute | solution.py:23
  21.7 1.9 collective-permute-start.2
  23.6 10.0 %all_gather.30 = f32[12,3,512]{2,1,0:T(4,128)} all-gather(f32[3,3,512]{2,1,0:T(4,128)} %param.27), channel_id=1, replica_groups=mesh['wide'=128,'narrow'=4] {'narrow'}, dimensions={0}, use_global_device_ids=true | all-gather | bytes 92160 | tf_op jit(solution)/shard_map/all_gather | solution.py:74
  33.6 5.9 collective-permute-start.1
  39.5 1.9 collective-permute-start
  47.7 7.1 psum.49
  57.1 8.1 %all-gather.1 = f32[4,3,64]{2,1,0:T(4,128)S(1)} all-gather(f32[1,3,64]{2,1,0:T(4,128)S(1)} %bitcast.364), channel_id=1, replica_groups=mesh['wide'=128,'narrow'=4] {'narrow'}, dimensions={0}, use_global_device_ids=true | all-gather | bytes 3840 | tf_op jit(solution)/shard_map/all_gather | solution.py:95
  65.2 1.3 iota_compare_fusion
  66.5 50.6 %all-gather.2 = f32[128,1,64]{2,1,0:T(1,128)S(1)} all-gather(f32[1,1,64]{2,1,0:T(1,128)S(1)} %bitcast.372), channel_id=1, replica_groups=mesh['wide'=128,'narrow'=4] {'wide'}, dimensions={0}, use_global_device_ids=true | all-gather | bytes 33024 | tf_op jit(solution)/shard_map/all_gather | solution.py:100
  117.1 3.9 copy.41
  121.1 1.7 fusion.100
  124.5 1.6 convolution_bitcast_fusion.10
  130.2 1.4 fusion.149
  133.0 1.4 reduce_max.9
  138.6 43.4 %while.30 = (s32[]{:T(128)}, f32[3,512]{1,0:T(4,128)S(1)}, s32[]{:T(128)}, f32[3,3,512]{2,1,0:T(4,128)S(1)}, s32[3,4]{0,1:T(4,128)}, /*index=5*/f32[36,3,512]{2,...) while((s32[]{:T(128)}, f32[3,512]{1,0:T(4,128)S(1)}, ...), condition=%wide.region_2.3_spmd, body=%wide.region_1.0_spmd.sunk | while | flops 19664908 | bytes 297243 | solution.py:89
  141.9 1.7 gather_fusion
  143.6 5.7 fusion.216
  152.6 1.7 gather_fusion
  154.3 5.7 fusion.216
  163.3 1.7 gather_fusion
  165.0 5.7 fusion.216
  174.0 1.7 gather_fusion
  175.7 5.7 fusion.216
  182.9 9.0 %all-gather.3 = f32[4,3,512]{2,1,0:T(4,128)S(1)} all-gather(f32[1,3,512]{2,1,0:T(4,128)S(1)} %bitcast.342), channel_id=1, replica_groups=mesh['wide'=128,'narrow'=4] {'narrow'}, dimensions={0}, use_global_device_ids=true | all-gather | bytes 30720 | tf_op jit(solution)/shard_map/all_gather | solution.py:94
  191.9 1.9 collective-permute-start.5
  193.8 5.2 collective-permute-start.4
  199.5 6.6 psum.51
  206.1 8.1 %all-gather.4 = f32[4,3,64]{2,1,0:T(4,128)S(1)} all-gather(f32[1,3,64]{2,1,0:T(4,128)S(1)} %bitcast.366), channel_id=1, replica_groups=mesh['wide'=128,'narrow'=4] {'narrow'}, dimensions={0}, use_global_device_ids=true | all-gather | bytes 3840 | tf_op jit(solution)/shard_map/all_gather | solution.py:95
  215.5 2.0 fusion.152
  217.5 46.4 %all-gather.5 = f32[128,1,64]{2,1,0:T(1,128)S(1)} all-gather(f32[1,1,64]{2,1,0:T(1,128)} %bitcast.374), channel_id=1, replica_groups=mesh['wide'=128,'narrow'=4] {'wide'}, dimensions={0}, use_global_device_ids=true | all-gather | bytes 33024 | tf_op jit(solution)/shard_map/all_gather | solution.py:100
  264.0 2.4 fusion.98
  274.4 45.9 %while.31 = (s32[]{:T(128)}, f32[3,512]{1,0:T(4,128)S(1)}, s32[]{:T(128)}, f32[3,3,512]{2,1,0:T(4,128)S(1)}, s32[3,4]{0,1:T(4,128)}, /*index=5*/f32[36,3,512]{2,...) while((s32[]{:T(128)}, f32[3,512]{1,0:T(4,128)S(1)}, ...), condition=%wide.region_7.10_spmd, body=%wide.region_6.9_spmd.sunk | while | flops 19664908 | bytes 297243 | solution.py:89
  278.2 1.7 gather_fusion.2
  280.0 5.7 fusion.221
  289.6 1.7 gather_fusion.2
  291.3 5.7 fusion.221
  300.9 1.7 gather_fusion.2
  302.6 5.7 fusion.221
  312.2 1.7 gather_fusion.2
  313.9 5.7 fusion.221
  320.3 1.3 multiply_reduce_fusion.2
  321.6 95.1 %all-reduce = (f32[]{:T(128)}, f32[]{:T(128)}) all-reduce(f32[]{:T(128)} %get-tuple-element.137, f32[]{:T(128)} %get-tuple-element.136), channel_id=1, replica_groups=mesh['wide'=128,'narrow'=4] {'wide','narrow'}, use_global_device_ids=true, to_apply=%region_5.8 | all-reduce | flops 2 | bytes 16 | tf_op jit(solution)/shard_map/psum | solution.py:121
  418.0 1.3 multiply_reduce_fusion.1
  419.4 94.4 %psum.53 = f32[]{:T(128)} all-reduce(f32[]{:T(128)} %get-tuple-element.188), channel_id=1, replica_groups=mesh['wide'=128,'narrow'=4] {'wide','narrow'}, use_global_device_ids=true, to_apply=%region_12.15 | all-reduce | flops 1 | bytes 8 | tf_op jit(solution)/shard_map/psum | solution.py:121
  515.1 9.0 %all-gather.6 = f32[4,3,512]{2,1,0:T(4,128)S(1)} all-gather(f32[1,3,512]{2,1,0:T(4,128)S(1)} %bitcast.350), channel_id=1, replica_groups=mesh['wide'=128,'narrow'=4] {'narrow'}, dimensions={0}, use_global_device_ids=true | all-gather | bytes 30720 | tf_op jit(solution)/shard_map/all_gather | solution.py:94
  524.1 5.5 collective-permute-start.7
  529.6 2.5 collective-permute-start.6
  532.6 7.9 %psum.54 = f32[1,64]{1,0:T(1,128)} all-reduce(f32[1,64]{1,0:T(1,128)S(1)} %convolution_bitcast_fusion.7), channel_id=1, replica_groups=mesh['wide'=128,'narrow'=4] {'narrow'}, use_global_device_ids=true, to_apply=%region_15.18 | all-reduce | flops 64 | bytes 512 | tf_op jit(solution)/shard_map/psum | solution.py:99
  540.4 8.1 %all-gather.7 = f32[4,3,64]{2,1,0:T(4,128)S(1)} all-gather(f32[1,3,64]{2,1,0:T(4,128)S(1)} %bitcast.368), channel_id=1, replica_groups=mesh['wide'=128,'narrow'=4] {'narrow'}, dimensions={0}, use_global_device_ids=true | all-gather | bytes 3840 | tf_op jit(solution)/shard_map/all_gather | solution.py:95
  549.9 2.0 fusion.155
  551.9 47.9 %all-gather.8 = f32[128,1,64]{2,1,0:T(1,128)S(1)} all-gather(f32[1,1,64]{2,1,0:T(1,128)} %bitcast.373), channel_id=1, replica_groups=mesh['wide'=128,'narrow'=4] {'wide'}, dimensions={0}, use_global_device_ids=true | all-gather | bytes 33024 | tf_op jit(solution)/shard_map/all_gather | solution.py:100
  599.8 2.4 fusion.96
  603.5 1.6 convolution_bitcast_fusion.6
  611.4 39.3 %while.32 = (s32[]{:T(128)}, f32[3,512]{1,0:T(4,128)S(1)}, s32[]{:T(128)}, f32[3,3,512]{2,1,0:T(4,128)S(1)}, s32[3,4]{0,1:T(4,128)}, /*index=5*/f32[36,3,512]{2,...) while((s32[]{:T(128)}, f32[3,512]{1,0:T(4,128)S(1)}, ...), condition=%wide.region_14.17_spmd, body=%wide.region_13.16_spmd.sunk | while | flops 19664908 | bytes 280831 | solution.py:89
  614.1 1.5 gather_fusion.4
  615.6 5.4 fusion.226
  623.7 1.5 gather_fusion.4
  625.3 5.4 fusion.226
  633.4 1.5 gather_fusion.4
  635.0 5.4 fusion.226
  643.1 1.5 gather_fusion.4
  644.7 5.4 fusion.226
  651.4 93.7 %psum.55 = f32[]{:T(128)} all-reduce(f32[]{:T(128)} %multiply_reduce_fusion), channel_id=1, replica_groups=mesh['wide'=128,'narrow'=4] {'wide','narrow'}, use_global_device_ids=true, to_apply=%region_17.20 | all-reduce | flops 1 | bytes 8 | tf_op jit(solution)/shard_map/psum | solution.py:127
  (275 shorter events, 73.1 us)
Async XLA Ops:
  0.6 126.2 %copy-start = (bf16[16,4,64,64]{3,2,1,0:T(8,128)(2,1)S(1)}, bf16[16,4,64,64]{3,2,1,0:T(8,128)(2,1)}, u32[]{:S(2)}) copy-start(bf16[16,4,64,64]{3,2,1,0:T(8,128)(2,1)} %param.36) | copy-start | bytes 1572868
  11.2 123.1 %collective-permute-start.3 = (f32[12,512]{1,0:T(8,128)S(1)}, f32[12,512]{1,0:T(8,128)}, u32[]{:S(2)}, u32[]{:S(2)}) collective-permute-start(f32[12,512]{1,0:T(8,128)S(1)} %reshape.206), channel_id=1, source_target_pairs={{4,0},{8,4},{12,8},{16,12},{20,16},{24,20},{28,24},{32,28},{36,32}... | collective-permute-start | bytes 73736 | tf_op jit(solution)/shard_map/ppermute | solution.py:23
  21.7 112.6 %collective-permute-start.2 = (f32[12,512]{1,0:T(8,128)S(1)}, f32[12,512]{1,0:T(8,128)}, u32[]{:S(2)}, u32[]{:S(2)}) collective-permute-start(f32[12,512]{1,0:T(8,128)S(1)} %reshape.206), channel_id=1, source_target_pairs={{0,4},{4,8},{8,12},{12,16},{16,20},{20,24},{24,28},{28,32},{32,36}... | collective-permute-start | bytes 73736 | tf_op jit(solution)/shard_map/ppermute | solution.py:22
  33.6 103.4 %collective-permute-start.1 = (f32[12,3,512]{2,1,0:T(4,128)}, f32[12,3,512]{2,1,0:T(4,128)}, u32[]{:S(2)}, u32[]{:S(2)}) collective-permute-start(f32[12,3,512]{2,1,0:T(4,128)} %all_gather.30), channel_id=1, source_target_pairs={{4,0},{8,4},{12,8},{16,12},{20,16},{24,20},{28,24},{32,28},{36,32}... | collective-permute-start | bytes 221192 | tf_op jit(solution)/shard_map/ppermute | solution.py:23
  39.5 95.6 %collective-permute-start = (f32[12,3,512]{2,1,0:T(4,128)}, f32[12,3,512]{2,1,0:T(4,128)}, u32[]{:S(2)}, u32[]{:S(2)}) collective-permute-start(f32[12,3,512]{2,1,0:T(4,128)} %all_gather.30), channel_id=1, source_target_pairs={{0,4},{4,8},{8,12},{12,16},{16,20},{20,24},{24,28},{28,32},{32,36}... | collective-permute-start | bytes 221192 | tf_op jit(solution)/shard_map/ppermute | solution.py:22
  44.8 81.9 %copy-start.12 = (pred[16,4]{1,0:T(8,128)(4,1)}, pred[16,4]{1,0:T(8,128)(4,1)S(1)}, u32[]{:S(2)}) copy-start(pred[16,4]{1,0:T(8,128)(4,1)S(1)} %copy.42) | copy-start | bytes 196
  55.5 74.6 %copy-start.15 = (f32[3,8]{1,0:T(4,128)}, f32[3,8]{1,0:T(4,128)S(1)}, u32[]{:S(2)}) copy-start(f32[3,8]{1,0:T(4,128)S(1)} %fusion.127) | copy-start | bytes 292
  56.3 73.2 %copy-start.16 = (s32[1024]{0:T(1024)}, s32[1024]{0:T(1024)S(1)}, u32[]{:S(2)}) copy-start(s32[1024]{0:T(1024)S(1)} %pad_clamp_fusion.5) | copy-start | bytes 12292
  57.0 69.0 %copy-start.6 = (s32[1024]{0:T(1024)}, s32[1024]{0:T(1024)S(1)}, u32[]{:S(2)}) copy-start(s32[1024]{0:T(1024)S(1)} %pad_clamp_fusion.3) | copy-start | bytes 12292
  117.1 5.7 copy-start.17
  121.0 8.2 %copy-start.4 = (bf16[3,64,64]{2,1,0:T(8,128)(2,1)S(1)}, bf16[3,64,64]{2,1,0:T(8,128)(2,1)}, u32[]{:S(2)}) copy-start(bf16[3,64,64]{2,1,0:T(8,128)(2,1)} %param.32) | copy-start | bytes 73732
  121.1 10.5 %copy-start.2 = (bf16[3,512,64]{1,2,0:T(8,128)(2,1)S(1)}, bf16[3,512,64]{1,2,0:T(8,128)(2,1)}, u32[]{:S(2)}) copy-start(bf16[3,512,64]{1,2,0:T(8,128)(2,1)} %param.31) | copy-start | bytes 589828
  122.8 15.8 %copy-start.1 = (f32[3,3,512]{2,1,0:T(4,128)S(1)}, f32[3,3,512]{2,1,0:T(4,128)}, u32[]{:S(2)}) copy-start(f32[3,3,512]{2,1,0:T(4,128)} %param.27) | copy-start | bytes 55300
  137.9 0.7 copy-start.3
  140.6 1.3 copy-start.9
  151.3 1.3 copy-start.9
  162.0 1.3 copy-start.9
  172.7 1.3 copy-start.9
  182.1 84.9 %copy-start.19 = (pred[6]{0:T(512)(128)(4,1)S(1)}, pred[6]{0:T(512)(128)(4,1)}, u32[]{:S(2)}) copy-start(pred[6]{0:T(512)(128)(4,1)} %compare_and_fusion.1) | copy-start | bytes 22
  182.1 86.0 %copy-start.18 = (s32[128]{0:T(128)S(1)}, s32[128]{0:T(128)}, u32[]{:S(2)}) copy-start(s32[128]{0:T(128)} %param.42) | copy-start | bytes 1540
  182.1 87.2 %copy-start.7 = (s32[1024]{0:T(1024)S(1)}, s32[1024]{0:T(1024)}, u32[]{:S(2)}) copy-start(s32[1024]{0:T(1024)} %copy-done.6) | copy-start | bytes 12292
  182.1 87.8 %copy-start.13 = (pred[16,4]{1,0:T(8,128)(4,1)S(1)}, pred[16,4]{1,0:T(8,128)(4,1)}, u32[]{:S(2)}) copy-start(pred[16,4]{1,0:T(8,128)(4,1)} %copy-done.12) | copy-start | bytes 196
  191.9 81.7 %collective-permute-start.5 = (f32[12,512]{1,0:T(8,128)S(1)}, f32[12,512]{1,0:T(8,128)}, u32[]{:S(2)}, u32[]{:S(2)}) collective-permute-start(f32[12,512]{1,0:T(8,128)S(1)} %reshape.212), channel_id=1, source_target_pairs={{4,0},{8,4},{12,8},{16,12},{20,16},{24,20},{28,24},{32,28},{36,32}... | collective-permute-start | bytes 73736 | tf_op jit(solution)/shard_map/ppermute | solution.py:23
  193.8 79.7 %collective-permute-start.4 = (f32[12,512]{1,0:T(8,128)S(1)}, f32[12,512]{1,0:T(8,128)}, u32[]{:S(2)}, u32[]{:S(2)}) collective-permute-start(f32[12,512]{1,0:T(8,128)S(1)} %reshape.212), channel_id=1, source_target_pairs={{0,4},{4,8},{8,12},{12,16},{16,20},{20,24},{24,28},{28,32},{32,36}... | collective-permute-start | bytes 73736 | tf_op jit(solution)/shard_map/ppermute | solution.py:22
  276.4 1.3 copy-start.10
  287.7 1.3 copy-start.10
  299.0 1.3 copy-start.10
  310.3 1.3 copy-start.10
  320.2 286.0 %copy-start.8 = (s32[1024]{0:T(1024)S(1)}, s32[1024]{0:T(1024)}, u32[]{:S(2)}) copy-start(s32[1024]{0:T(1024)} %copy-done.6) | copy-start | bytes 12292
  320.3 286.6 %copy-start.14 = (pred[16,4]{1,0:T(8,128)(4,1)S(1)}, pred[16,4]{1,0:T(8,128)(4,1)}, u32[]{:S(2)}) copy-start(pred[16,4]{1,0:T(8,128)(4,1)} %copy-done.12) | copy-start | bytes 196
  524.1 86.4 %collective-permute-start.7 = (f32[12,512]{1,0:T(8,128)S(1)}, f32[12,512]{1,0:T(8,128)}, u32[]{:S(2)}, u32[]{:S(2)}) collective-permute-start(f32[12,512]{1,0:T(8,128)S(1)} %reshape.218), channel_id=1, source_target_pairs={{4,0},{8,4},{12,8},{16,12},{20,16},{24,20},{28,24},{32,28},{36,32}... | collective-permute-start | bytes 73736 | tf_op jit(solution)/shard_map/ppermute | solution.py:23
  529.6 81.0 %collective-permute-start.6 = (f32[12,512]{1,0:T(8,128)S(1)}, f32[12,512]{1,0:T(8,128)}, u32[]{:S(2)}, u32[]{:S(2)}) collective-permute-start(f32[12,512]{1,0:T(8,128)S(1)} %reshape.218), channel_id=1, source_target_pairs={{0,4},{4,8},{8,12},{12,16},{16,20},{20,24},{24,28},{28,32},{32,36}... | collective-permute-start | bytes 73736 | tf_op jit(solution)/shard_map/ppermute | solution.py:22
  611.4 39.4 %copy-start.5 = (f32[3,512]{1,0:T(4,128)S(1)}, f32[3,512]{1,0:T(4,128)}, u32[]{:S(2)}) copy-start(f32[3,512]{1,0:T(4,128)} %param.28) | copy-start | bytes 18436
  611.4 135.0 %copy-start.11 = (f32[3,512]{1,0:T(4,128)S(1)}, f32[3,512]{1,0:T(4,128)}, u32[]{:S(2)}) copy-start(f32[3,512]{1,0:T(4,128)} %param.30) | copy-start | bytes 18436
where the time goes:
time: 750 us; the launch traced here: 747 us
  blocking collectives  512 us (68%)
  matrix products  98 us (13%)
  local copies, waits for them, and re-layouts  51.9 us (7%)
  starting transfers between devices  35.3 us (5%)
  other arithmetic  34.1 us (5%)
  loops' own time  10.2 us (1%)
    psum x2, blocking collectives, squares(): return lax.psum(jnp.sum(vector * vector), ('wide', 'narrow'))  190 us
    all_gather x3, blocking collectives, operator_apply(): all_coef = lax.all_gather(own_coef[None, :], 'wide', axis=0, tiled=True)  145 us
    psum x1, blocking collectives, local(): lax.psum(jnp.sum(direction * mapped), ('wide', 'narrow'))  93.7 us
    dot_general x12, matrix products, add_slot(): jnp.einsum('bij,bj->bi', kernel_tile, source_values, precision=highest)  67.2 us
    all_gather x3, blocking collectives, operator_apply(): lax.all_gather(values, 'narrow', axis=0, tiled=True)  28.6 us
    all_gather x3, blocking collectives, operator_apply(): lax.all_gather(coefficients, 'narrow', axis=0, tiled=True)  24.2 us
    ppermute x4, starting transfers between devices, padded(): after = lax.ppermute(first, axis, down)  23.7 us
    psum x3, blocking collectives, operator_apply(): own_coef = lax.psum(partial_coef, 'narrow')  21.5 us
  transfers between devices with their start and end apart: 8, of which 0 were waited for; matrix products, arithmetic and copies ran while one was open for 8% of the time, Pallas kernels for 0%

commit v1 on v0

v1 whole, which is shorter than its diff:
```python
import functools

import jax
import jax.numpy as jnp
from jax import lax
from jax.experimental import pallas as pl
from jax.experimental.pallas import tpu as pltpu
from jax.sharding import PartitionSpec as P

amplitude = 1.0 / 16.0
rate = 1.7320508075688772 / 1.5
log2_e = 1.4426950408889634
LEAVES = 3
NARROW = 4
GROUP = LEAVES * NARROW
POINTS = 512
RANK = 64
NEAR = 4
FAR = 8
FAR_GROUP = 6
FAR_TOP = 4
LANES = 128
PIECES = POINTS // LANES
FIELD = LEAVES * PIECES
PACK = FIELD + 4
COORDS = 3 * FIELD
PAIR = 2 * NARROW
WINDOW = 3 * GROUP
CHUNK = 32
VMEM = pl.BlockSpec(memory_space=pltpu.VMEM)
SMEM = pl.BlockSpec(memory_space=pltpu.SMEM)
f32 = jnp.float32


def shape(*dims, dtype=f32):
    return jax.ShapeDtypeStruct(dims, dtype)


def cost(flops, bytes_accessed):
    return pl.CostEstimate(flops=flops, bytes_accessed=bytes_accessed, transcendentals=0)


def rows_of(array):
    return lax.broadcasted_iota(jnp.int32, array.shape, 0)


def times(vectors, matrix, transposed):
    high = vectors.astype(jnp.bfloat16).astype(f32)
    rest = vectors - high
    middle = rest.astype(jnp.bfloat16).astype(f32)
    parts = jnp.concatenate([high, middle, rest - middle], axis=0).astype(jnp.bfloat16)
    dims = (((1,), (1 if transposed else 0,)), ((), ()))
    out = lax.dot_general(parts, matrix, dims, preferred_element_type=f32)
    count = vectors.shape[0]
    return out[:count] + (out[count : 2 * count] + out[2 * count :])


def row_by_leaf(terms):
    out = jnp.zeros_like(terms[0])
    for leaf, term in enumerate(terms):
        out = jnp.where(rows_of(term) == leaf, term, out)
    return out


def fold_half(row):
    return row[:, :RANK] + row[:, RANK:]


def lane_sums(product):
    total = jnp.sum(product, axis=0, keepdims=True)
    total = total[:, :128] + total[:, 128:256] + (total[:, 256:384] + total[:, 384:])
    return fold_half(total)


def pack(values, scalar, basis, transfer, packed):
    for leaf in range(LEAVES):
        for piece in range(PIECES):
            packed[0, pl.ds(leaf * PIECES + piece, 1), :] = values[
                leaf : leaf + 1, piece * LANES : (piece + 1) * LANES
            ]
    coefs = row_by_leaf([times(values, basis[leaf], True) for leaf in range(LEAVES)])
    partial = row_by_leaf([times(coefs, transfer[leaf], False) for leaf in range(LEAVES)])
    partial = jnp.sum(partial, axis=0, keepdims=True)
    empty = jnp.zeros((1, RANK), f32)
    beside = [scalar, empty, empty]
    for leaf in range(LEAVES):
        packed[0, pl.ds(FIELD + leaf, 1), :] = jnp.concatenate(
            [coefs[leaf : leaf + 1], beside[leaf]], axis=1
        )
    packed[0, pl.ds(FIELD + 3, 1), :] = jnp.concatenate([partial, empty], axis=1)
    whole = packed[0]
    for copy in range(1, PAIR):
        packed[copy] = whole


def padded(ref, scratch):
    scratch[...] = jnp.zeros(scratch.shape, f32)
    scratch[0:LEAVES, :] = ref[...]
    return scratch[...]


def begin_kernel(warm, coords, basis, transfer, packed, values, scratch):
    field = padded(warm, scratch)
    values[...] = field
    for leaf in range(LEAVES):
        for axis in range(3):
            for piece in range(PIECES):
                packed[0, pl.ds(PACK + (leaf * 3 + axis) * PIECES + piece, 1), :] = coords[
                    leaf, axis : axis + 1, piece * LANES : (piece + 1) * LANES
                ]
    pack(field, jnp.zeros((1, RANK), f32), basis, transfer, packed)


def fold_kernel(blocks, top_transfer, copies, fields):
    own = lax.rem(lax.axis_index("wide"), 2)
    sums = []
    for row in (FIELD + 3, FIELD):
        for group in range(2):
            first = group * NARROW
            line = [blocks[first + i, row : row + 1, :] for i in range(NARROW)]
            line = (line[0] + line[1]) + (line[2] + line[3])
            if row == FIELD + 3:
                partial = jnp.broadcast_to(line[:, :RANK], (8, RANK))
                lifted = times(partial, top_transfer[group], False)[:1]
                line = jnp.concatenate([line[:, :RANK], lifted], axis=1)
            sums.append(line)
    sums = jnp.concatenate(sums, axis=0)
    copies[...] = jnp.broadcast_to(sums[None], copies.shape)
    for i in range(NARROW):
        device = own * NARROW + i
        fields[i, 0:FIELD, :] = blocks[device, 0:FIELD, :]
        if fields.shape[1] > FIELD:
            fields[i, FIELD:, :] = blocks[device, PACK:, :]


def near_kernel(evaluate, *refs):
    if evaluate:
        (near_list, near_count, far_list, far_count, blocks, extra, values, noise, coupling,
         columns, tiles, base, leaf_far, window, sources, scratch, coefs, totals) = refs
    else:
        (near_list, near_count, far_list, far_count, blocks, extra, values, noise, coupling,
         tiles, base, leaf_far, window, scratch, coefs, totals) = refs
    wide = lax.axis_index("wide")
    own = lax.rem(wide, 2)
    first_group = wide - own

    for device in range(PAIR):
        for leaf in range(LEAVES):
            at = device * LEAVES + leaf
            window[at] = blocks[device, leaf * PIECES : (leaf + 1) * PIECES, :]
            if evaluate:
                rows = PACK + leaf * FIELD
                sources[at] = blocks[device, rows : rows + FIELD, :]
    for device in range(NARROW):
        for leaf in range(LEAVES):
            at = (PAIR + device) * LEAVES + leaf
            window[at] = extra[device, leaf * PIECES : (leaf + 1) * PIECES, :]
            if evaluate:
                rows = FIELD + leaf * FIELD
                sources[at] = extra[device, rows : rows + FIELD, :]

    coefs[...] = jnp.zeros(coefs.shape, f32)
    for device in range(NARROW):
        coefs[device * LEAVES : (device + 1) * LEAVES, :] = blocks[
            own * NARROW + device, FIELD : FIELD + LEAVES, :
        ]
    lane = lax.broadcasted_iota(jnp.int32, (16, LANES), 1)
    row = lax.broadcasted_iota(jnp.int32, (16, LANES), 0)
    far_rows = []
    for leaf in range(LEAVES):
        out = times(coefs[:, :RANK], coupling[leaf].reshape(FAR * RANK, RANK), True)
        total = jnp.zeros((16, LANES), f32)
        for two in range(FAR // 2):
            at = []
            for slot in (2 * two, 2 * two + 1):
                member = far_list[leaf, slot] - wide * GROUP
                at.append(jnp.where(slot < far_count[leaf], member, -1))
            listed = jnp.where(lane < RANK, at[0], at[1]) == row
            total = total + jnp.where(listed, out[:, two * LANES : (two + 1) * LANES], 0.0)
        far_rows.append(fold_half(jnp.sum(total, axis=0, keepdims=True)))
    leaf_far[...] = row_by_leaf([jnp.broadcast_to(one, (8, RANK)) for one in far_rows])

    def place(leaf, slot):
        listed = near_list[leaf, slot]
        group = lax.div(listed, GROUP)
        member = listed - group * GROUP
        turn = group - first_group
        turn = jnp.where((turn >= 0) & (turn < 2), turn, 2)
        return jnp.where(slot < near_count[leaf], turn * GROUP + member, wide * 0)

    eye = lax.broadcasted_iota(jnp.int32, (LANES, LANES), 0) == lax.broadcasted_iota(
        jnp.int32, (LANES, LANES), 1
    )
    near_rows = []
    for leaf in range(LEAVES):
        places = [place(leaf, slot) for slot in range(NEAR)]
        weights = [
            jnp.where(slot < near_count[leaf], 1.0, 0.0).astype(f32) for slot in range(NEAR)
        ]
        fields = [window[places[slot]] * weights[slot] for slot in range(NEAR)]

        def step(chunk, _):
            start = pl.multiple_of(chunk * CHUNK, CHUNK)
            acc = jnp.zeros((CHUNK, LANES), f32)
            if evaluate:
                column = columns[leaf, pl.ds(start, CHUNK), :]
                target = [
                    jnp.broadcast_to(column[:, axis : axis + 1], (CHUNK, LANES)) for axis in range(3)
                ]
            for slot in range(NEAR):
                for piece in range(PIECES):
                    cut = slice(piece * LANES, (piece + 1) * LANES)
                    if evaluate:
                        squared = None
                        for axis in range(3):
                            at = axis * PIECES + piece
                            between = target[axis] - sources[places[slot], pl.ds(at, 1), :]
                            between = between * between
                            squared = between if squared is None else squared + between
                        squared = jnp.maximum(squared, 1e-30)
                        distance = squared * lax.rsqrt(squared)
                        decay = jnp.exp2(distance * (-rate * log2_e))
                        tile = (distance * (amplitude * rate) + amplitude) * decay
                        tiles[leaf * NEAR + slot, pl.ds(start, CHUNK), cut] = tile
                    else:
                        tile = tiles[leaf * NEAR + slot, pl.ds(start, CHUNK), cut]
                    acc = acc + tile * fields[slot][piece : piece + 1, :]
            totals[pl.ds(start, CHUNK), :] = acc
            return 0

        lax.fori_loop(0, POINTS // CHUNK, step, 0)
        pieces = []
        for piece in range(PIECES):
            column = jnp.sum(totals[piece * LANES : (piece + 1) * LANES, :], axis=1, keepdims=True)
            pieces.append(jnp.sum(jnp.where(eye, column, 0.0), axis=0, keepdims=True))
        near_rows.append(jnp.concatenate(pieces, axis=1))
    near = row_by_leaf([jnp.broadcast_to(one, (8, POINTS)) for one in near_rows])
    base[...] = padded(noise, scratch) * values[...] + near


def near_apply(lists, blocks, extra, values, noise, coupling, columns, tiles):
    evaluate = tiles is None
    rows = NEAR * LEAVES
    small = [shape(8, POINTS), shape(8, RANK)]
    scratch = [pltpu.VMEM((WINDOW, PIECES, LANES), f32)]
    if evaluate:
        scratch.append(pltpu.VMEM((WINDOW, FIELD, LANES), f32))
    scratch += [
        pltpu.VMEM((8, POINTS), f32),
        pltpu.VMEM((16, LANES), f32),
        pltpu.VMEM((POINTS, LANES), f32),
    ]
    last = columns if evaluate else tiles
    return pl.pallas_call(
        functools.partial(near_kernel, evaluate),
        out_shape=([shape(rows, POINTS, POINTS)] if evaluate else []) + small,
        in_specs=[SMEM] * 4 + [VMEM] * 6,
        out_specs=[VMEM] * (3 if evaluate else 2),
        scratch_shapes=scratch,
        cost_estimate=cost(3 * 10**8 if evaluate else 10**7, 2 * 10**6),
        compiler_params=pltpu.CompilerParams(vmem_limit_bytes=(24 if evaluate else 24) << 20),
    )(*lists, blocks, extra, values, noise, coupling, last)


def far_field(rows, base, leaf_far, group_far, parent, top_far, places, group_coupling,
              own_pair, top_transfer, transfer, basis):
    wide = lax.axis_index("wide")
    count = rows.shape[0]
    at = lax.broadcasted_iota(jnp.int32, (16, count), 1)
    row = lax.broadcasted_iota(jnp.int32, (16, count), 0)
    kind = at & 3
    chosen = (row == FAR_GROUP + FAR_TOP) & (kind >= 2)
    for slot in range(FAR_GROUP):
        group = group_far[0, slot]
        spot = lax.div(group, 2) * 4 + lax.rem(group, 2)
        chosen = chosen | ((row == slot) & (at == spot))
    own_parent = parent[wide]
    for slot in range(FAR_TOP):
        box = top_far[slot, own_parent]
        chosen = chosen | ((row == FAR_GROUP + slot) & (places[...] == box))
    select = jnp.where(chosen, 1.0, 0.0).astype(jnp.bfloat16)
    gathered = rows[...]
    picked = jnp.zeros((16, LANES), f32)
    for part in range(3):
        piece = gathered.astype(jnp.bfloat16)
        gathered = gathered - piece.astype(f32)
        picked = picked + jnp.dot(select, piece, preferred_element_type=f32)

    def listed(vectors, matrices, slots, first):
        out = times(vectors, matrices[...].reshape(slots * RANK, RANK), True)
        lane = lax.broadcasted_iota(jnp.int32, (16, LANES), 1)
        line = lax.broadcasted_iota(jnp.int32, (16, LANES), 0)
        total = jnp.zeros((16, LANES), f32)
        for two in range(slots // 2):
            own = line == first + 2 * two + jnp.where(lane < RANK, 0, 1)
            total = total + jnp.where(own, out[:, two * LANES : (two + 1) * LANES], 0.0)
        return fold_half(jnp.sum(total, axis=0, keepdims=True))

    top_in = listed(picked[:, RANK:], own_pair, FAR_TOP, FAR_GROUP)
    group_in = listed(picked[:, :RANK], group_coupling, FAR_GROUP, 0)
    group_in = group_in + times(jnp.broadcast_to(top_in, (8, RANK)), top_transfer[lax.rem(wide, 2)], True)
    leaf_in = leaf_far[...] + row_by_leaf(
        [times(group_in, transfer[leaf], True) for leaf in range(LEAVES)]
    )
    far = row_by_leaf([times(leaf_in, basis[leaf], False) for leaf in range(LEAVES)])
    sums = picked[FAR_GROUP + FAR_TOP : FAR_GROUP + FAR_TOP + 1, RANK:]
    return base[...] + far, jnp.sum(sums, axis=1, keepdims=True)


def residual_kernel(*refs):
    *common, observed, packed, residual, scratch = refs
    mapped, _ = far_field(*common)
    field = padded(observed, scratch) - mapped
    residual[...] = field
    pack(field, lane_sums(field * field), common[-1], common[-2], packed)


def second_kernel(*refs):
    *common, residual, packed, first, unit, norm = refs
    mapped, norm_now = far_field(*common)
    first[...] = mapped
    field = mapped * lax.rsqrt(norm_now)
    unit[...] = field
    norm[...] = jnp.broadcast_to(norm_now, norm.shape)
    scalar = lane_sums(residual[...] * mapped)
    pack(field, scalar, common[-1], common[-2], packed)


def third_kernel(*refs):
    *common, residual, first, norm, copies, lower, lower_mapped, step, curve = refs
    mapped, bend = far_field(*common)
    norm_now = norm[:1, :1]
    size = norm_now / bend
    before, image = residual[...], first[...]
    low = before - size * image
    low_mapped = image - (size * jnp.sqrt(norm_now)) * mapped
    lower[...] = low
    lower_mapped[...] = low_mapped
    step[...] = jnp.broadcast_to(size, step.shape)
    curve[...] = jnp.broadcast_to(bend, curve.shape)
    products = [low * low, low * low_mapped, before * low_mapped + low * image]
    sums = jnp.zeros((8, RANK), f32)
    for at, product in enumerate(products):
        sums = jnp.where(rows_of(sums) == at, lane_sums(product), sums)
    sums = jnp.concatenate([sums, jnp.zeros((8, RANK), f32)], axis=1)
    copies[...] = jnp.broadcast_to(sums[None], copies.shape)


def total_kernel(blocks, copies):
    total = blocks[0]
    for device in range(1, blocks.shape[0]):
        total = total + blocks[device]
    copies[...] = jnp.broadcast_to(total[None], copies.shape)


def end_kernel(blocks, warm, residual, first, lower, lower_mapped, norm, step, curve,
               solution_field, last_residual):
    total = blocks[0]
    for device in range(1, blocks.shape[0]):
        total = total + blocks[device]
    total = jnp.sum(total, axis=1, keepdims=True)
    norm_next, bend, cross = total[0:1], total[1:2], total[2:3]
    norm_now, size = norm[:1, :1], step[:1, :1]
    ratio = norm_next / norm_now
    second = norm_next / (bend + ratio * (cross + ratio * curve[:1, :1]))
    keep = slice(0, LEAVES)
    solution_field[...] = warm[...] + size * residual[keep] + second * (
        lower[keep] + ratio * residual[keep]
    )
    last_residual[...] = lower[keep] - second * (lower_mapped[keep] + ratio * first[keep])


def simple(kernel, out_shape, in_specs, scratch=()):
    return pl.pallas_call(
        kernel,
        out_shape=out_shape,
        in_specs=in_specs,
        out_specs=[VMEM] * len(out_shape),
        scratch_shapes=list(scratch),
        cost_estimate=cost(10**6, 10**6),
        compiler_params=pltpu.CompilerParams(vmem_limit_bytes=8 << 20),
    )


def exchange(copies, stride):
    members = copies.shape[0]
    devices = lax.axis_size("wide") * lax.axis_size("narrow")
    span = members * stride
    groups = [
        [base + offset + stride * i for i in range(members)]
        for base in range(0, devices, span)
        for offset in range(stride)
    ]
    return lax.all_to_all(
        copies, ("wide", "narrow"), 0, 0, tiled=True, axis_index_groups=groups
    )


def neighbours(fields):
    wide = lax.axis_size("wide")
    across = []
    for first in range(1, wide - 1, 2):
        across += [(first, first + 1), (first + 1, first)]
    return lax.ppermute(fields, "wide", across)


def local(
    coords,
    noise_var,
    observed,
    warm_start,
    leaf_basis,
    leaf_transfer,
    leaf_coupling,
    group_coupling,
    top_transfer,
    top_coupling,
    near_list,
    near_count,
    far_list,
    far_count,
    group_far,
    parent,
    top_far,
):
    groups = parent.shape[0]
    pairs = groups // 2
    lists = (near_list, near_count, far_list, far_count)
    basis = jnp.transpose(leaf_basis, (0, 2, 1))
    columns = jnp.transpose(coords, (0, 2, 1))
    top_far = top_far.T
    places = jnp.pad(parent.reshape(pairs, 2), ((0, 0), (0, 2)), constant_values=-1)
    places = places.reshape(1, 4 * pairs)
    wide = lax.axis_index("wide")
    tops = lax.dynamic_slice_in_dim(top_transfer, wide // 2 * 2, 2, 0)
    own_pair = lax.dynamic_index_in_dim(
        top_coupling, lax.dynamic_index_in_dim(parent, wide, 0, False), 0, False
    )

    def gather(packed, values, tiles):
        blocks = exchange(packed, 1)
        copies, fields = simple(
            fold_kernel,
            [shape(pairs, 4, LANES), shape(NARROW, packed.shape[1] - 4, LANES)],
            [VMEM] * 2,
        )(blocks, tops)
        extra = neighbours(fields)
        rows = exchange(copies, PAIR).reshape(4 * pairs, LANES)
        out = near_apply(
            lists, blocks, extra, values, noise_var, leaf_coupling, columns, tiles
        )
        base, leaf_far = out[-2:]
        common = (
            rows, base, leaf_far, group_far, parent, top_far, places, group_coupling[0],
            own_pair, tops, leaf_transfer, basis,
        )
        return common, out[0] if tiles is None else tiles

    common_specs = [VMEM] * 3 + [SMEM] * 3 + [VMEM] * 6
    wide_field, packed_shape = shape(8, POINTS), shape(PAIR, PACK, LANES)
    scratch = [pltpu.VMEM((8, POINTS), f32)]
    scalar = shape(8, LANES)

    packed, values = simple(
        begin_kernel,
        [shape(PAIR, PACK + COORDS, LANES), wide_field],
        [VMEM] * 4,
        scratch,
    )(warm_start, coords, basis, leaf_transfer)
    common, tiles = gather(packed, values, None)
    packed, residual = simple(
        residual_kernel, [packed_shape, wide_field], common_specs + [VMEM], scratch
    )(*common, observed)
    common, _ = gather(packed, residual, tiles)
    packed, first, unit, norm = simple(
        second_kernel, [packed_shape, wide_field, wide_field, scalar], common_specs + [VMEM]
    )(*common, residual)
    common, _ = gather(packed, unit, tiles)
    sums, lower, lower_mapped, step, curve = simple(
        third_kernel,
        [shape(PAIR, 8, LANES), wide_field, wide_field, scalar, scalar],
        common_specs + [VMEM] * 3,
    )(*common, residual, first, norm)
    blocks = exchange(sums, 1)
    (copies,) = simple(total_kernel, [shape(pairs, 8, LANES)], [VMEM])(blocks)
    blocks = exchange(copies, PAIR)
    own = shape(LEAVES, POINTS)
    return tuple(
        simple(end_kernel, [own, own], [VMEM] * 9)(
            blocks, warm_start, residual, first, lower, lower_mapped, norm, step, curve
        )
    )


def solution(mesh):
    placed = (
        P(("wide", "narrow"), None, None),
        P(("wide", "narrow"), None),
        P(("wide", "narrow"), None),
        P(("wide", "narrow"), None),
        P(("wide", "narrow"), None, None),
        P(("wide", "narrow"), None, None),
        P(("wide", "narrow"), None, None, None),
        P("wide", None, None, None),
        P(),
        P(),
        P(("wide", "narrow"), None),
        P(("wide", "narrow")),
        P(("wide", "narrow"), None),
        P(("wide", "narrow")),
        P("wide", None),
        P(),
        P(),
    )
    return jax.shard_map(
        local,
        mesh=mesh,
        in_specs=placed,
        out_specs=(P(("wide", "narrow"), None), P(("wide", "narrow"), None)),
        check_vma=False,
    )
```

time: 750 us -> 190 us (0.25)
  blocking collectives: 512 us -> 49.1 us
  matrix products: 98 us -> 0 us
  other arithmetic: 34.1 us -> 0 us
  Pallas kernels: 0 us -> 27.9 us
  starting transfers between devices: 35.3 us -> 60.5 us
  local copies, waits for them, and re-layouts: 51.9 us -> 36.4 us
  waiting for transfers between devices: 0.02 us -> 11.3 us
  loops' own time: 10.2 us -> 0 us
    psum x6 -> x0, blocking collectives: 305 us -> none  [the longest x2 190 us: squares(): return lax.psum(jnp.sum(vector * vector), ('wide', 'narrow'))]
    all_gather x10 -> x0, blocking collectives: 208 us -> none  [the longest x3 145 us: operator_apply(): all_coef = lax.all_gather(own_coef[None, :], 'wide', axis=0, tiled=True)]
    dot_general x45 -> x0, matrix products: 98 us -> none  [the longest x12 67.2 us: add_slot(): jnp.einsum('bij,bj->bi', kernel_tile, source_values, precision=highest)]
    all_to_all x0 -> x4, starting transfers between devices: none -> 49.3 us  [exchange(): lax.all_to_all(copies, ('wide', 'narrow'), 0, 0, tiled=True, axis_index_g...]
    all_to_all x0 -> x4, blocking collectives: none -> 49.1 us  [exchange(): lax.all_to_all(copies, ('wide', 'narrow'), 0, 0, tiled=True, axis_index_g...]
    gather x33 -> x0, local copies, waits for them, and re-layouts: 32 us -> none  [the longest x12 19.4 us: add_slot(): source_points = jnp.take(coord_window, sources, axis=0, mode='clip')]
    pallas_call x0 -> x12, Pallas kernels: none -> 27.9 us  [the longest x3 18.3 us: near_apply(): pl.pallas_call(functools.partial(near_kernel, evaluate), out_shape=([shap...]
    unnamed x46 -> x82, local copies, waits for them, and re-layouts: 7.4 us -> 32.6 us
  transfers between devices with their start and end apart: 8 -> 7, of which waited for: 0 -> 4; matrix products, arithmetic and copies ran while one was open for 8% -> 3% of each run, Pallas kernels for 0% -> 10%
where the time goes in v1:
time: 190 us; the launch traced here: 188 us
  starting transfers between devices  60.5 us (32%)
  blocking collectives  49.1 us (26%)
  local copies, waits for them, and re-layouts  36.4 us (19%)
  Pallas kernels  27.9 us (15%)
  waiting for transfers between devices  11.3 us (6%)
  between operations  2.93 us (2%)
    all_to_all x4, starting transfers between devices, exchange(): lax.all_to_all(copies, ('wide', 'narrow'), 0, 0, tiled=True, axis_index_g...  49.3 us
    all_to_all x4, blocking collectives, exchange(): lax.all_to_all(copies, ('wide', 'narrow'), 0, 0, tiled=True, axis_index_g...  49.1 us
    unnamed x82, local copies, waits for them, and re-layouts  32.6 us
    pallas_call x3, Pallas kernels, near_apply(): pl.pallas_call(functools.partial(near_kernel, evaluate), out_shape=([shap...  18.3 us
    ppermute x3, starting transfers between devices, neighbours(): return lax.ppermute(fields, 'wide', across)  11.3 us
    ppermute x3, waiting for transfers between devices, neighbours(): return lax.ppermute(fields, 'wide', across)  7.23 us
    all_to_all x4, waiting for transfers between devices, exchange(): lax.all_to_all(copies, ('wide', 'narrow'), 0, 0, tiled=True, axis_index_g...  4.09 us
  transfers between devices with their start and end apart: 7, of which 4 were waited for; matrix products, arithmetic and copies ran while one was open for 3% of the time, Pallas kernels for 10%

profile of v1, /device:TPU:1, one launch (start us, length us, event | category | flops | bytes accessed | tf_op | source)
XLA Modules:
  0.0 188.2 jit_solution(5909688307979550874)
XLA Ops:
  0.6 0.0 copy-start
  0.6 0.0 copy-start.6
  0.7 1.0 copy-done.7
  1.7 0.8 copy-done.12
  2.5 0.7 copy-done.15
  3.2 0.7 copy-done.19
  4.0 0.0 copy-start.39
  4.0 0.0 copy-start.18
  4.0 0.0 copy-start.34
  4.0 0.0 copy-start.37
  4.0 1.0 shard_map.176
  5.1 10.2 %all-to-all-start = ((f32[8,52,128]{2,1,0:T(8,128)}), f32[8,52,128]{2,1,0:T(8,128)S(1)}, u32[]{:S(2)}, u32[]{:S(2)}) async-start(f32[8,52,128]{2,1,0:T(8,128)} %get-tuple-element.28), calls=%async_computation | async-start | bytes 458752 | tf_op jit(solution)/shard_map/all_to_all | solution.py:394
  15.3 1.6 constant_dynamic-slice_fusion
  16.9 0.5 copy.23.top_transfer.refs_9_
  17.4 4.1 %all-to-all-done.blocks.refs_4_ = f32[8,52,128]{2,1,0:T(8,128)S(1)} async-done(((f32[8,52,128]{2,1,0:T(8,128)}), f32[8,52,128]{2,1,0:T(8,128)S(1)}, u32[]{:S(2)}, u32[]{:S(2)}) %all-to-all-start) | async-done | bytes 213024 | tf_op jit(solution)/shard_map/all_to_all | solution.py:394
  21.5 0.9 shard_map.177
  22.4 11.9 %all-to-all-start.1 = ((f32[64,4,128]{2,1,0:T(4,128)}), f32[64,4,128]{2,1,0:T(4,128)S(1)}, u32[]{:S(2)}, u32[]{:S(2)}) async-start(f32[64,4,128]{2,1,0:T(4,128)} %get-tuple-element.29), calls=%async_computation.1 | async-start | bytes 262144 | tf_op jit(solution)/shard_map/all_to_all | solution.py:394
  34.3 1.0 copy.22
  35.3 0.8 reshape.20
  36.1 0.1 reshape.21.refs_6_
  36.2 1.2 dynamic_slice.12
  39.4 3.7 %collective-permute-start = (f32[4,48,128]{2,1,0:T(8,128)S(1)}, f32[4,48,128]{2,1,0:T(8,128)S(1)}, u32[]{:S(2)}, u32[]{:S(2)}) collective-permute-start(f32[4,48,128]{2,1,0:T(8,128)S(1)} %get-tuple-element.30), channel_id=1, source_target_pairs={{4,8},{8,4},{12,16},{16,12},{20,24},{24,20},{28,32},{32,28},{36,40... | collective-permute-start | bytes 294920 | tf_op jit(solution)/shard_map/ppermute | solution.py:404
  43.2 2.6 %collective-permute-done.refs_5_ = f32[4,48,128]{2,1,0:T(8,128)S(1)} collective-permute-done((f32[4,48,128]{2,1,0:T(8,128)S(1)}, f32[4,48,128]{2,1,0:T(8,128)S(1)}, u32[]{:S(2)}, u32[]{:S(2)}) %collective-permute-start) | collective-permute-done | bytes 98336 | tf_op jit(solution)/shard_map/ppermute | solution.py:404
  45.8 1.0 copy-done.4
  46.8 0.7 copy-done.16
  47.5 0.7 copy-done.23
  48.2 0.7 copy-done.26
  48.9 0.7 copy-done.32
  49.5 0.7 copy-done.35
  50.2 12.8 %shard_map.178 = (f32[12,512,512]{2,1,0:T(8,128)S(1)}, f32[8,512]{1,0:T(8,128)S(1)}, f32[8,64]{1,0:T(8,128)S(1)}) custom-call(s32[3,4]{1,0:T(4,128)S(1)} %copy-done.23, s32[3]{0:T(128)S(1)} %copy-done.32, s32[3,8]{1,0:T(4,128)S(1)} %copy-done.26, s32[3]{0:T(128)S(1)} %copy-done.35, f32[8,52,128]{2,1,0:T(8,128)S(1)} %all-to-all-done.blocks.refs_4_, ...), custom_call_target="tpu_custom_call" | custom-call | flops 300000000 | bytes 2000000 | tf_op jit(solution)/shard_map/pallas_call | solution.py:254
  63.0 4.6 %copy-done.1 = f32[12,512,512]{2,1,0:T(8,128)} copy-done((f32[12,512,512]{2,1,0:T(8,128)}, f32[12,512,512]{2,1,0:T(8,128)S(1)}, u32[]{:S(2)}) %copy-start.1) | copy-done | bytes 12582936
  67.6 0.9 copy-done.8
  68.5 0.9 copy-done.10
  69.4 0.8 copy-done.13
  70.2 0.7 copy-done.21
  70.9 0.7 copy-done.29
  71.6 0.7 copy-done.30
  72.2 0.7 copy-done.38
  72.9 1.8 shard_map.179
  74.7 7.8 %all_to_all.40.blocks.refs_4_ = f32[8,16,128]{2,1,0:T(8,128)S(1)} all-to-all(f32[8,16,128]{2,1,0:T(8,128)S(1)} %get-tuple-element.34), channel_id=1, replica_groups={{0,1,2,3,4,5,6,7},{8,9,10,11,12,13,14,15},{16,17,18,19,20,21,22,23},{24..., dimensions={0} | all-to-all | bytes 131072 | tf_op jit(solution)/shard_map/all_to_all | solution.py:394
  82.5 0.9 shard_map.180
  83.4 13.8 %all-to-all-start.3 = ((f32[64,4,128]{2,1,0:T(4,128)}), f32[64,4,128]{2,1,0:T(4,128)S(1)}, u32[]{:S(2)}, u32[]{:S(2)}) async-start(f32[64,4,128]{2,1,0:T(4,128)} %get-tuple-element.35), calls=%async_computation.3 | async-start | bytes 262144 | tf_op jit(solution)/shard_map/all_to_all | solution.py:394
  97.2 3.8 %collective-permute-start.1 = (f32[4,12,128]{2,1,0:T(8,128)S(1)}, f32[4,12,128]{2,1,0:T(8,128)S(1)}, u32[]{:S(2)}, u32[]{:S(2)}) collective-permute-start(f32[4,12,128]{2,1,0:T(8,128)S(1)} %get-tuple-element.36), channel_id=1, source_target_pairs={{4,8},{8,4},{12,16},{16,12},{20,24},{24,20},{28,32},{32,28},{36,40... | collective-permute-start | bytes 73736 | tf_op jit(solution)/shard_map/ppermute | solution.py:404
  101.0 2.3 %collective-permute-done.1.refs_5_ = f32[4,12,128]{2,1,0:T(8,128)S(1)} collective-permute-done((f32[4,12,128]{2,1,0:T(8,128)S(1)}, f32[4,12,128]{2,1,0:T(8,128)S(1)}, u32[]{:S(2)}, u32[]{:S(2)}) %collective-permute-start.1) | collective-permute-done | bytes 24608 | tf_op jit(solution)/shard_map/ppermute | solution.py:404
  103.3 4.6 %copy-done.2 = f32[12,512,512]{2,1,0:T(8,128)S(1)} copy-done((f32[12,512,512]{2,1,0:T(8,128)S(1)}, f32[12,512,512]{2,1,0:T(8,128)}, u32[]{:S(2)}) %copy-start.2) | copy-done | bytes 12582936
  107.8 1.0 copy-done.5
  108.8 0.7 copy-done.17
  109.5 0.7 copy-done.24
  110.2 0.7 copy-done.27
  110.9 0.7 copy-done.33
  111.6 0.7 copy-done.36
  112.2 2.7 %shard_map.181 = (f32[8,512]{1,0:T(8,128)S(1)}, f32[8,64]{1,0:T(8,128)S(1)}) custom-call(s32[3,4]{1,0:T(4,128)S(1)} %copy-done.24, s32[3]{0:T(128)S(1)} %copy-done.33, s32[3,8]{1,0:T(4,128)S(1)} %copy-done.27, s32[3]{0:T(128)S(1)} %copy-done.36, f32[8,16,128]{2,1,0:T(8,128)S(1)} %all_to_all.40.blocks.refs_4_, ...), custom_call_target="tpu_custom_call" | custom-call | flops 10000000 | bytes 2000000 | tf_op jit(solution)/shard_map/pallas_call | solution.py:254
  115.0 1.8 shard_map.182
  116.8 7.5 %all_to_all.41.blocks.refs_4_ = f32[8,16,128]{2,1,0:T(8,128)S(1)} all-to-all(f32[8,16,128]{2,1,0:T(8,128)S(1)} %get-tuple-element.41), channel_id=1, replica_groups={{0,1,2,3,4,5,6,7},{8,9,10,11,12,13,14,15},{16,17,18,19,20,21,22,23},{24..., dimensions={0} | all-to-all | bytes 131072 | tf_op jit(solution)/shard_map/all_to_all | solution.py:394
  124.3 0.9 shard_map.183
  125.2 13.4 %all-to-all-start.5 = ((f32[64,4,128]{2,1,0:T(4,128)}), f32[64,4,128]{2,1,0:T(4,128)S(1)}, u32[]{:S(2)}, u32[]{:S(2)}) async-start(f32[64,4,128]{2,1,0:T(4,128)} %get-tuple-element.42), calls=%async_computation.5 | async-start | bytes 262144 | tf_op jit(solution)/shard_map/all_to_all | solution.py:394
  138.6 3.8 %collective-permute-start.2 = (f32[4,12,128]{2,1,0:T(8,128)S(1)}, f32[4,12,128]{2,1,0:T(8,128)S(1)}, u32[]{:S(2)}, u32[]{:S(2)}) collective-permute-start(f32[4,12,128]{2,1,0:T(8,128)S(1)} %get-tuple-element.43), channel_id=1, source_target_pairs={{4,8},{8,4},{12,16},{16,12},{20,24},{24,20},{28,32},{32,28},{36,40... | collective-permute-start | bytes 73736 | tf_op jit(solution)/shard_map/ppermute | solution.py:404
  142.4 2.3 %collective-permute-done.2.refs_5_ = f32[4,12,128]{2,1,0:T(8,128)S(1)} collective-permute-done((f32[4,12,128]{2,1,0:T(8,128)S(1)}, f32[4,12,128]{2,1,0:T(8,128)S(1)}, u32[]{:S(2)}, u32[]{:S(2)}) %collective-permute-start.2) | collective-permute-done | bytes 24608 | tf_op jit(solution)/shard_map/ppermute | solution.py:404
  144.8 4.6 %copy-done.3 = f32[12,512,512]{2,1,0:T(8,128)S(1)} copy-done((f32[12,512,512]{2,1,0:T(8,128)S(1)}, f32[12,512,512]{2,1,0:T(8,128)}, u32[]{:S(2)}) %copy-start.3) | copy-done | bytes 12582936
  149.3 2.7 %shard_map.184 = (f32[8,512]{1,0:T(8,128)S(1)}, f32[8,64]{1,0:T(8,128)S(1)}) custom-call(s32[3,4]{1,0:T(4,128)S(1)} %copy-done.25, s32[3]{0:T(128)S(1)} %copy-done.34, s32[3,8]{1,0:T(4,128)S(1)} %copy-done.28, s32[3]{0:T(128)S(1)} %copy-done.37, f32[8,16,128]{2,1,0:T(8,128)S(1)} %all_to_all.41.blocks.refs_4_, ...), custom_call_target="tpu_custom_call" | custom-call | flops 10000000 | bytes 2000000 | tf_op jit(solution)/shard_map/pallas_call | solution.py:254
  152.1 1.6 shard_map.185
  153.6 7.5 %all_to_all.42.blocks = f32[8,8,128]{2,1,0:T(8,128)S(1)} all-to-all(f32[8,8,128]{2,1,0:T(8,128)S(1)} %get-tuple-element.49), channel_id=1, replica_groups={{0,1,2,3,4,5,6,7},{8,9,10,11,12,13,14,15},{16,17,18,19,20,21,22,23},{24..., dimensions={0} | all-to-all | bytes 65536 | tf_op jit(solution)/shard_map/all_to_all | solution.py:394
  161.1 26.2 %all_to_all.43.blocks = f32[64,8,128]{2,1,0:T(8,128)S(1)} all-to-all(f32[64,8,128]{2,1,0:T(8,128)S(1)} %shard_map.186), channel_id=1, replica_groups={{0,8,16,24,32,40,48,56,64,72,80,88,96,104,112,120,128,136,144,152,160,1..., dimensions={0} | all-to-all | bytes 524288 | tf_op jit(solution)/shard_map/all_to_all | solution.py:394
  187.4 0.8 shard_map.187
  (54 shorter events, 0.1 us)
Async XLA Ops:
  0.6 42.5 %copy-start = (bf16[16,4,64,64]{3,2,1,0:T(8,128)(2,1)S(1)}, bf16[16,4,64,64]{3,2,1,0:T(8,128)(2,1)}, u32[]{:S(2)}) copy-start(bf16[16,4,64,64]{3,2,1,0:T(8,128)(2,1)} %param.26) | copy-start | bytes 1572868
  0.6 144.1 %copy-start.6 = (bf16[3,8,64,64]{3,2,1,0:T(8,128)(2,1)S(1)}, bf16[3,8,64,64]{3,2,1,0:T(8,128)(2,1)}, u32[]{:S(2)}) copy-start(bf16[3,8,64,64]{3,2,1,0:T(8,128)(2,1)} %refs_8_.5) | copy-start | bytes 589828
  0.7 1.0 copy-start.7
  1.7 0.8 copy-start.12
  2.5 0.7 copy-start.15
  3.2 0.7 copy-start.19
  3.9 111.0 %copy-start.9 = (bf16[3,512,64]{1,2,0:T(8,128)(2,1)S(1)}, bf16[3,512,64]{1,2,0:T(8,128)(2,1)}, u32[]{:S(2)}) copy-start(bf16[3,512,64]{1,2,0:T(8,128)(2,1)} %param.21) | copy-start | bytes 589828
  3.9 111.0 %copy-start.11 = (bf16[1,6,64,64]{3,2,1,0:T(8,128)(2,1)S(1)}, bf16[1,6,64,64]{3,2,1,0:T(8,128)(2,1)}, u32[]{:S(2)}) copy-start(bf16[1,6,64,64]{3,2,1,0:T(8,128)(2,1)} %param.24) | copy-start | bytes 147460
  3.9 111.0 %copy-start.14 = (bf16[3,64,64]{2,1,0:T(8,128)(2,1)S(1)}, bf16[3,64,64]{2,1,0:T(8,128)(2,1)}, u32[]{:S(2)}) copy-start(bf16[3,64,64]{2,1,0:T(8,128)(2,1)} %refs_10_.5) | copy-start | bytes 73732
  3.9 111.0 %copy-start.22 = (s32[16,4]{0,1:T(4,128)S(1)}, s32[16,4]{0,1:T(4,128)}, u32[]{:S(2)}) copy-start(s32[16,4]{0,1:T(4,128)} %param.33) | copy-start | bytes 772
  3.9 111.0 %copy-start.31 = (s32[128]{0:T(128)S(1)}, s32[128]{0:T(128)}, u32[]{:S(2)}) copy-start(s32[128]{0:T(128)} %refs_4_.5) | copy-start | bytes 1540
  4.0 111.0 %copy-start.39 = (s32[1,6]{1,0:T(1,128)S(1)}, s32[1,6]{1,0:T(1,128)}, u32[]{:S(2)}) copy-start(s32[1,6]{1,0:T(1,128)} %refs_3_.11) | copy-start | bytes 76
  4.0 140.7 %copy-start.18 = (f32[3,512]{1,0:T(4,128)S(1)}, f32[3,512]{1,0:T(4,128)}, u32[]{:S(2)}) copy-start(f32[3,512]{1,0:T(4,128)} %refs_7_.5) | copy-start | bytes 18436
  4.0 140.7 %copy-start.25 = (s32[3,4]{1,0:T(4,128)S(1)}, s32[3,4]{1,0:T(4,128)}, u32[]{:S(2)}) copy-start(s32[3,4]{1,0:T(4,128)} %refs_0_.5) | copy-start | bytes 148
  4.0 140.7 %copy-start.28 = (s32[3,8]{1,0:T(4,128)S(1)}, s32[3,8]{1,0:T(4,128)}, u32[]{:S(2)}) copy-start(s32[3,8]{1,0:T(4,128)} %refs_2_.5) | copy-start | bytes 292
  4.0 140.7 %copy-start.34 = (s32[3]{0:T(128)S(1)}, s32[3]{0:T(128)}, u32[]{:S(2)}) copy-start(s32[3]{0:T(128)} %refs_1_.5) | copy-start | bytes 40
  4.0 140.7 %copy-start.37 = (s32[3]{0:T(128)S(1)}, s32[3]{0:T(128)}, u32[]{:S(2)}) copy-start(s32[3]{0:T(128)} %refs_3_.10) | copy-start | bytes 40
  5.1 16.4 %all-to-all-start = ((f32[8,52,128]{2,1,0:T(8,128)}), f32[8,52,128]{2,1,0:T(8,128)S(1)}, u32[]{:S(2)}, u32[]{:S(2)}) async-start(f32[8,52,128]{2,1,0:T(8,128)} %get-tuple-element.28), calls=%async_computation | async-start | bytes 458752 | tf_op jit(solution)/shard_map/all_to_all | solution.py:394
  22.4 45.2 %all-to-all-start.1 = ((f32[64,4,128]{2,1,0:T(4,128)}), f32[64,4,128]{2,1,0:T(4,128)S(1)}, u32[]{:S(2)}, u32[]{:S(2)}) async-start(f32[64,4,128]{2,1,0:T(4,128)} %get-tuple-element.29), calls=%async_computation.1 | async-start | bytes 262144 | tf_op jit(solution)/shard_map/all_to_all | solution.py:394
  39.4 6.4 %collective-permute-start = (f32[4,48,128]{2,1,0:T(8,128)S(1)}, f32[4,48,128]{2,1,0:T(8,128)S(1)}, u32[]{:S(2)}, u32[]{:S(2)}) collective-permute-start(f32[4,48,128]{2,1,0:T(8,128)S(1)} %get-tuple-element.30), channel_id=1, source_target_pairs={{4,8},{8,4},{12,16},{16,12},{20,24},{24,20},{28,32},{32,28},{36,40... | collective-permute-start | bytes 294920 | tf_op jit(solution)/shard_map/ppermute | solution.py:404
  45.8 1.0 copy-start.4
  46.8 0.7 copy-start.16
  47.5 0.7 copy-start.23
  48.2 0.7 copy-start.26
  48.9 0.7 copy-start.32
  49.5 0.7 copy-start.35
  63.0 4.6 %copy-start.1 = (f32[12,512,512]{2,1,0:T(8,128)}, f32[12,512,512]{2,1,0:T(8,128)S(1)}, u32[]{:S(2)}) copy-start(f32[12,512,512]{2,1,0:T(8,128)S(1)} %get-tuple-element.38.refs_9_) | copy-start | bytes 37748740
  67.6 0.9 copy-start.8
  68.5 0.9 copy-start.10
  69.4 0.8 copy-start.13
  70.2 0.7 copy-start.21
  70.9 0.7 copy-start.29
  71.6 0.7 copy-start.30
  72.2 0.7 copy-start.38
  83.4 31.5 %all-to-all-start.3 = ((f32[64,4,128]{2,1,0:T(4,128)}), f32[64,4,128]{2,1,0:T(4,128)S(1)}, u32[]{:S(2)}, u32[]{:S(2)}) async-start(f32[64,4,128]{2,1,0:T(4,128)} %get-tuple-element.35), calls=%async_computation.3 | async-start | bytes 262144 | tf_op jit(solution)/shard_map/all_to_all | solution.py:394
  97.2 6.1 %collective-permute-start.1 = (f32[4,12,128]{2,1,0:T(8,128)S(1)}, f32[4,12,128]{2,1,0:T(8,128)S(1)}, u32[]{:S(2)}, u32[]{:S(2)}) collective-permute-start(f32[4,12,128]{2,1,0:T(8,128)S(1)} %get-tuple-element.36), channel_id=1, source_target_pairs={{4,8},{8,4},{12,16},{16,12},{20,24},{24,20},{28,32},{32,28},{36,40... | collective-permute-start | bytes 73736 | tf_op jit(solution)/shard_map/ppermute | solution.py:404
  103.3 4.6 %copy-start.2 = (f32[12,512,512]{2,1,0:T(8,128)S(1)}, f32[12,512,512]{2,1,0:T(8,128)}, u32[]{:S(2)}) copy-start(f32[12,512,512]{2,1,0:T(8,128)} %copy-done.1) | copy-start | bytes 37748740
  107.8 1.0 copy-start.5
  108.8 0.7 copy-start.17
  109.5 0.7 copy-start.24
  110.2 0.7 copy-start.27
  110.9 0.7 copy-start.33
  111.6 0.7 copy-start.36
  112.2 75.1 %copy-start.20 = (f32[3,512]{1,0:T(4,128)S(1)}, f32[3,512]{1,0:T(4,128)}, u32[]{:S(2)}) copy-start(f32[3,512]{1,0:T(4,128)} %warm.3) | copy-start | bytes 18436
  125.2 26.8 %all-to-all-start.5 = ((f32[64,4,128]{2,1,0:T(4,128)}), f32[64,4,128]{2,1,0:T(4,128)S(1)}, u32[]{:S(2)}, u32[]{:S(2)}) async-start(f32[64,4,128]{2,1,0:T(4,128)} %get-tuple-element.42), calls=%async_computation.5 | async-start | bytes 262144 | tf_op jit(solution)/shard_map/all_to_all | solution.py:394
  138.6 6.1 %collective-permute-start.2 = (f32[4,12,128]{2,1,0:T(8,128)S(1)}, f32[4,12,128]{2,1,0:T(8,128)S(1)}, u32[]{:S(2)}, u32[]{:S(2)}) collective-permute-start(f32[4,12,128]{2,1,0:T(8,128)S(1)} %get-tuple-element.43), channel_id=1, source_target_pairs={{4,8},{8,4},{12,16},{16,12},{20,24},{24,20},{28,32},{32,28},{36,40... | collective-permute-start | bytes 73736 | tf_op jit(solution)/shard_map/ppermute | solution.py:404
  144.7 4.6 %copy-start.3 = (f32[12,512,512]{2,1,0:T(8,128)S(1)}, f32[12,512,512]{2,1,0:T(8,128)}, u32[]{:S(2)}) copy-start(f32[12,512,512]{2,1,0:T(8,128)} %copy-done.1) | copy-start | bytes 37748740

commit v2 on v1

v2 whole, which is shorter than its diff:
```python
import functools

import jax
import jax.numpy as jnp
from jax import lax
from jax.experimental import pallas as pl
from jax.experimental.pallas import tpu as pltpu
from jax.sharding import PartitionSpec as P

amplitude = 1.0 / 16.0
rate = 1.7320508075688772 / 1.5
log2_e = 1.4426950408889634
LEAVES = 3
NARROW = 4
GROUP = LEAVES * NARROW
POINTS = 512
RANK = 64
NEAR = 4
FAR = 8
FAR_GROUP = 6
FAR_TOP = 4
LANES = 128
PIECES = POINTS // LANES
FIELD = LEAVES * PIECES
PACK = FIELD + 4
COORDS = 3 * FIELD
PAIR = 2 * NARROW
WINDOW = 3 * GROUP
NEAR_LIST = 0
NEAR_COUNT = NEAR_LIST + LEAVES * NEAR
FAR_LIST = NEAR_COUNT + LEAVES
FAR_COUNT = FAR_LIST + LEAVES * FAR
GROUP_FAR = FAR_COUNT + LEAVES
TOP_FAR = GROUP_FAR + FAR_GROUP
PARENT = TOP_FAR + FAR_TOP
CHUNK = 64
QUARTER = 128
VMEM = pl.BlockSpec(memory_space=pltpu.VMEM)
SMEM = pl.BlockSpec(memory_space=pltpu.SMEM)
HBM = pl.BlockSpec(memory_space=pltpu.HBM)
f32 = jnp.float32


def shape(*dims, dtype=f32):
    return jax.ShapeDtypeStruct(dims, dtype)


def in_hbm(*arrays):
    return tuple(pltpu.with_memory_space_constraint(one, pltpu.HBM) for one in arrays)


def cost(flops, bytes_accessed):
    return pl.CostEstimate(flops=flops, bytes_accessed=bytes_accessed, transcendentals=0)


def rows_of(array):
    return lax.broadcasted_iota(jnp.int32, array.shape, 0)


def times(vectors, matrix, transposed):
    high = vectors.astype(jnp.bfloat16).astype(f32)
    rest = vectors - high
    middle = rest.astype(jnp.bfloat16).astype(f32)
    parts = jnp.concatenate([high, middle, rest - middle], axis=0).astype(jnp.bfloat16)
    dims = (((1,), (1 if transposed else 0,)), ((), ()))
    out = lax.dot_general(parts, matrix, dims, preferred_element_type=f32)
    count = vectors.shape[0]
    return out[:count] + (out[count : 2 * count] + out[2 * count :])


def row_by_leaf(terms):
    out = jnp.zeros_like(terms[0])
    for leaf, term in enumerate(terms):
        out = jnp.where(rows_of(term) == leaf, term, out)
    return out


def fold_half(row):
    return row[:, :RANK] + row[:, RANK:]


def lane_sums(product):
    total = jnp.sum(product, axis=0, keepdims=True)
    total = total[:, :128] + total[:, 128:256] + (total[:, 256:384] + total[:, 384:])
    return fold_half(total)


def pack(values, scalar, basis, transfer, packed):
    for leaf in range(LEAVES):
        for piece in range(PIECES):
            packed[0, pl.ds(leaf * PIECES + piece, 1), :] = values[
                leaf : leaf + 1, piece * LANES : (piece + 1) * LANES
            ]
    coefs = row_by_leaf([times(values, basis[leaf], True) for leaf in range(LEAVES)])
    partial = row_by_leaf([times(coefs, transfer[leaf], False) for leaf in range(LEAVES)])
    partial = jnp.sum(partial, axis=0, keepdims=True)
    empty = jnp.zeros((1, RANK), f32)
    beside = [scalar, empty, empty]
    for leaf in range(LEAVES):
        packed[0, pl.ds(FIELD + leaf, 1), :] = jnp.concatenate(
            [coefs[leaf : leaf + 1], beside[leaf]], axis=1
        )
    packed[0, pl.ds(FIELD + 3, 1), :] = jnp.concatenate([partial, empty], axis=1)
    whole = packed[0]
    for copy in range(1, PAIR):
        packed[copy] = whole


def padded(ref, scratch):
    scratch[...] = jnp.zeros(scratch.shape, f32)
    scratch[0:LEAVES, :] = ref[...]
    return scratch[...]


def fetch(pairs, sems):
    copies = [pltpu.make_async_copy(one, two, sems.at[i]) for i, (one, two) in enumerate(pairs)]
    for copy in copies:
        copy.start()
    return copies


def begin_kernel(warm_in, coords_in, basis_in, transfer_in, packed, values, basis, transfer,
                 warm, coords, scratch, sems):
    pairs = [(warm_in, warm), (coords_in, coords), (basis_in, basis), (transfer_in, transfer)]
    for copy in fetch(pairs, sems):
        copy.wait()
    field = padded(warm, scratch)
    values[...] = field
    for leaf in range(LEAVES):
        for axis in range(3):
            for piece in range(PIECES):
                packed[0, pl.ds(PACK + (leaf * 3 + axis) * PIECES + piece, 1), :] = coords[
                    leaf, axis : axis + 1, piece * LANES : (piece + 1) * LANES
                ]
    pack(field, jnp.zeros((1, RANK), f32), basis, transfer, packed)


def fold_kernel(blocks, top_transfer, copies):
    sums = []
    for row in (FIELD + 3, FIELD):
        for group in range(2):
            first = group * NARROW
            line = [blocks[first + i, row : row + 1, :] for i in range(NARROW)]
            line = (line[0] + line[1]) + (line[2] + line[3])
            if row == FIELD + 3:
                partial = jnp.broadcast_to(line[:, :RANK], (8, RANK))
                lifted = times(partial, top_transfer[group], False)[:1]
                line = jnp.concatenate([line[:, :RANK], lifted], axis=1)
            sums.append(line)
    sums = jnp.concatenate(sums, axis=0)
    copies[...] = jnp.broadcast_to(sums[None], copies.shape)


def selection(table, parent):
    count = 2 * parent.shape[1]
    at = lax.broadcasted_iota(jnp.int32, (16, count), 1)
    row = lax.broadcasted_iota(jnp.int32, (16, count), 0)
    kind = at & 3
    group = lax.broadcasted_iota(jnp.int32, (parent.shape[1], count), 0)
    spot = lax.broadcasted_iota(jnp.int32, (parent.shape[1], count), 1)
    spread = jnp.where((group >> 1) * 4 + (group & 1) == spot, 1.0, 0.0).astype(jnp.bfloat16)
    parents = jnp.broadcast_to(parent[...], (16, parent.shape[1])).astype(f32)
    parents = jnp.dot(parents.astype(jnp.bfloat16), spread, preferred_element_type=f32)
    chosen = (row == FAR_GROUP + FAR_TOP) & (kind >= 2)
    for slot in range(FAR_GROUP):
        one = table[GROUP_FAR + slot]
        chosen = chosen | ((row == slot) & (at == (one >> 1) * 4 + (one & 1)))
    for slot in range(FAR_TOP):
        box = table[TOP_FAR + slot].astype(f32)
        chosen = chosen | ((row == FAR_GROUP + slot) & (kind < 2) & (parents == box))
    return jnp.where(chosen, 1.0, 0.0).astype(jnp.bfloat16)


def near_kernel(evaluate, *refs):
    if evaluate:
        (table, blocks, shifted, values, coords_in, noise_in, coupling_in, group_in, observed_in,
         parent_in, top_in, tiles, base, leaf_far, select, own_pair, noise, coupling, group,
         observed, window, sources, coords, columns, parent, scratch, near, coefs, totals, spread,
         kept, sems, tile_sems) = refs
        wide = lax.axis_index("wide")
        copies = fetch(
            [
                (coords_in, coords), (parent_in, parent), (coupling_in, coupling),
                (noise_in, noise), (group_in, group), (observed_in, observed),
                (top_in.at[table[PARENT]], own_pair),
            ],
            sems,
        )
    else:
        (table, blocks, shifted, values, noise, coupling, tiles, base, leaf_far,
         window, scratch, near, coefs, totals, spread, kept, tile_sems) = refs
        wide = lax.axis_index("wide")
    own = lax.rem(wide, 2)
    first_group = wide - own

    def tile_copy(leaf, quarter):
        part = (pl.ds(leaf * NEAR, NEAR), pl.ds(quarter * QUARTER, QUARTER), slice(None))
        sem = tile_sems.at[leaf * PIECES + quarter]
        if evaluate:
            return pltpu.make_async_copy(kept.at[part], tiles.at[part], sem)
        return pltpu.make_async_copy(tiles.at[part], kept.at[part], sem)

    if not evaluate:
        for leaf in range(LEAVES):
            for quarter in range(PIECES):
                tile_copy(leaf, quarter).start()

    for device in range(PAIR + NARROW):
        for leaf in range(LEAVES):
            at = device * LEAVES + leaf
            if device < PAIR:
                held, index = blocks, device
            else:
                held, index = shifted, own * NARROW + device - PAIR
            window[at] = held[index, leaf * PIECES : (leaf + 1) * PIECES, :]
            if evaluate:
                rows = PACK + leaf * FIELD
                sources[at] = held[index, rows : rows + FIELD, :]

    if evaluate:
        copies[0].wait()
        copies[1].wait()
        for leaf in range(LEAVES):
            columns[leaf] = jnp.transpose(padded(coords.at[leaf], scratch))
        select[...] = selection(table, parent)

    def leaf_step(leaf, _):
        for slot in range(NEAR):
            listed = table[NEAR_LIST + leaf * NEAR + slot]
            used = slot < table[NEAR_COUNT + leaf]
            of_group = lax.div(listed, GROUP)
            turn = of_group - first_group
            turn = jnp.where((turn >= 0) & (turn < 2), turn, 2)
            place = jnp.where(used, turn * GROUP + listed - of_group * GROUP, 0)
            weight = jnp.where(used, 1.0, 0.0).astype(f32)
            field = window[place] * weight
            for piece in range(PIECES):
                spread[slot, piece] = jnp.broadcast_to(field[piece : piece + 1], (8, LANES))
            if evaluate:
                point = sources[place]
                for at in range(FIELD):
                    spread[slot, PIECES + at] = jnp.broadcast_to(point[at : at + 1], (8, LANES))

        def quarter_step(quarter, _):
            if not evaluate:
                tile_copy(leaf, quarter).wait()

            def step(chunk, _):
                start = pl.multiple_of(quarter * QUARTER + chunk * CHUNK, CHUNK)
                acc = jnp.zeros((CHUNK // 8, 8, LANES), f32)
                if evaluate:
                    column = columns[leaf, pl.ds(start, CHUNK), :]
                    target = [
                        jnp.broadcast_to(column[:, axis : axis + 1], (CHUNK, LANES)).reshape(
                            CHUNK // 8, 8, LANES
                        )
                        for axis in range(3)
                    ]
                for slot in range(NEAR):
                    for piece in range(PIECES):
                        cut = slice(piece * LANES, (piece + 1) * LANES)
                        where = (leaf * NEAR + slot, pl.ds(start, CHUNK), cut)
                        if evaluate:
                            squared = None
                            for axis in range(3):
                                source = spread[slot, PIECES + axis * PIECES + piece]
                                between = target[axis] - source[None]
                                between = between * between
                                squared = between if squared is None else squared + between
                            squared = jnp.maximum(squared, 1e-30)
                            distance = squared * lax.rsqrt(squared)
                            decay = jnp.exp2(distance * (-rate * log2_e))
                            tile = (distance * (amplitude * rate) + amplitude) * decay
                            kept[where] = tile.reshape(CHUNK, LANES)
                        else:
                            tile = kept[where].reshape(CHUNK // 8, 8, LANES)
                        acc = acc + tile * spread[slot, piece][None]
                totals[pl.ds(start, CHUNK), :] = acc.reshape(CHUNK, LANES)
                return 0

            lax.fori_loop(0, QUARTER // CHUNK, step, 0)
            if evaluate:
                tile_copy(leaf, quarter).start()
            return 0

        lax.fori_loop(0, PIECES, quarter_step, 0)
        eye = lax.broadcasted_iota(jnp.int32, (LANES, LANES), 0) == lax.broadcasted_iota(
            jnp.int32, (LANES, LANES), 1
        )
        pieces = []
        for piece in range(PIECES):
            column = jnp.sum(totals[piece * LANES : (piece + 1) * LANES, :], axis=1, keepdims=True)
            pieces.append(jnp.sum(jnp.where(eye, column, 0.0), axis=0, keepdims=True))
        near[pl.ds(leaf, 1), :] = jnp.concatenate(pieces, axis=1)
        return 0

    near[...] = jnp.zeros(near.shape, f32)
    lax.fori_loop(0, LEAVES, leaf_step, 0)

    if evaluate:
        for copy in copies[2:]:
            copy.wait()
    coefs[...] = jnp.zeros(coefs.shape, f32)
    for device in range(NARROW):
        coefs[device * LEAVES : (device + 1) * LEAVES, :] = blocks[
            own * NARROW + device, FIELD : FIELD + LEAVES, :
        ]
    lane = lax.broadcasted_iota(jnp.int32, (16, LANES), 1)
    row = lax.broadcasted_iota(jnp.int32, (16, LANES), 0)
    far_rows = []
    for leaf in range(LEAVES):
        out = times(coefs[:, :RANK], coupling[leaf].reshape(FAR * RANK, RANK), True)
        total = jnp.zeros((16, LANES), f32)
        for two in range(FAR // 2):
            at = []
            for slot in (2 * two, 2 * two + 1):
                member = table[FAR_LIST + leaf * FAR + slot] - wide * GROUP
                at.append(jnp.where(slot < table[FAR_COUNT + leaf], member, -1))
            listed = jnp.where(lane < RANK, at[0], at[1]) == row
            total = total + jnp.where(listed, out[:, two * LANES : (two + 1) * LANES], 0.0)
        far_rows.append(fold_half(jnp.sum(total, axis=0, keepdims=True)))
    leaf_far[...] = row_by_leaf([jnp.broadcast_to(one, (8, RANK)) for one in far_rows])
    base[...] = padded(noise, scratch) * values[...] + near[...]
    if evaluate:
        for leaf in range(LEAVES):
            for quarter in range(PIECES):
                tile_copy(leaf, quarter).wait()


def near_apply(evaluate, operands):
    tiles = shape(NEAR * LEAVES, POINTS, POINTS)
    bf16 = jnp.bfloat16
    out_shape = [shape(8, POINTS), shape(8, RANK)]
    out_specs = [VMEM] * 2
    scratch = [pltpu.VMEM((WINDOW, PIECES, LANES), f32)]
    if evaluate:
        out_shape = [pltpu.HBM(tiles.shape, f32)] + out_shape + [
            shape(16, 256 * operands[9].shape[1] // LANES, dtype=bf16),
            shape(FAR_TOP, RANK, RANK, dtype=bf16),
            shape(LEAVES, POINTS),
            shape(LEAVES, FAR, RANK, RANK, dtype=bf16),
            shape(FAR_GROUP, RANK, RANK, dtype=bf16),
            shape(LEAVES, POINTS),
        ]
        out_specs = [HBM] + [VMEM] * 8
        scratch += [
            pltpu.VMEM((WINDOW, FIELD, LANES), f32),
            pltpu.VMEM((LEAVES, 3, POINTS), f32),
            pltpu.VMEM((LEAVES, POINTS, 8), f32),
            pltpu.VMEM(operands[9].shape, jnp.int32),
        ]
    scratch += [
        pltpu.VMEM((8, POINTS), f32),
        pltpu.VMEM((8, POINTS), f32),
        pltpu.VMEM((16, LANES), f32),
        pltpu.VMEM((POINTS, LANES), f32),
        pltpu.VMEM((NEAR, PIECES + FIELD, 8, LANES), f32),
        pltpu.VMEM(tiles.shape, f32),
    ]
    if evaluate:
        scratch.append(pltpu.SemaphoreType.DMA((7,)))
    scratch.append(pltpu.SemaphoreType.DMA((LEAVES * PIECES,)))
    places = [HBM] * 7 if evaluate else [VMEM, VMEM, HBM]
    return pl.pallas_call(
        functools.partial(near_kernel, evaluate),
        out_shape=out_shape,
        in_specs=[SMEM] + [VMEM] * 3 + places,
        out_specs=out_specs,
        scratch_shapes=scratch,
        cost_estimate=cost(3 * 10**8 if evaluate else 3 * 10**7, 2 * 10**7),
        compiler_params=pltpu.CompilerParams(vmem_limit_bytes=24 << 20),
    )(*operands)


def far_field(rows, base, leaf_far, select, group_coupling, own_pair, top_transfer, transfer,
              basis):
    wide = lax.axis_index("wide")
    gathered = rows[...]
    picked = jnp.zeros((16, LANES), f32)
    for part in range(3):
        piece = gathered.astype(jnp.bfloat16)
        gathered = gathered - piece.astype(f32)
        picked = picked + jnp.dot(select[...], piece, preferred_element_type=f32)

    def listed(vectors, matrices, slots, first):
        out = times(vectors, matrices[...].reshape(slots * RANK, RANK), True)
        lane = lax.broadcasted_iota(jnp.int32, (16, LANES), 1)
        line = lax.broadcasted_iota(jnp.int32, (16, LANES), 0)
        total = jnp.zeros((16, LANES), f32)
        for two in range(slots // 2):
            own = line == first + 2 * two + jnp.where(lane < RANK, 0, 1)
            total = total + jnp.where(own, out[:, two * LANES : (two + 1) * LANES], 0.0)
        return fold_half(jnp.sum(total, axis=0, keepdims=True))

    top_in = listed(picked[:, RANK:], own_pair, FAR_TOP, FAR_GROUP)
    group_in = listed(picked[:, :RANK], group_coupling, FAR_GROUP, 0)
    group_in = group_in + times(jnp.broadcast_to(top_in, (8, RANK)), top_transfer[lax.rem(wide, 2)], True)
    leaf_in = leaf_far[...] + row_by_leaf(
        [times(group_in, transfer[leaf], True) for leaf in range(LEAVES)]
    )
    far = row_by_leaf([times(leaf_in, basis[leaf], False) for leaf in range(LEAVES)])
    sums = picked[FAR_GROUP + FAR_TOP : FAR_GROUP + FAR_TOP + 1, RANK:]
    return base[...] + far, jnp.sum(sums, axis=1, keepdims=True)


def residual_kernel(*refs):
    *common, observed, packed, residual, scratch = refs
    mapped, _ = far_field(*common)
    field = padded(observed, scratch) - mapped
    residual[...] = field
    pack(field, lane_sums(field * field), common[-1], common[-2], packed)


def second_kernel(*refs):
    *common, residual, packed, first, unit, norm = refs
    mapped, norm_now = far_field(*common)
    first[...] = mapped
    field = mapped * lax.rsqrt(norm_now)
    unit[...] = field
    norm[...] = jnp.broadcast_to(norm_now, norm.shape)
    scalar = lane_sums(residual[...] * mapped)
    pack(field, scalar, common[-1], common[-2], packed)


def third_kernel(*refs):
    *common, residual, first, norm, copies, lower, lower_mapped, step, curve = refs
    mapped, bend = far_field(*common)
    norm_now = norm[:1, :1]
    size = norm_now / bend
    before, image = residual[...], first[...]
    low = before - size * image
    low_mapped = image - (size * jnp.sqrt(norm_now)) * mapped
    lower[...] = low
    lower_mapped[...] = low_mapped
    step[...] = jnp.broadcast_to(size, step.shape)
    curve[...] = jnp.broadcast_to(bend, curve.shape)
    products = [low * low, low * low_mapped, before * low_mapped + low * image]
    sums = [lane_sums(product) for product in products] + [jnp.zeros((1, RANK), f32)]
    first_row = jnp.concatenate(sums[:2], axis=1)
    second_row = jnp.concatenate(sums[2:], axis=1)
    block = jnp.broadcast_to(first_row, (8, LANES))
    block = jnp.where(rows_of(block) == 0, block, second_row)
    copies[...] = jnp.broadcast_to(block[None], copies.shape)


def total_kernel(blocks, copies):
    total = blocks[0]
    for device in range(1, blocks.shape[0]):
        total = total + blocks[device]
    copies[...] = jnp.broadcast_to(total[:2][None], copies.shape)


def step_kernel(warm, residual, step, moved):
    moved[...] = warm[...] + step[:1, :1] * residual[...]


def end_kernel(blocks, moved, residual, first, lower, lower_mapped, norm, curve,
               solution_field, last_residual):
    total = jnp.sum(blocks[...], axis=0)
    norm_next = jnp.sum(total[:1, :RANK], axis=1, keepdims=True)
    bend = jnp.sum(total[:1, RANK:], axis=1, keepdims=True)
    cross = jnp.sum(total[1:2, :RANK], axis=1, keepdims=True)
    norm_now = norm[:1, :1]
    ratio = norm_next / norm_now
    second = norm_next / (bend + ratio * (cross + ratio * curve[:1, :1]))
    keep = slice(0, LEAVES)
    solution_field[...] = moved[keep] + second * (lower[keep] + ratio * residual[keep])
    last_residual[...] = lower[keep] - second * (lower_mapped[keep] + ratio * first[keep])


def simple(kernel, out_shape, in_specs, scratch=()):
    return pl.pallas_call(
        kernel,
        out_shape=out_shape,
        in_specs=in_specs,
        out_specs=[VMEM] * len(out_shape),
        scratch_shapes=list(scratch),
        cost_estimate=cost(10**6, 10**6),
        compiler_params=pltpu.CompilerParams(vmem_limit_bytes=8 << 20),
    )


def exchange(copies, stride, shift=0):
    members = copies.shape[0]
    devices = lax.axis_size("wide") * lax.axis_size("narrow")
    span = members * stride
    groups = [
        [(base + offset + stride * i + shift) % devices for i in range(members)]
        for base in range(0, devices, span)
        for offset in range(stride)
    ]
    return lax.all_to_all(
        copies, ("wide", "narrow"), 0, 0, tiled=True, axis_index_groups=groups
    )


def local(
    coords,
    noise_var,
    observed,
    warm_start,
    leaf_basis,
    leaf_transfer,
    leaf_coupling,
    group_coupling,
    top_transfer,
    top_coupling,
    near_list,
    near_count,
    far_list,
    far_count,
    group_far,
    parent,
    top_far,
):
    groups = parent.shape[0]
    pairs = groups // 2
    wide = lax.axis_index("wide")
    own_parent = lax.dynamic_slice_in_dim(parent, wide, 1, 0)
    own_tops = lax.dynamic_slice_in_dim(top_far, own_parent[0], 1, 0)
    table = [near_list, near_count, far_list, far_count, group_far, own_tops, own_parent]
    table = jnp.concatenate([one.reshape(-1) for one in table])
    tops = lax.dynamic_slice_in_dim(top_transfer, wide // 2 * 2, 2, 0)
    field, scalar = shape(8, POINTS), shape(8, LANES)
    packed_shape = shape(PAIR, PACK, LANES)
    scratch = [pltpu.VMEM((8, POINTS), f32)]

    def gather(packed, rest, evaluate):
        blocks = exchange(packed, 1)
        shifted = exchange(packed, 1, NARROW)
        (copies,) = simple(fold_kernel, [shape(pairs, 4, LANES)], [VMEM] * 2)(blocks, tops)
        rows = exchange(copies, PAIR).reshape(4 * pairs, LANES)
        return rows, near_apply(evaluate, (table, blocks, shifted) + rest)

    packed, values, basis, transfer = simple(
        begin_kernel,
        [
            shape(PAIR, PACK + COORDS, LANES),
            field,
            shape(LEAVES, RANK, POINTS, dtype=jnp.bfloat16),
            shape(LEAVES, RANK, RANK, dtype=jnp.bfloat16),
        ],
        [HBM] * 4,
        [pltpu.VMEM((LEAVES, POINTS), f32), pltpu.VMEM((LEAVES, 3, POINTS), f32)]
        + scratch
        + [pltpu.SemaphoreType.DMA((4,))],
    )(*in_hbm(warm_start, coords, jnp.transpose(leaf_basis, (0, 2, 1)), leaf_transfer))
    rows, near = gather(
        packed,
        (values,)
        + in_hbm(
            coords, noise_var, leaf_coupling, group_coupling[0], observed,
            parent.reshape(1, groups), top_coupling,
        ),
        True,
    )
    tiles, base, leaf_far, select, own_pair, noise, coupling, group, observed = near
    far_data = (select, group, own_pair, tops, transfer, basis)
    packed, residual = simple(
        residual_kernel, [packed_shape, field], [VMEM] * 10, scratch
    )(rows, base, leaf_far, *far_data, observed)

    rows, near = gather(packed, (residual, noise, coupling) + in_hbm(tiles), False)
    packed, first, unit, norm = simple(
        second_kernel, [packed_shape, field, field, scalar], [VMEM] * 10
    )(rows, *near, *far_data, residual)

    rows, near = gather(packed, (unit, noise, coupling) + in_hbm(tiles), False)
    sums, lower, lower_mapped, step, curve = simple(
        third_kernel,
        [shape(PAIR, 8, LANES), field, field, scalar, scalar],
        [VMEM] * 12,
    )(rows, *near, *far_data, residual, first, norm)
    blocks = exchange(sums, 1)
    (copies,) = simple(total_kernel, [shape(pairs, 2, LANES)], [VMEM])(blocks)
    blocks = exchange(copies, PAIR)
    (moved,) = simple(step_kernel, [field], [VMEM] * 3)(values, residual, step)
    own = shape(LEAVES, POINTS)
    return tuple(
        simple(end_kernel, [own, own], [VMEM] * 8)(
            blocks, moved, residual, first, lower, lower_mapped, norm, curve
        )
    )


def solution(mesh):
    placed = (
        P(("wide", "narrow"), None, None),
        P(("wide", "narrow"), None),
        P(("wide", "narrow"), None),
        P(("wide", "narrow"), None),
        P(("wide", "narrow"), None, None),
        P(("wide", "narrow"), None, None),
        P(("wide", "narrow"), None, None, None),
        P("wide", None, None, None),
        P(),
        P(),
        P(("wide", "narrow"), None),
        P(("wide", "narrow")),
        P(("wide", "narrow"), None),
        P(("wide", "narrow")),
        P("wide", None),
        P(),
        P(),
    )
    return jax.shard_map(
        local,
        mesh=mesh,
        in_specs=placed,
        out_specs=(P(("wide", "narrow"), None), P(("wide", "narrow"), None)),
        check_vma=False,
    )
```

time: 190 us -> 177 us (0.932)
  local copies, waits for them, and re-layouts: 36.4 us -> 5.96 us
  waiting for transfers between devices: 11.3 us -> 37.6 us
  starting transfers between devices: 60.5 us -> 52.2 us
  Pallas kernels: 27.9 us -> 35.1 us
  blocking collectives: 49.1 us -> 42.7 us
    all_to_all x4 -> x7, waiting for transfers between devices: 4.09 us -> 37.6 us  [exchange(): lax.all_to_all(copies, ('wide', 'narrow'), 0, 0, tiled=True, axis_index_g...]
    unnamed x82 -> x3, local copies, waits for them, and re-layouts: 32.6 us -> 0.52 us
    ppermute x3 -> x0, starting transfers between devices: 11.3 us -> none  [neighbours(): return lax.ppermute(fields, 'wide', across)]
    ppermute x3 -> x0, waiting for transfers between devices: 7.23 us -> none  [neighbours(): return lax.ppermute(fields, 'wide', across)]
    pallas_call x12 -> x13, Pallas kernels: 27.9 us -> 35.1 us  [the longest x3 24.2 us: near_apply(): pl.pallas_call(functools.partial(near_kernel, evaluate), out_shape=out_sh...]
    all_to_all x4, blocking collectives: 49.1 us -> 42.7 us  [exchange(): lax.all_to_all(copies, ('wide', 'narrow'), 0, 0, tiled=True, axis_index_g...]
    all_to_all x4 -> x7, starting transfers between devices: 49.3 us -> 52.2 us  [exchange(): lax.all_to_all(copies, ('wide', 'narrow'), 0, 0, tiled=True, axis_index_g...]
  transfers between devices with their start and end apart: 7 -> 7, of which waited for: 4 -> 6; matrix products, arithmetic and copies ran while one was open for 3% -> 3% of each run, Pallas kernels for 10% -> 15%
where the time goes in v2:
time: 177 us; the launch traced here: 176 us
  starting transfers between devices  52.2 us (29%)
  blocking collectives  42.7 us (24%)
  waiting for transfers between devices  37.6 us (21%)
  Pallas kernels  35.1 us (20%)
  local copies, waits for them, and re-layouts  5.96 us (3%)
  between operations  2.73 us (2%)
    all_to_all x7, starting transfers between devices, exchange(): lax.all_to_all(copies, ('wide', 'narrow'), 0, 0, tiled=True, axis_index_g...  52.2 us
    all_to_all x4, blocking collectives, exchange(): lax.all_to_all(copies, ('wide', 'narrow'), 0, 0, tiled=True, axis_index_g...  42.7 us
    all_to_all x7, waiting for transfers between devices, exchange(): lax.all_to_all(copies, ('wide', 'narrow'), 0, 0, tiled=True, axis_index_g...  37.6 us
    pallas_call x3, Pallas kernels, near_apply(): pl.pallas_call(functools.partial(near_kernel, evaluate), out_shape=out_sh...  24.2 us
  transfers between devices with their start and end apart: 7, of which 6 were waited for; matrix products, arithmetic and copies ran while one was open for 3% of the time, Pallas kernels for 15%

profile of v2, /device:TPU:1, one launch (start us, length us, event | category | flops | bytes accessed | tf_op | source)
XLA Modules:
  0.0 176.3 jit_solution(3600416425187299287)
XLA Ops:
  0.6 0.0 copy-start
  0.6 2.1 %shard_map.176 = (f32[8,52,128]{2,1,0:T(8,128)}, f32[8,512]{1,0:T(8,128)S(1)}, bf16[3,64,512]{2,1,0:T(8,128)(2,1)S(1)}, bf16[3,64,64]{2,1,0:T(8,128)(2,1)S(1)}) custom-call(f32[3,512]{1,0:T(4,128)} %warm_in.1, f32[3,3,512]{2,1,0:T(4,128)} %refs_4_.1, bf16[3,64,512]{2,1,0:T(8,128)(2,1)} %bitcast.11, bf16[3,64,64]{2,1,0:T(8,128)(2,1)} %transfer_in.1), custom_call_target="tpu_custom_call" | custom-call | flops 1000000 | bytes 1000000 | tf_op jit(solution)/shard_map/pallas_call | solution.py:535
  2.8 16.4 %all_to_all.55.blocks.refs_1_ = f32[8,52,128]{2,1,0:T(8,128)S(1)} all-to-all(f32[8,52,128]{2,1,0:T(8,128)} %get-tuple-element.30), channel_id=1, replica_groups={{0,1,2,3,4,5,6,7},{8,9,10,11,12,13,14,15},{16,17,18,19,20,21,22,23},{24..., dimensions={0} | all-to-all | bytes 425984 | tf_op jit(solution)/shard_map/all_to_all | solution.py:492
  19.2 3.4 %all-to-all-start.2 = ((f32[8,52,128]{2,1,0:T(8,128)}), f32[8,52,128]{2,1,0:T(8,128)S(1)}, u32[]{:S(2)}, u32[]{:S(2)}) async-start(f32[8,52,128]{2,1,0:T(8,128)} %get-tuple-element.30), calls=%async_computation.2 | async-start | bytes 458752 | tf_op jit(solution)/shard_map/all_to_all | solution.py:492
  22.6 0.0 copy-done
  22.6 0.4 constant_dynamic-slice_fusion
  23.0 0.5 copy.20.top_transfer.refs_6_
  23.5 0.9 shard_map.177
  24.4 4.6 %all-to-all-done.2.refs_2_ = f32[8,52,128]{2,1,0:T(8,128)S(1)} async-done(((f32[8,52,128]{2,1,0:T(8,128)}), f32[8,52,128]{2,1,0:T(8,128)S(1)}, u32[]{:S(2)}, u32[]{:S(2)}) %all-to-all-start.2) | async-done | bytes 213024 | tf_op jit(solution)/shard_map/all_to_all | solution.py:492
  29.0 14.0 %all-to-all-start.1 = ((f32[64,4,128]{2,1,0:T(4,128)}), f32[64,4,128]{2,1,0:T(4,128)S(1)}, u32[]{:S(2)}, u32[]{:S(2)}) async-start(f32[64,4,128]{2,1,0:T(4,128)} %shard_map.177), calls=%async_computation.1 | async-start | bytes 262144 | tf_op jit(solution)/shard_map/all_to_all | solution.py:492
  43.1 1.2 dynamic_slice.10
  45.6 0.8 reshape.29
  46.4 0.8 reshape.30
  47.8 0.9 dynamic-slice_reduce_fusion
  48.7 1.4 concatenate.3.refs_0_
  50.1 12.6 %shard_map.178 = (f32[12,512,512]{2,1,0:T(8,128)}, f32[8,512]{1,0:T(8,128)S(1)}, f32[8,64]{1,0:T(8,128)S(1)}, bf16[16,256]{1,0:T(8,128)(2,1)S(1)}, bf16[4,64,64]...) custom-call(s32[53]{0:T(128)S(1)} %concatenate.3.refs_0_, ...), custom_call_target="tpu_custom_call" | custom-call | flops 300000000 | bytes 20000000 | tf_op jit(solution)/shard_map/pallas_call | solution.py:364
  62.7 0.0 all-to-all-done.1
  62.7 1.8 %shard_map.179 = (f32[8,16,128]{2,1,0:T(8,128)}, f32[8,512]{1,0:T(8,128)S(1)}) custom-call(f32[256,128]{1,0:T(8,128)S(1)} %bitcast.8, f32[8,512]{1,0:T(8,128)S(1)} %get-tuple-element.32.refs_1_, f32[8,64]{1,0:T(8,128)S(1)} %get-tuple-element.33.refs_2_, bf16[16,256]{1,0:T(8,128)(2,1)S(1)} %get-tuple-element.34.refs_3_, ...), custom_call_target="tpu_custom_call" | custom-call | flops 1000000 | bytes 1000000 | tf_op jit(solution)/shard_map/pallas_call | solution.py:559
  64.5 8.6 %all_to_all.56.blocks.refs_1_ = f32[8,16,128]{2,1,0:T(8,128)S(1)} all-to-all(f32[8,16,128]{2,1,0:T(8,128)} %get-tuple-element.40), channel_id=1, replica_groups={{0,1,2,3,4,5,6,7},{8,9,10,11,12,13,14,15},{16,17,18,19,20,21,22,23},{24..., dimensions={0} | all-to-all | bytes 131072 | tf_op jit(solution)/shard_map/all_to_all | solution.py:492
  73.1 3.7 %all-to-all-start.5 = ((f32[8,16,128]{2,1,0:T(8,128)}), f32[8,16,128]{2,1,0:T(8,128)S(1)}, u32[]{:S(2)}, u32[]{:S(2)}) async-start(f32[8,16,128]{2,1,0:T(8,128)} %get-tuple-element.40), calls=%async_computation.5 | async-start | bytes 131072 | tf_op jit(solution)/shard_map/all_to_all | solution.py:492
  76.8 0.9 shard_map.180
  77.7 5.0 %all-to-all-done.5.refs_2_ = f32[8,16,128]{2,1,0:T(8,128)S(1)} async-done(((f32[8,16,128]{2,1,0:T(8,128)}), f32[8,16,128]{2,1,0:T(8,128)S(1)}, u32[]{:S(2)}, u32[]{:S(2)}) %all-to-all-start.5) | async-done | bytes 65568 | tf_op jit(solution)/shard_map/all_to_all | solution.py:492
  82.7 12.5 %all-to-all-start.4 = ((f32[64,4,128]{2,1,0:T(4,128)}), f32[64,4,128]{2,1,0:T(4,128)S(1)}, u32[]{:S(2)}, u32[]{:S(2)}) async-start(f32[64,4,128]{2,1,0:T(4,128)} %shard_map.180), calls=%async_computation.4 | async-start | bytes 262144 | tf_op jit(solution)/shard_map/all_to_all | solution.py:492
  95.2 5.8 %shard_map.181 = (f32[8,512]{1,0:T(8,128)S(1)}, f32[8,64]{1,0:T(8,128)S(1)}) custom-call(s32[53]{0:T(128)S(1)} %concatenate.3.refs_0_, f32[8,16,128]{2,1,0:T(8,128)S(1)} %all_to_all.56.blocks.refs_1_, f32[8,16,128]{2,1,0:T(8,128)S(1)} %all-to-all-done.5.refs_2_, f32[8,512]{1,0:T(8,128)S(1)} %get-tuple-element.41.refs_3_.refs_9_.residual, ...), custom_call_target="tpu_custom_call" | custom-call | flops 30000000 | bytes 20000000 | tf_op jit(solution)/shard_map/pallas_call | solution.py:364
  101.0 5.7 %all-to-all-done.4 = f32[64,4,128]{2,1,0:T(4,128)S(1)} async-done(((f32[64,4,128]{2,1,0:T(4,128)}), f32[64,4,128]{2,1,0:T(4,128)S(1)}, u32[]{:S(2)}, u32[]{:S(2)}) %all-to-all-start.4) | async-done | bytes 131104 | tf_op jit(solution)/shard_map/all_to_all | solution.py:492
  106.7 1.8 %shard_map.182 = (f32[8,16,128]{2,1,0:T(8,128)}, f32[8,512]{1,0:T(8,128)S(1)}, f32[8,512]{1,0:T(8,128)S(1)}, f32[8,128]{1,0:T(8,128)S(1)}) custom-call(f32[256,128]{1,0:T(8,128)S(1)} %bitcast.10, f32[8,512]{1,0:T(8,128)S(1)} %get-tuple-element.45.refs_1_, f32[8,64]{1,0:T(8,128)S(1)} %get-tuple-element.46.refs_2_, ...), custom_call_target="tpu_custom_call" | custom-call | flops 1000000 | bytes 1000000 | tf_op jit(solution)/shard_map/pallas_call | solution.py:564
  108.5 10.3 %all_to_all.57.blocks.refs_1_ = f32[8,16,128]{2,1,0:T(8,128)S(1)} all-to-all(f32[8,16,128]{2,1,0:T(8,128)} %get-tuple-element.47), channel_id=1, replica_groups={{0,1,2,3,4,5,6,7},{8,9,10,11,12,13,14,15},{16,17,18,19,20,21,22,23},{24..., dimensions={0} | all-to-all | bytes 131072 | tf_op jit(solution)/shard_map/all_to_all | solution.py:492
  118.9 3.3 %all-to-all-start.8 = ((f32[8,16,128]{2,1,0:T(8,128)}), f32[8,16,128]{2,1,0:T(8,128)S(1)}, u32[]{:S(2)}, u32[]{:S(2)}) async-start(f32[8,16,128]{2,1,0:T(8,128)} %get-tuple-element.47), calls=%async_computation.8 | async-start | bytes 131072 | tf_op jit(solution)/shard_map/all_to_all | solution.py:492
  122.2 0.9 shard_map.183
  123.1 5.1 %all-to-all-done.8.refs_2_ = f32[8,16,128]{2,1,0:T(8,128)S(1)} async-done(((f32[8,16,128]{2,1,0:T(8,128)}), f32[8,16,128]{2,1,0:T(8,128)S(1)}, u32[]{:S(2)}, u32[]{:S(2)}) %all-to-all-start.8) | async-done | bytes 65568 | tf_op jit(solution)/shard_map/all_to_all | solution.py:492
  128.2 9.2 %all-to-all-start.7 = ((f32[64,4,128]{2,1,0:T(4,128)}), f32[64,4,128]{2,1,0:T(4,128)S(1)}, u32[]{:S(2)}, u32[]{:S(2)}) async-start(f32[64,4,128]{2,1,0:T(4,128)} %shard_map.183), calls=%async_computation.7 | async-start | bytes 262144 | tf_op jit(solution)/shard_map/all_to_all | solution.py:492
  137.5 5.8 %shard_map.184 = (f32[8,512]{1,0:T(8,128)S(1)}, f32[8,64]{1,0:T(8,128)S(1)}) custom-call(s32[53]{0:T(128)S(1)} %concatenate.3.refs_0_, f32[8,16,128]{2,1,0:T(8,128)S(1)} %all_to_all.57.blocks.refs_1_, f32[8,16,128]{2,1,0:T(8,128)S(1)} %all-to-all-done.8.refs_2_, f32[8,512]{1,0:T(8,128)S(1)} %get-tuple-element.48.refs_3_, ...), custom_call_target="tpu_custom_call" | custom-call | flops 30000000 | bytes 20000000 | tf_op jit(solution)/shard_map/pallas_call | solution.py:364
  143.3 6.1 %all-to-all-done.7 = f32[64,4,128]{2,1,0:T(4,128)S(1)} async-done(((f32[64,4,128]{2,1,0:T(4,128)}), f32[64,4,128]{2,1,0:T(4,128)S(1)}, u32[]{:S(2)}, u32[]{:S(2)}) %all-to-all-start.7) | async-done | bytes 131104 | tf_op jit(solution)/shard_map/all_to_all | solution.py:492
  149.4 1.0 shard_map.185
  150.4 7.4 %all_to_all.58.blocks = f32[8,8,128]{2,1,0:T(8,128)S(1)} all-to-all(f32[8,8,128]{2,1,0:T(8,128)S(1)} %get-tuple-element.53), channel_id=1, replica_groups={{0,1,2,3,4,5,6,7},{8,9,10,11,12,13,14,15},{16,17,18,19,20,21,22,23},{24..., dimensions={0} | all-to-all | bytes 65536 | tf_op jit(solution)/shard_map/all_to_all | solution.py:492
  157.7 0.7 shard_map.186
  158.4 6.0 %all-to-all-start.10 = ((f32[64,2,128]{2,1,0:T(2,128)}), f32[64,2,128]{2,1,0:T(2,128)S(1)}, u32[]{:S(2)}, u32[]{:S(2)}) async-start(f32[64,2,128]{2,1,0:T(2,128)} %shard_map.186), calls=%async_computation.10 | async-start | bytes 131072 | tf_op jit(solution)/shard_map/all_to_all | solution.py:492
  164.4 11.1 %all-to-all-done.10.blocks = f32[64,2,128]{2,1,0:T(2,128)S(1)} async-done(((f32[64,2,128]{2,1,0:T(2,128)}), f32[64,2,128]{2,1,0:T(2,128)S(1)}, u32[]{:S(2)}, u32[]{:S(2)}) %all-to-all-start.10) | async-done | bytes 65568 | tf_op jit(solution)/shard_map/all_to_all | solution.py:492
  175.5 0.9 shard_map.188
  (1 shorter events, 0.0 us)
Async XLA Ops:
  0.6 22.0 %copy-start = (bf16[128,64,64]{0,2,1:T(8,128)(2,1)S(1)}, bf16[128,64,64]{0,2,1:T(8,128)(2,1)}, u32[]{:S(2)}) copy-start(bf16[128,64,64]{0,2,1:T(8,128)(2,1)} %param.25) | copy-start | bytes 3145732
  19.2 9.9 %all-to-all-start.2 = ((f32[8,52,128]{2,1,0:T(8,128)}), f32[8,52,128]{2,1,0:T(8,128)S(1)}, u32[]{:S(2)}, u32[]{:S(2)}) async-start(f32[8,52,128]{2,1,0:T(8,128)} %get-tuple-element.30), calls=%async_computation.2 | async-start | bytes 458752 | tf_op jit(solution)/shard_map/all_to_all | solution.py:492
  29.0 33.6 %all-to-all-start.1 = ((f32[64,4,128]{2,1,0:T(4,128)}), f32[64,4,128]{2,1,0:T(4,128)S(1)}, u32[]{:S(2)}, u32[]{:S(2)}) async-start(f32[64,4,128]{2,1,0:T(4,128)} %shard_map.177), calls=%async_computation.1 | async-start | bytes 262144 | tf_op jit(solution)/shard_map/all_to_all | solution.py:492
  73.1 9.6 %all-to-all-start.5 = ((f32[8,16,128]{2,1,0:T(8,128)}), f32[8,16,128]{2,1,0:T(8,128)S(1)}, u32[]{:S(2)}, u32[]{:S(2)}) async-start(f32[8,16,128]{2,1,0:T(8,128)} %get-tuple-element.40), calls=%async_computation.5 | async-start | bytes 131072 | tf_op jit(solution)/shard_map/all_to_all | solution.py:492
  82.7 24.0 %all-to-all-start.4 = ((f32[64,4,128]{2,1,0:T(4,128)}), f32[64,4,128]{2,1,0:T(4,128)S(1)}, u32[]{:S(2)}, u32[]{:S(2)}) async-start(f32[64,4,128]{2,1,0:T(4,128)} %shard_map.180), calls=%async_computation.4 | async-start | bytes 262144 | tf_op jit(solution)/shard_map/all_to_all | solution.py:492
  118.9 9.4 %all-to-all-start.8 = ((f32[8,16,128]{2,1,0:T(8,128)}), f32[8,16,128]{2,1,0:T(8,128)S(1)}, u32[]{:S(2)}, u32[]{:S(2)}) async-start(f32[8,16,128]{2,1,0:T(8,128)} %get-tuple-element.47), calls=%async_computation.8 | async-start | bytes 131072 | tf_op jit(solution)/shard_map/all_to_all | solution.py:492
  128.2 21.1 %all-to-all-start.7 = ((f32[64,4,128]{2,1,0:T(4,128)}), f32[64,4,128]{2,1,0:T(4,128)S(1)}, u32[]{:S(2)}, u32[]{:S(2)}) async-start(f32[64,4,128]{2,1,0:T(4,128)} %shard_map.183), calls=%async_computation.7 | async-start | bytes 262144 | tf_op jit(solution)/shard_map/all_to_all | solution.py:492
  158.4 17.1 %all-to-all-start.10 = ((f32[64,2,128]{2,1,0:T(2,128)}), f32[64,2,128]{2,1,0:T(2,128)S(1)}, u32[]{:S(2)}, u32[]{:S(2)}) async-start(f32[64,2,128]{2,1,0:T(2,128)} %shard_map.186), calls=%async_computation.10 | async-start | bytes 131072 | tf_op jit(solution)/shard_map/all_to_all | solution.py:492

commit v3 on v2

--- a/solution.py
+++ b/solution.py
@@ -26,17 +26,9 @@
 COORDS = 3 * FIELD
 PAIR = 2 * NARROW
 WINDOW = 3 * GROUP
-NEAR_LIST = 0
-NEAR_COUNT = NEAR_LIST + LEAVES * NEAR
-FAR_LIST = NEAR_COUNT + LEAVES
-FAR_COUNT = FAR_LIST + LEAVES * FAR
-GROUP_FAR = FAR_COUNT + LEAVES
-TOP_FAR = GROUP_FAR + FAR_GROUP
-PARENT = TOP_FAR + FAR_TOP
 CHUNK = 64
 QUARTER = 128
 VMEM = pl.BlockSpec(memory_space=pltpu.VMEM)
-SMEM = pl.BlockSpec(memory_space=pltpu.SMEM)
 HBM = pl.BlockSpec(memory_space=pltpu.HBM)
 f32 = jnp.float32
 
@@ -135,7 +127,7 @@
     pack(field, jnp.zeros((1, RANK), f32), basis, transfer, packed)
 
 
-def fold_kernel(blocks, top_transfer, copies):
+def fold_kernel(blocks, top_transfer, copies, fields):
     sums = []
     for row in (FIELD + 3, FIELD):
         for group in range(2):
@@ -149,9 +141,15 @@
             sums.append(line)
     sums = jnp.concatenate(sums, axis=0)
     copies[...] = jnp.broadcast_to(sums[None], copies.shape)
-
-
-def selection(table, parent):
+    own = lax.rem(lax.axis_index("wide"), 2)
+    for i in range(NARROW):
+        device = own * NARROW + i
+        fields[i, 0:FIELD, :] = blocks[device, 0:FIELD, :]
+        if fields.shape[1] > FIELD:
+            fields[i, FIELD:, :] = blocks[device, PACK:, :]
+
+
+def selection(group_far, top_far, own_parent, parent):
     count = 2 * parent.shape[1]
     at = lax.broadcasted_iota(jnp.int32, (16, count), 1)
     row = lax.broadcasted_iota(jnp.int32, (16, count), 0)
@@ -163,87 +161,39 @@
     parents = jnp.dot(parents.astype(jnp.bfloat16), spread, preferred_element_type=f32)
     chosen = (row == FAR_GROUP + FAR_TOP) & (kind >= 2)
     for slot in range(FAR_GROUP):
-        one = table[GROUP_FAR + slot]
+        one = group_far[0, slot]
         chosen = chosen | ((row == slot) & (at == (one >> 1) * 4 + (one & 1)))
     for slot in range(FAR_TOP):
-        box = table[TOP_FAR + slot].astype(f32)
+        box = top_far[slot, own_parent].astype(f32)
         chosen = chosen | ((row == FAR_GROUP + slot) & (kind < 2) & (parents == box))
     return jnp.where(chosen, 1.0, 0.0).astype(jnp.bfloat16)
 
 
-def near_kernel(evaluate, *refs):
-    if evaluate:
-        (table, blocks, shifted, values, coords_in, noise_in, coupling_in, group_in, observed_in,
-         parent_in, top_in, tiles, base, leaf_far, select, own_pair, noise, coupling, group,
-         observed, window, sources, coords, columns, parent, scratch, near, coefs, totals, spread,
-         kept, sems, tile_sems) = refs
-        wide = lax.axis_index("wide")
-        copies = fetch(
-            [
-                (coords_in, coords), (parent_in, parent), (coupling_in, coupling),
-                (noise_in, noise), (group_in, group), (observed_in, observed),
-                (top_in.at[table[PARENT]], own_pair),
-            ],
-            sems,
-        )
-    else:
-        (table, blocks, shifted, values, noise, coupling, tiles, base, leaf_far,
-         window, scratch, near, coefs, totals, spread, kept, tile_sems) = refs
-        wide = lax.axis_index("wide")
-    own = lax.rem(wide, 2)
-    first_group = wide - own
-
-    def tile_copy(leaf, quarter):
-        part = (pl.ds(leaf * NEAR, NEAR), pl.ds(quarter * QUARTER, QUARTER), slice(None))
-        sem = tile_sems.at[leaf * PIECES + quarter]
-        if evaluate:
-            return pltpu.make_async_copy(kept.at[part], tiles.at[part], sem)
-        return pltpu.make_async_copy(tiles.at[part], kept.at[part], sem)
-
-    if not evaluate:
-        for leaf in range(LEAVES):
-            for quarter in range(PIECES):
-                tile_copy(leaf, quarter).start()
-
-    for device in range(PAIR + NARROW):
-        for leaf in range(LEAVES):
-            at = device * LEAVES + leaf
-            if device < PAIR:
-                held, index = blocks, device
-            else:
-                held, index = shifted, own * NARROW + device - PAIR
-            window[at] = held[index, leaf * PIECES : (leaf + 1) * PIECES, :]
+def tile_copy(evaluate, slots, kept, tiles, sems, leaf, quarter):
+    part = (pl.ds(leaf * slots, slots), pl.ds(quarter * QUARTER, QUARTER), slice(None))
+    source, target = (kept, tiles) if evaluate else (tiles, kept)
+    return pltpu.make_async_copy(source.at[part], target.at[part], sems.at[leaf * PIECES + quarter])
+
+
+def begin_tiles(slots, kept, tiles, sems):
+    for leaf in range(LEAVES):
+        for quarter in range(PIECES):
+            tile_copy(False, slots, kept, tiles, sems, leaf, quarter).start()
+
+
+def tile_products(evaluate, slots, fill, near, columns, spread, totals, kept, tiles, sems):
+    def leaf_step(leaf, _):
+        for slot in range(slots):
+            field, point = fill(leaf, slot)
+            for piece in range(PIECES):
+                spread[slot, piece] = jnp.broadcast_to(field(piece), (8, LANES))
             if evaluate:
-                rows = PACK + leaf * FIELD
-                sources[at] = held[index, rows : rows + FIELD, :]
-
-    if evaluate:
-        copies[0].wait()
-        copies[1].wait()
-        for leaf in range(LEAVES):
-            columns[leaf] = jnp.transpose(padded(coords.at[leaf], scratch))
-        select[...] = selection(table, parent)
-
-    def leaf_step(leaf, _):
-        for slot in range(NEAR):
-            listed = table[NEAR_LIST + leaf * NEAR + slot]
-            used = slot < table[NEAR_COUNT + leaf]
-            of_group = lax.div(listed, GROUP)
-            turn = of_group - first_group
-            turn = jnp.where((turn >= 0) & (turn < 2), turn, 2)
-            place = jnp.where(used, turn * GROUP + listed - of_group * GROUP, 0)
-            weight = jnp.where(used, 1.0, 0.0).astype(f32)
-            field = window[place] * weight
-            for piece in range(PIECES):
-                spread[slot, piece] = jnp.broadcast_to(field[piece : piece + 1], (8, LANES))
-            if evaluate:
-                point = sources[place]
                 for at in range(FIELD):
-                    spread[slot, PIECES + at] = jnp.broadcast_to(point[at : at + 1], (8, LANES))
+                    spread[slot, PIECES + at] = jnp.broadcast_to(point(at), (8, LANES))
 
         def quarter_step(quarter, _):
             if not evaluate:
-                tile_copy(leaf, quarter).wait()
+                tile_copy(False, slots, kept, tiles, sems, leaf, quarter).wait()
 
             def step(chunk, _):
                 start = pl.multiple_of(quarter * QUARTER + chunk * CHUNK, CHUNK)
@@ -256,10 +206,10 @@
                         )
                         for axis in range(3)
                     ]
-                for slot in range(NEAR):
+                for slot in range(slots):
                     for piece in range(PIECES):
                         cut = slice(piece * LANES, (piece + 1) * LANES)
-                        where = (leaf * NEAR + slot, pl.ds(start, CHUNK), cut)
+                        where = (leaf * slots + slot, pl.ds(start, CHUNK), cut)
                         if evaluate:
                             squared = None
                             for axis in range(3):
@@ -280,7 +230,7 @@
 
             lax.fori_loop(0, QUARTER // CHUNK, step, 0)
             if evaluate:
-                tile_copy(leaf, quarter).start()
+                tile_copy(True, slots, kept, tiles, sems, leaf, quarter).start()
             return 0
 
         lax.fori_loop(0, PIECES, quarter_step, 0)
@@ -297,14 +247,96 @@
     near[...] = jnp.zeros(near.shape, f32)
     lax.fori_loop(0, LEAVES, leaf_step, 0)
 
+
+def end_tiles(slots, kept, tiles, sems):
+    for leaf in range(LEAVES):
+        for quarter in range(PIECES):
+            tile_copy(True, slots, kept, tiles, sems, leaf, quarter).wait()
+
+
+def own_kernel(evaluate, *refs):
     if evaluate:
-        for copy in copies[2:]:
-            copy.wait()
+        values, coords_in, tiles, own_near, coords, columns, scratch, sem, *loop = refs
+        (copy,) = fetch([(coords_in, coords)], sem)
+        copy.wait()
+        for leaf in range(LEAVES):
+            columns[leaf] = jnp.transpose(padded(coords.at[leaf], scratch))
+    else:
+        values, tiles, own_near, *loop = refs
+        coords = columns = None
+    spread, totals, kept, sems = loop
+    if not evaluate:
+        begin_tiles(1, kept, tiles, sems)
+
+    def fill(leaf, slot):
+        def field(piece):
+            part = values[:, piece * LANES : (piece + 1) * LANES]
+            return jnp.sum(jnp.where(rows_of(part) == leaf, part, 0.0), axis=0, keepdims=True)
+
+        def point(at):
+            axis, piece = divmod(at, PIECES)
+            return coords[leaf, axis : axis + 1, piece * LANES : (piece + 1) * LANES]
+
+        return field, point
+
+    tile_products(evaluate, 1, fill, own_near, columns, spread, totals, kept, tiles, sems)
+    if evaluate:
+        end_tiles(1, kept, tiles, sems)
+
+
+def near_kernel(evaluate, *refs):
+    if evaluate:
+        (near_list_in, near_count_in, far_list_in, far_count_in, blocks, extra, values, own_near,
+         coords_in, noise_in, coupling_in, group_in, observed_in, parent_in, parents_in,
+         group_far_in, top_far_in, top_in, tiles, base, leaf_far, select, own_pair, noise,
+         coupling, group, observed, near_list, near_count, far_list, far_count, sems, window,
+         sources, coords, columns, parent, parents, group_far, top_far, scratch, near, coefs,
+         spread, totals, kept, tile_sems) = refs
+    else:
+        (near_list_in, near_count_in, far_list_in, far_count_in, blocks, extra, values, own_near,
+         noise, coupling, tiles, base, leaf_far, near_list, near_count, far_list, far_count, sems,
+         window, scratch, near, coefs, spread, totals, kept, tile_sems) = refs
+    slots = NEAR - 1
+    pairs = [
+        (near_list_in, near_list), (near_count_in, near_count),
+        (far_list_in, far_list), (far_count_in, far_count),
+    ]
+    if evaluate:
+        pairs += [
+            (parent_in, parent), (group_far_in, group_far), (top_far_in, top_far),
+            (parents_in, parents), (coords_in, coords), (coupling_in, coupling),
+            (noise_in, noise), (group_in, group), (observed_in, observed),
+        ]
+    copies = fetch(pairs, sems)
+    if not evaluate:
+        begin_tiles(slots, kept, tiles, tile_sems)
+    wide = lax.axis_index("wide")
+    own = lax.rem(wide, 2)
+    first_group = wide - own
+    for device in range(PAIR + NARROW):
+        held, index = (blocks, device) if device < PAIR else (extra, device - PAIR)
+        more = PACK if device < PAIR else FIELD
+        for leaf in range(LEAVES):
+            at = device * LEAVES + leaf
+            window[at] = held[index, leaf * PIECES : (leaf + 1) * PIECES, :]
+            if evaluate:
+                rows = more + leaf * FIELD
+                sources[at] = held[index, rows : rows + FIELD, :]
     coefs[...] = jnp.zeros(coefs.shape, f32)
     for device in range(NARROW):
         coefs[device * LEAVES : (device + 1) * LEAVES, :] = blocks[
             own * NARROW + device, FIELD : FIELD + LEAVES, :
         ]
+    for copy in copies:
+        copy.wait()
+    if evaluate:
+        own_parent = parent[wide]
+        top_copy = pltpu.make_async_copy(top_in.at[own_parent], own_pair, sems.at[0])
+        top_copy.start()
+        for leaf in range(LEAVES):
+            columns[leaf] = jnp.transpose(padded(coords.at[leaf], scratch))
+        select[...] = selection(group_far, top_far, own_parent, parents)
+
     lane = lax.broadcasted_iota(jnp.int32, (16, LANES), 1)
     row = lax.broadcasted_iota(jnp.int32, (16, LANES), 0)
     far_rows = []
@@ -314,28 +346,86 @@
         for two in range(FAR // 2):
             at = []
             for slot in (2 * two, 2 * two + 1):
-                member = table[FAR_LIST + leaf * FAR + slot] - wide * GROUP
-                at.append(jnp.where(slot < table[FAR_COUNT + leaf], member, -1))
+                member = far_list[leaf, slot] - wide * GROUP
+                at.append(jnp.where(slot < far_count[leaf], member, -1))
             listed = jnp.where(lane < RANK, at[0], at[1]) == row
             total = total + jnp.where(listed, out[:, two * LANES : (two + 1) * LANES], 0.0)
         far_rows.append(fold_half(jnp.sum(total, axis=0, keepdims=True)))
     leaf_far[...] = row_by_leaf([jnp.broadcast_to(one, (8, RANK)) for one in far_rows])
-    base[...] = padded(noise, scratch) * values[...] + near[...]
+    local_part = padded(noise, scratch) * values[...] + own_near[...]
+
+    def fill(leaf, slot):
+        listed = near_list[leaf, slot + 1]
+        used = slot + 1 < near_count[leaf]
+        of_group = lax.div(listed, GROUP)
+        turn = of_group - first_group
+        turn = jnp.where((turn >= 0) & (turn < 2), turn, 2)
+        place = jnp.where(used, turn * GROUP + listed - of_group * GROUP, 0)
+        field = window[place] * jnp.where(used, 1.0, 0.0).astype(f32)
+        points = sources[place] if evaluate else None
+        return lambda piece: field[piece : piece + 1], lambda at: points[at : at + 1]
+
+    tile_products(
+        evaluate, slots, fill, near, columns if evaluate else None, spread, totals, kept, tiles,
+        tile_sems,
+    )
+    base[...] = local_part + near[...]
     if evaluate:
-        for leaf in range(LEAVES):
-            for quarter in range(PIECES):
-                tile_copy(leaf, quarter).wait()
-
-
-def near_apply(evaluate, operands):
-    tiles = shape(NEAR * LEAVES, POINTS, POINTS)
+        top_copy.wait()
+        end_tiles(slots, kept, tiles, tile_sems)
+
+
+def loop_scratch(slots):
+    return [
+        pltpu.VMEM((slots, PIECES + FIELD, 8, LANES), f32),
+        pltpu.VMEM((POINTS, LANES), f32),
+        pltpu.VMEM((slots * LEAVES, POINTS, POINTS), f32),
+        pltpu.SemaphoreType.DMA((LEAVES * PIECES,)),
+    ]
+
+
+def column_scratch():
+    return [pltpu.VMEM((LEAVES, 3, POINTS), f32), pltpu.VMEM((LEAVES, POINTS, 8), f32)]
+
+
+def own_apply(evaluate, values, other):
+    out_shape, out_specs, scratch = [shape(8, POINTS)], [VMEM], []
+    if evaluate:
+        out_shape = [pltpu.HBM((LEAVES, POINTS, POINTS), f32)] + out_shape
+        out_specs = [HBM] + out_specs
+        scratch = column_scratch() + [
+            pltpu.VMEM((8, POINTS), f32), pltpu.SemaphoreType.DMA((1,))
+        ]
+    return pl.pallas_call(
+        functools.partial(own_kernel, evaluate),
+        out_shape=out_shape,
+        in_specs=[VMEM, HBM],
+        out_specs=out_specs,
+        scratch_shapes=scratch + loop_scratch(1),
+        cost_estimate=cost(10**8, 4 * 10**6),
+        compiler_params=pltpu.CompilerParams(vmem_limit_bytes=16 << 20),
+    )(values, *in_hbm(other))
+
+
+def near_apply(evaluate, lists, near_data, other):
     bf16 = jnp.bfloat16
+    slots = NEAR - 1
+    smem = [
+        pltpu.SMEM((LEAVES, NEAR), jnp.int32),
+        pltpu.SMEM((LEAVES,), jnp.int32),
+        pltpu.SMEM((LEAVES, FAR), jnp.int32),
+        pltpu.SMEM((LEAVES,), jnp.int32),
+    ]
     out_shape = [shape(8, POINTS), shape(8, RANK)]
     out_specs = [VMEM] * 2
-    scratch = [pltpu.VMEM((WINDOW, PIECES, LANES), f32)]
+    scratch = smem + [
+        pltpu.SemaphoreType.DMA((13 if evaluate else 4,)),
+        pltpu.VMEM((WINDOW, PIECES, LANES), f32),
+    ]
     if evaluate:
-        out_shape = [pltpu.HBM(tiles.shape, f32)] + out_shape + [
-            shape(16, 256 * operands[9].shape[1] // LANES, dtype=bf16),
+        groups = other[5].shape[0]
+        out_shape = [pltpu.HBM((slots * LEAVES, POINTS, POINTS), f32)] + out_shape + [
+            shape(16, 2 * groups, dtype=bf16),
             shape(FAR_TOP, RANK, RANK, dtype=bf16),
             shape(LEAVES, POINTS),
             shape(LEAVES, FAR, RANK, RANK, dtype=bf16),
@@ -343,33 +433,28 @@
             shape(LEAVES, POINTS),
         ]
         out_specs = [HBM] + [VMEM] * 8
-        scratch += [
-            pltpu.VMEM((WINDOW, FIELD, LANES), f32),
-            pltpu.VMEM((LEAVES, 3, POINTS), f32),
-            pltpu.VMEM((LEAVES, POINTS, 8), f32),
-            pltpu.VMEM(operands[9].shape, jnp.int32),
+        scratch += [pltpu.VMEM((WINDOW, FIELD, LANES), f32)] + column_scratch() + [
+            pltpu.SMEM((groups,), jnp.int32),
+            pltpu.VMEM((1, groups), jnp.int32),
+            pltpu.SMEM((1, FAR_GROUP), jnp.int32),
+            pltpu.SMEM(other[8].shape, jnp.int32),
         ]
     scratch += [
         pltpu.VMEM((8, POINTS), f32),
         pltpu.VMEM((8, POINTS), f32),
         pltpu.VMEM((16, LANES), f32),
-        pltpu.VMEM((POINTS, LANES), f32),
-        pltpu.VMEM((NEAR, PIECES + FIELD, 8, LANES), f32),
-        pltpu.VMEM(tiles.shape, f32),
-    ]
-    if evaluate:
-        scratch.append(pltpu.SemaphoreType.DMA((7,)))
-    scratch.append(pltpu.SemaphoreType.DMA((LEAVES * PIECES,)))
-    places = [HBM] * 7 if evaluate else [VMEM, VMEM, HBM]
+    ] + loop_scratch(slots)
+    places = [HBM] * 10 if evaluate else [VMEM, VMEM, HBM]
+    other = in_hbm(*other) if evaluate else other[:2] + in_hbm(*other[2:])
     return pl.pallas_call(
         functools.partial(near_kernel, evaluate),
         out_shape=out_shape,
-        in_specs=[SMEM] + [VMEM] * 3 + places,
+        in_specs=[HBM] * 4 + [VMEM] * 4 + places,
         out_specs=out_specs,
         scratch_shapes=scratch,
-        cost_estimate=cost(3 * 10**8 if evaluate else 3 * 10**7, 2 * 10**7),
+        cost_estimate=cost(3 * 10**8, 2 * 10**7),
         compiler_params=pltpu.CompilerParams(vmem_limit_bytes=24 << 20),
-    )(*operands)
+    )(*in_hbm(*lists), *near_data, *other)
 
 
 def far_field(rows, base, leaf_far, select, group_coupling, own_pair, top_transfer, transfer,
@@ -480,18 +565,26 @@
     )
 
 
-def exchange(copies, stride, shift=0):
+def exchange(copies, stride):
     members = copies.shape[0]
     devices = lax.axis_size("wide") * lax.axis_size("narrow")
     span = members * stride
     groups = [
-        [(base + offset + stride * i + shift) % devices for i in range(members)]
+        [base + offset + stride * i for i in range(members)]
         for base in range(0, devices, span)
         for offset in range(stride)
     ]
     return lax.all_to_all(
         copies, ("wide", "narrow"), 0, 0, tiled=True, axis_index_groups=groups
     )
+
+
+def neighbours(fields):
+    wide = lax.axis_size("wide")
+    across = []
+    for first in range(1, wide - 1, 2):
+        across += [(first, first + 1), (first + 1, first)]
+    return lax.ppermute(fields, "wide", across)
 
 
 def local(
@@ -516,21 +609,24 @@
     groups = parent.shape[0]
     pairs = groups // 2
     wide = lax.axis_index("wide")
-    own_parent = lax.dynamic_slice_in_dim(parent, wide, 1, 0)
-    own_tops = lax.dynamic_slice_in_dim(top_far, own_parent[0], 1, 0)
-    table = [near_list, near_count, far_list, far_count, group_far, own_tops, own_parent]
-    table = jnp.concatenate([one.reshape(-1) for one in table])
+    lists = (near_list, near_count, far_list, far_count)
     tops = lax.dynamic_slice_in_dim(top_transfer, wide // 2 * 2, 2, 0)
     field, scalar = shape(8, POINTS), shape(8, LANES)
     packed_shape = shape(PAIR, PACK, LANES)
     scratch = [pltpu.VMEM((8, POINTS), f32)]
 
-    def gather(packed, rest, evaluate):
+    def gather(packed, values, own_other, other, evaluate):
         blocks = exchange(packed, 1)
-        shifted = exchange(packed, 1, NARROW)
-        (copies,) = simple(fold_kernel, [shape(pairs, 4, LANES)], [VMEM] * 2)(blocks, tops)
+        *own_tiles, own_near = own_apply(evaluate, values, own_other)
+        copies, fields = simple(
+            fold_kernel,
+            [shape(pairs, 4, LANES), shape(NARROW, packed.shape[1] - 4, LANES)],
+            [VMEM] * 2,
+        )(blocks, tops)
+        extra = neighbours(fields)
         rows = exchange(copies, PAIR).reshape(4 * pairs, LANES)
-        return rows, near_apply(evaluate, (table, blocks, shifted) + rest)
+        near = near_apply(evaluate, lists, (blocks, extra, values, own_near), other)
+        return rows, near, own_tiles
 
     packed, values, basis, transfer = simple(
         begin_kernel,
@@ -545,12 +641,13 @@
         + scratch
         + [pltpu.SemaphoreType.DMA((4,))],
     )(*in_hbm(warm_start, coords, jnp.transpose(leaf_basis, (0, 2, 1)), leaf_transfer))
-    rows, near = gather(
+    rows, near, (own_tiles,) = gather(
         packed,
-        (values,)
-        + in_hbm(
+        values,
+        coords,
+        (
             coords, noise_var, leaf_coupling, group_coupling[0], observed,
-            parent.reshape(1, groups), top_coupling,
+            parent, parent.reshape(1, groups), group_far, top_far.T, top_coupling,
         ),
         True,
     )
@@ -560,20 +657,20 @@
         residual_kernel, [packed_shape, field], [VMEM] * 10, scratch
     )(rows, base, leaf_far, *far_data, observed)
 
-    rows, near = gather(packed, (residual, noise, coupling) + in_hbm(tiles), False)
+    rows, near, _ = gather(packed, residual, own_tiles, (noise, coupling, tiles), False)
     packed, first, unit, norm = simple(
         second_kernel, [packed_shape, field, field, scalar], [VMEM] * 10
     )(rows, *near, *far_data, residual)
 
-    rows, near = gather(packed, (unit, noise, coupling) + in_hbm(tiles), False)
+    rows, near, _ = gather(packed, unit, own_tiles, (noise, coupling, tiles), False)
     sums, lower, lower_mapped, step, curve = simple(
         third_kernel,
-        [shape(PAIR, 8, LANES), field, field, scalar, scalar],
+        [shape(2 * PAIR, 8, LANES), field, field, scalar, scalar],
         [VMEM] * 12,
     )(rows, *near, *far_data, residual, first, norm)
     blocks = exchange(sums, 1)
-    (copies,) = simple(total_kernel, [shape(pairs, 2, LANES)], [VMEM])(blocks)
-    blocks = exchange(copies, PAIR)
+    (copies,) = simple(total_kernel, [shape(pairs // 2, 2, LANES)], [VMEM])(blocks)
+    blocks = exchange(copies, 2 * PAIR)
     (moved,) = simple(step_kernel, [field], [VMEM] * 3)(values, residual, step)
     own = shape(LEAVES, POINTS)
     return tuple(

time: 177 us -> 153 us (0.86)
  waiting for transfers between devices: 37.6 us -> 19.4 us
  blocking collectives: 42.7 us -> 27.7 us
  starting transfers between devices: 52.2 us -> 64.5 us
  local copies, waits for them, and re-layouts: 5.96 us -> 0.91 us
  Pallas kernels: 35.1 us -> 38.6 us
  between operations: 2.73 us -> 0.8 us
    all_to_all x7 -> x5, waiting for transfers between devices: 37.6 us -> 19 us  [exchange(): lax.all_to_all(copies, ('wide', 'narrow'), 0, 0, tiled=True, axis_index_g...]
    all_to_all x4 -> x3, blocking collectives: 42.7 us -> 27.7 us  [exchange(): lax.all_to_all(copies, ('wide', 'narrow'), 0, 0, tiled=True, axis_index_g...]
    ppermute x0 -> x3, starting transfers between devices: none -> 11.3 us  [neighbours(): return lax.ppermute(fields, 'wide', across)]
    pallas_call x5 -> x8, Pallas kernels: 4.29 us -> 14.5 us  [the longest x3 10.2 us: own_apply(): pl.pallas_call(functools.partial(own_kernel, evaluate), out_shape=out_sha...]
    pallas_call x3, Pallas kernels: 24.2 us -> 18.7 us  [near_apply(): pl.pallas_call(functools.partial(near_kernel, evaluate), out_shape=out_sh...]
    dynamic_slice x2 -> x0, local copies, waits for them, and re-layouts: 2.11 us -> none  [the longest x1 1.24 us: local(): own_parent = lax.dynamic_slice_in_dim(parent, wide, 1, 0)]
    all_to_all x7 -> x5, starting transfers between devices: 52.2 us -> 53.2 us  [exchange(): lax.all_to_all(copies, ('wide', 'narrow'), 0, 0, tiled=True, axis_index_g...]
  transfers between devices with their start and end apart: 7 -> 8, of which waited for: 6 -> 6; matrix products, arithmetic and copies ran while one was open for 3% -> 1% of each run, Pallas kernels for 15% -> 19%
where the time goes in v3:
time: 153 us; the launch traced here: 152 us
  starting transfers between devices  64.5 us (42%)
  Pallas kernels  38.6 us (25%)
  blocking collectives  27.7 us (18%)
  waiting for transfers between devices  19.4 us (13%)
    all_to_all x5, starting transfers between devices, exchange(): lax.all_to_all(copies, ('wide', 'narrow'), 0, 0, tiled=True, axis_index_g...  53.2 us
    all_to_all x3, blocking collectives, exchange(): lax.all_to_all(copies, ('wide', 'narrow'), 0, 0, tiled=True, axis_index_g...  27.7 us
    all_to_all x5, waiting for transfers between devices, exchange(): lax.all_to_all(copies, ('wide', 'narrow'), 0, 0, tiled=True, axis_index_g...  19 us
    pallas_call x3, Pallas kernels, near_apply(): pl.pallas_call(functools.partial(near_kernel, evaluate), out_shape=out_sh...  18.7 us
    ppermute x3, starting transfers between devices, neighbours(): return lax.ppermute(fields, 'wide', across)  11.3 us
    pallas_call x3, Pallas kernels, own_apply(): pl.pallas_call(functools.partial(own_kernel, evaluate), out_shape=out_sha...  10.2 us
  transfers between devices with their start and end apart: 8, of which 6 were waited for; matrix products, arithmetic and copies ran while one was open for 1% of the time, Pallas kernels for 19%

profile of v3, /device:TPU:1, one launch (start us, length us, event | category | flops | bytes accessed | tf_op | source)
XLA Modules:
  0.0 151.9 jit_solution(3512212782250595429)
XLA Ops:
  0.6 0.0 copy-start
  0.6 2.1 %shard_map.176 = (f32[8,52,128]{2,1,0:T(8,128)}, f32[8,512]{1,0:T(8,128)S(1)}, bf16[3,64,512]{2,1,0:T(8,128)(2,1)S(1)}, bf16[3,64,64]{2,1,0:T(8,128)(2,1)S(1)}) custom-call(f32[3,512]{1,0:T(4,128)} %warm_in.1, f32[3,3,512]{2,1,0:T(4,128)} %refs_8_.1, bf16[3,64,512]{2,1,0:T(8,128)(2,1)} %bitcast.10, bf16[3,64,64]{2,1,0:T(8,128)(2,1)} %transfer_in.1), custom_call_target="tpu_custom_call" | custom-call | flops 1000000 | bytes 1000000 | tf_op jit(solution)/shard_map/pallas_call | solution.py:631
  2.8 10.2 %all-to-all-start = ((f32[8,52,128]{2,1,0:T(8,128)}), f32[8,52,128]{2,1,0:T(8,128)S(1)}, u32[]{:S(2)}, u32[]{:S(2)}) async-start(f32[8,52,128]{2,1,0:T(8,128)} %get-tuple-element.38), calls=%async_computation | async-start | bytes 458752 | tf_op jit(solution)/shard_map/all_to_all | solution.py:577
  13.0 0.0 copy-done
  13.0 0.4 constant_dynamic-slice_fusion
  13.4 0.5 copy.20.top_transfer.refs_6_
  13.9 5.3 %all-to-all-done.blocks.refs_4_ = f32[8,52,128]{2,1,0:T(8,128)S(1)} async-done(((f32[8,52,128]{2,1,0:T(8,128)}), f32[8,52,128]{2,1,0:T(8,128)S(1)}, u32[]{:S(2)}, u32[]{:S(2)}) %all-to-all-start) | async-done | bytes 213024 | tf_op jit(solution)/shard_map/all_to_all | solution.py:577
  19.2 0.9 shard_map.177
  20.1 11.9 %all-to-all-start.1 = ((f32[64,4,128]{2,1,0:T(4,128)}), f32[64,4,128]{2,1,0:T(4,128)S(1)}, u32[]{:S(2)}, u32[]{:S(2)}) async-start(f32[64,4,128]{2,1,0:T(4,128)} %get-tuple-element.39), calls=%async_computation.1 | async-start | bytes 262144 | tf_op jit(solution)/shard_map/all_to_all | solution.py:577
  32.0 3.7 %collective-permute-start = (f32[4,48,128]{2,1,0:T(8,128)S(1)}, f32[4,48,128]{2,1,0:T(8,128)S(1)}, u32[]{:S(2)}, u32[]{:S(2)}) collective-permute-start(f32[4,48,128]{2,1,0:T(8,128)S(1)} %get-tuple-element.40), channel_id=1, source_target_pairs={{4,8},{8,4},{12,16},{16,12},{20,24},{24,20},{28,32},{32,28},{36,40... | collective-permute-start | bytes 294920 | tf_op jit(solution)/shard_map/ppermute | solution.py:587
  35.8 6.0 %shard_map.178 = (f32[3,512,512]{2,1,0:T(8,128)}, f32[8,512]{1,0:T(8,128)S(1)}) custom-call(f32[8,512]{1,0:T(8,128)S(1)} %get-tuple-element.41.refs_0_.refs_6_.warm, f32[3,3,512]{2,1,0:T(4,128)} %refs_8_.1), custom_call_target="tpu_custom_call" | custom-call | flops 100000000 | bytes 4000000 | tf_op jit(solution)/shard_map/pallas_call | solution.py:399
  41.8 0.0 collective-permute-done.refs_5_
  41.8 10.6 %shard_map.179 = (f32[9,512,512]{2,1,0:T(8,128)}, f32[8,512]{1,0:T(8,128)S(1)}, f32[8,64]{1,0:T(8,128)S(1)}, bf16[16,256]{1,0:T(8,128)(2,1)S(1)}, bf16[4,64,64]{...) custom-call(s32[3,4]{1,0:T(4,128)} %refs_0_.5, ...), custom_call_target="tpu_custom_call" | custom-call | flops 300000000 | bytes 20000000 | tf_op jit(solution)/shard_map/pallas_call | solution.py:449
  52.4 0.0 all-to-all-done.1
  52.4 1.2 shard_map.180
  53.6 7.9 %all_to_all.40.blocks.refs_4_ = f32[8,16,128]{2,1,0:T(8,128)S(1)} all-to-all(f32[8,16,128]{2,1,0:T(8,128)S(1)} %get-tuple-element.51), channel_id=1, replica_groups={{0,1,2,3,4,5,6,7},{8,9,10,11,12,13,14,15},{16,17,18,19,20,21,22,23},{24..., dimensions={0} | all-to-all | bytes 131072 | tf_op jit(solution)/shard_map/all_to_all | solution.py:577
  61.5 0.9 shard_map.181
  62.4 11.4 %all-to-all-start.3 = ((f32[64,4,128]{2,1,0:T(4,128)}), f32[64,4,128]{2,1,0:T(4,128)S(1)}, u32[]{:S(2)}, u32[]{:S(2)}) async-start(f32[64,4,128]{2,1,0:T(4,128)} %get-tuple-element.52), calls=%async_computation.3 | async-start | bytes 262144 | tf_op jit(solution)/shard_map/all_to_all | solution.py:577
  73.8 3.8 %collective-permute-start.1 = (f32[4,12,128]{2,1,0:T(8,128)S(1)}, f32[4,12,128]{2,1,0:T(8,128)S(1)}, u32[]{:S(2)}, u32[]{:S(2)}) collective-permute-start(f32[4,12,128]{2,1,0:T(8,128)S(1)} %get-tuple-element.53), channel_id=1, source_target_pairs={{4,8},{8,4},{12,16},{16,12},{20,24},{24,20},{28,32},{32,28},{36,40... | collective-permute-start | bytes 73736 | tf_op jit(solution)/shard_map/ppermute | solution.py:587
  77.6 2.1 %shard_map.182.refs_7_ = f32[8,512]{1,0:T(8,128)S(1)} custom-call(f32[8,512]{1,0:T(8,128)S(1)} %get-tuple-element.54.refs_0_.refs_6_.refs_9_.residual, f32[3,512,512]{2,1,0:T(8,128)} %get-tuple-element.55.refs_1_), custom_call_target="tpu_custom_call" | custom-call | flops 100000000 | bytes 4000000 | tf_op jit(solution)/shard_map/pallas_call | solution.py:399
  79.7 0.2 collective-permute-done.1.refs_5_
  79.9 4.1 %shard_map.183 = (f32[8,512]{1,0:T(8,128)S(1)}, f32[8,64]{1,0:T(8,128)S(1)}) custom-call(s32[3,4]{1,0:T(4,128)} %refs_0_.5, s32[3]{0:T(128)} %refs_1_.7, s32[3,8]{1,0:T(4,128)} %refs_2_.5, s32[3]{0:T(128)} %refs_3_.5, f32[8,16,128]{2,1,0:T(8,128)S(1)} %all_to_all.40.blocks.refs_4_, f32[4,12,128]{2,1,0:T(8,128)S(1)} %collective-permute-done.1.refs_5_, ...), custom_call_target="tpu_custom_call" | custom-call | flops 300000000 | bytes 20000000 | tf_op jit(solution)/shard_map/pallas_call | solution.py:449
  83.9 1.3 all-to-all-done.3
  85.3 1.2 shard_map.184
  86.5 9.4 %all_to_all.41.blocks.refs_4_ = f32[8,16,128]{2,1,0:T(8,128)S(1)} all-to-all(f32[8,16,128]{2,1,0:T(8,128)S(1)} %get-tuple-element.61), channel_id=1, replica_groups={{0,1,2,3,4,5,6,7},{8,9,10,11,12,13,14,15},{16,17,18,19,20,21,22,23},{24..., dimensions={0} | all-to-all | bytes 131072 | tf_op jit(solution)/shard_map/all_to_all | solution.py:577
  95.9 0.9 shard_map.185
  96.8 10.2 %all-to-all-start.5 = ((f32[64,4,128]{2,1,0:T(4,128)}), f32[64,4,128]{2,1,0:T(4,128)S(1)}, u32[]{:S(2)}, u32[]{:S(2)}) async-start(f32[64,4,128]{2,1,0:T(4,128)} %get-tuple-element.62), calls=%async_computation.5 | async-start | bytes 262144 | tf_op jit(solution)/shard_map/all_to_all | solution.py:577
  107.0 3.8 %collective-permute-start.2 = (f32[4,12,128]{2,1,0:T(8,128)S(1)}, f32[4,12,128]{2,1,0:T(8,128)S(1)}, u32[]{:S(2)}, u32[]{:S(2)}) collective-permute-start(f32[4,12,128]{2,1,0:T(8,128)S(1)} %get-tuple-element.63), channel_id=1, source_target_pairs={{4,8},{8,4},{12,16},{16,12},{20,24},{24,20},{28,32},{32,28},{36,40... | collective-permute-start | bytes 73736 | tf_op jit(solution)/shard_map/ppermute | solution.py:587
  110.8 2.1 %shard_map.186.refs_7_ = f32[8,512]{1,0:T(8,128)S(1)} custom-call(f32[8,512]{1,0:T(8,128)S(1)} %get-tuple-element.64.refs_0_.refs_6_, f32[3,512,512]{2,1,0:T(8,128)} %get-tuple-element.55.refs_1_), custom_call_target="tpu_custom_call" | custom-call | flops 100000000 | bytes 4000000 | tf_op jit(solution)/shard_map/pallas_call | solution.py:399
  112.9 0.2 collective-permute-done.2.refs_5_
  113.0 4.1 %shard_map.187 = (f32[8,512]{1,0:T(8,128)S(1)}, f32[8,64]{1,0:T(8,128)S(1)}) custom-call(s32[3,4]{1,0:T(4,128)} %refs_0_.5, s32[3]{0:T(128)} %refs_1_.7, s32[3,8]{1,0:T(4,128)} %refs_2_.5, s32[3]{0:T(128)} %refs_3_.5, f32[8,16,128]{2,1,0:T(8,128)S(1)} %all_to_all.41.blocks.refs_4_, f32[4,12,128]{2,1,0:T(8,128)S(1)} %collective-permute-done.2.refs_5_, ...), custom_call_target="tpu_custom_call" | custom-call | flops 300000000 | bytes 20000000 | tf_op jit(solution)/shard_map/pallas_call | solution.py:449
  117.1 1.3 all-to-all-done.5
  118.5 1.0 shard_map.188
  119.5 10.4 %all_to_all.42.blocks = f32[16,8,128]{2,1,0:T(8,128)S(1)} all-to-all(f32[16,8,128]{2,1,0:T(8,128)S(1)} %get-tuple-element.69), channel_id=1, replica_groups={{0,1,2,3,4,5,6,7,8,9,10,11,12,13,14,15},{16,17,18,19,20,21,22,23,24,25,..., dimensions={0} | all-to-all | bytes 131072 | tf_op jit(solution)/shard_map/all_to_all | solution.py:577
  129.8 0.6 shard_map.189
  130.5 9.5 %all-to-all-start.7 = ((f32[32,2,128]{2,1,0:T(2,128)}), f32[32,2,128]{2,1,0:T(2,128)S(1)}, u32[]{:S(2)}, u32[]{:S(2)}) async-start(f32[32,2,128]{2,1,0:T(2,128)} %shard_map.189), calls=%async_computation.7 | async-start | bytes 65536 | tf_op jit(solution)/shard_map/all_to_all | solution.py:577
  140.0 11.1 %all-to-all-done.7.blocks = f32[32,2,128]{2,1,0:T(2,128)S(1)} async-done(((f32[32,2,128]{2,1,0:T(2,128)}), f32[32,2,128]{2,1,0:T(2,128)S(1)}, u32[]{:S(2)}, u32[]{:S(2)}) %all-to-all-start.7) | async-done | bytes 32800 | tf_op jit(solution)/shard_map/all_to_all | solution.py:577
  151.1 0.8 shard_map.191
  (1 shorter events, 0.0 us)
Async XLA Ops:
  0.6 12.4 %copy-start = (bf16[128,64,64]{0,2,1:T(8,128)(2,1)S(1)}, bf16[128,64,64]{0,2,1:T(8,128)(2,1)}, u32[]{:S(2)}) copy-start(bf16[128,64,64]{0,2,1:T(8,128)(2,1)} %param.25) | copy-start | bytes 3145732
  2.8 16.4 %all-to-all-start = ((f32[8,52,128]{2,1,0:T(8,128)}), f32[8,52,128]{2,1,0:T(8,128)S(1)}, u32[]{:S(2)}, u32[]{:S(2)}) async-start(f32[8,52,128]{2,1,0:T(8,128)} %get-tuple-element.38), calls=%async_computation | async-start | bytes 458752 | tf_op jit(solution)/shard_map/all_to_all | solution.py:577
  20.1 32.3 %all-to-all-start.1 = ((f32[64,4,128]{2,1,0:T(4,128)}), f32[64,4,128]{2,1,0:T(4,128)S(1)}, u32[]{:S(2)}, u32[]{:S(2)}) async-start(f32[64,4,128]{2,1,0:T(4,128)} %get-tuple-element.39), calls=%async_computation.1 | async-start | bytes 262144 | tf_op jit(solution)/shard_map/all_to_all | solution.py:577
  32.0 9.8 %collective-permute-start = (f32[4,48,128]{2,1,0:T(8,128)S(1)}, f32[4,48,128]{2,1,0:T(8,128)S(1)}, u32[]{:S(2)}, u32[]{:S(2)}) collective-permute-start(f32[4,48,128]{2,1,0:T(8,128)S(1)} %get-tuple-element.40), channel_id=1, source_target_pairs={{4,8},{8,4},{12,16},{16,12},{20,24},{24,20},{28,32},{32,28},{36,40... | collective-permute-start | bytes 294920 | tf_op jit(solution)/shard_map/ppermute | solution.py:587
  62.4 22.9 %all-to-all-start.3 = ((f32[64,4,128]{2,1,0:T(4,128)}), f32[64,4,128]{2,1,0:T(4,128)S(1)}, u32[]{:S(2)}, u32[]{:S(2)}) async-start(f32[64,4,128]{2,1,0:T(4,128)} %get-tuple-element.52), calls=%async_computation.3 | async-start | bytes 262144 | tf_op jit(solution)/shard_map/all_to_all | solution.py:577
  73.8 6.0 %collective-permute-start.1 = (f32[4,12,128]{2,1,0:T(8,128)S(1)}, f32[4,12,128]{2,1,0:T(8,128)S(1)}, u32[]{:S(2)}, u32[]{:S(2)}) collective-permute-start(f32[4,12,128]{2,1,0:T(8,128)S(1)} %get-tuple-element.53), channel_id=1, source_target_pairs={{4,8},{8,4},{12,16},{16,12},{20,24},{24,20},{28,32},{32,28},{36,40... | collective-permute-start | bytes 73736 | tf_op jit(solution)/shard_map/ppermute | solution.py:587
  96.8 21.7 %all-to-all-start.5 = ((f32[64,4,128]{2,1,0:T(4,128)}), f32[64,4,128]{2,1,0:T(4,128)S(1)}, u32[]{:S(2)}, u32[]{:S(2)}) async-start(f32[64,4,128]{2,1,0:T(4,128)} %get-tuple-element.62), calls=%async_computation.5 | async-start | bytes 262144 | tf_op jit(solution)/shard_map/all_to_all | solution.py:577
  107.0 6.0 %collective-permute-start.2 = (f32[4,12,128]{2,1,0:T(8,128)S(1)}, f32[4,12,128]{2,1,0:T(8,128)S(1)}, u32[]{:S(2)}, u32[]{:S(2)}) collective-permute-start(f32[4,12,128]{2,1,0:T(8,128)S(1)} %get-tuple-element.63), channel_id=1, source_target_pairs={{4,8},{8,4},{12,16},{16,12},{20,24},{24,20},{28,32},{32,28},{36,40... | collective-permute-start | bytes 73736 | tf_op jit(solution)/shard_map/ppermute | solution.py:587
  130.5 20.6 %all-to-all-start.7 = ((f32[32,2,128]{2,1,0:T(2,128)}), f32[32,2,128]{2,1,0:T(2,128)S(1)}, u32[]{:S(2)}, u32[]{:S(2)}) async-start(f32[32,2,128]{2,1,0:T(2,128)} %shard_map.189), calls=%async_computation.7 | async-start | bytes 65536 | tf_op jit(solution)/shard_map/all_to_all | solution.py:577

commit v4 on v3

--- a/solution.py
+++ b/solution.py
@@ -127,7 +127,8 @@
     pack(field, jnp.zeros((1, RANK), f32), basis, transfer, packed)
 
 
-def fold_kernel(blocks, top_transfer, copies, fields):
+def fold_kernel(blocks, top_transfer, *refs):
+    copies, fields = refs[-2:]
     sums = []
     for row in (FIELD + 3, FIELD):
         for group in range(2):
@@ -254,89 +255,14 @@
             tile_copy(True, slots, kept, tiles, sems, leaf, quarter).wait()
 
 
-def own_kernel(evaluate, *refs):
-    if evaluate:
-        values, coords_in, tiles, own_near, coords, columns, scratch, sem, *loop = refs
-        (copy,) = fetch([(coords_in, coords)], sem)
-        copy.wait()
-        for leaf in range(LEAVES):
-            columns[leaf] = jnp.transpose(padded(coords.at[leaf], scratch))
-    else:
-        values, tiles, own_near, *loop = refs
-        coords = columns = None
-    spread, totals, kept, sems = loop
-    if not evaluate:
-        begin_tiles(1, kept, tiles, sems)
-
-    def fill(leaf, slot):
-        def field(piece):
-            part = values[:, piece * LANES : (piece + 1) * LANES]
-            return jnp.sum(jnp.where(rows_of(part) == leaf, part, 0.0), axis=0, keepdims=True)
-
-        def point(at):
-            axis, piece = divmod(at, PIECES)
-            return coords[leaf, axis : axis + 1, piece * LANES : (piece + 1) * LANES]
-
-        return field, point
-
-    tile_products(evaluate, 1, fill, own_near, columns, spread, totals, kept, tiles, sems)
-    if evaluate:
-        end_tiles(1, kept, tiles, sems)
-
-
-def near_kernel(evaluate, *refs):
-    if evaluate:
-        (near_list_in, near_count_in, far_list_in, far_count_in, blocks, extra, values, own_near,
-         coords_in, noise_in, coupling_in, group_in, observed_in, parent_in, parents_in,
-         group_far_in, top_far_in, top_in, tiles, base, leaf_far, select, own_pair, noise,
-         coupling, group, observed, near_list, near_count, far_list, far_count, sems, window,
-         sources, coords, columns, parent, parents, group_far, top_far, scratch, near, coefs,
-         spread, totals, kept, tile_sems) = refs
-    else:
-        (near_list_in, near_count_in, far_list_in, far_count_in, blocks, extra, values, own_near,
-         noise, coupling, tiles, base, leaf_far, near_list, near_count, far_list, far_count, sems,
-         window, scratch, near, coefs, spread, totals, kept, tile_sems) = refs
-    slots = NEAR - 1
-    pairs = [
-        (near_list_in, near_list), (near_count_in, near_count),
-        (far_list_in, far_list), (far_count_in, far_count),
-    ]
-    if evaluate:
-        pairs += [
-            (parent_in, parent), (group_far_in, group_far), (top_far_in, top_far),
-            (parents_in, parents), (coords_in, coords), (coupling_in, coupling),
-            (noise_in, noise), (group_in, group), (observed_in, observed),
-        ]
-    copies = fetch(pairs, sems)
-    if not evaluate:
-        begin_tiles(slots, kept, tiles, tile_sems)
+def leaf_coupling(blocks, coupling, far_list, far_count, coefs, leaf_far):
     wide = lax.axis_index("wide")
     own = lax.rem(wide, 2)
-    first_group = wide - own
-    for device in range(PAIR + NARROW):
-        held, index = (blocks, device) if device < PAIR else (extra, device - PAIR)
-        more = PACK if device < PAIR else FIELD
-        for leaf in range(LEAVES):
-            at = device * LEAVES + leaf
-            window[at] = held[index, leaf * PIECES : (leaf + 1) * PIECES, :]
-            if evaluate:
-                rows = more + leaf * FIELD
-                sources[at] = held[index, rows : rows + FIELD, :]
     coefs[...] = jnp.zeros(coefs.shape, f32)
     for device in range(NARROW):
         coefs[device * LEAVES : (device + 1) * LEAVES, :] = blocks[
             own * NARROW + device, FIELD : FIELD + LEAVES, :
         ]
-    for copy in copies:
-        copy.wait()
-    if evaluate:
-        own_parent = parent[wide]
-        top_copy = pltpu.make_async_copy(top_in.at[own_parent], own_pair, sems.at[0])
-        top_copy.start()
-        for leaf in range(LEAVES):
-            columns[leaf] = jnp.transpose(padded(coords.at[leaf], scratch))
-        select[...] = selection(group_far, top_far, own_parent, parents)
-
     lane = lax.broadcasted_iota(jnp.int32, (16, LANES), 1)
     row = lax.broadcasted_iota(jnp.int32, (16, LANES), 0)
     far_rows = []
@@ -352,7 +278,132 @@
             total = total + jnp.where(listed, out[:, two * LANES : (two + 1) * LANES], 0.0)
         far_rows.append(fold_half(jnp.sum(total, axis=0, keepdims=True)))
     leaf_far[...] = row_by_leaf([jnp.broadcast_to(one, (8, RANK)) for one in far_rows])
+
+
+def own_kernel(evaluate, *refs):
+    if evaluate:
+        values, coords_in, tiles, own_near, coords, columns, scratch, sem, *loop = refs
+        (copy,) = fetch([(coords_in, coords)], sem)
+        copy.wait()
+        for leaf in range(LEAVES):
+            columns[leaf] = jnp.transpose(padded(coords.at[leaf], scratch))
+    else:
+        (values, tiles, blocks, coupling, far_list_in, far_count_in, own_near, leaf_far, far_list,
+         far_count, coefs, sem, *loop) = refs
+        coords = columns = None
+    spread, totals, kept, sems = loop
+    if not evaluate:
+        copies = fetch([(far_list_in, far_list), (far_count_in, far_count)], sem)
+        begin_tiles(1, kept, tiles, sems)
+        for copy in copies:
+            copy.wait()
+        leaf_coupling(blocks, coupling, far_list, far_count, coefs, leaf_far)
+
+    def fill(leaf, slot):
+        def field(piece):
+            part = values[:, piece * LANES : (piece + 1) * LANES]
+            return jnp.sum(jnp.where(rows_of(part) == leaf, part, 0.0), axis=0, keepdims=True)
+
+        def point(at):
+            axis, piece = divmod(at, PIECES)
+            return coords[leaf, axis : axis + 1, piece * LANES : (piece + 1) * LANES]
+
+        return field, point
+
+    tile_products(evaluate, 1, fill, own_near, columns, spread, totals, kept, tiles, sems)
+    if evaluate:
+        end_tiles(1, kept, tiles, sems)
+
+
+def mid_kernel(
+    blocks, far_list_in, far_count_in, parent_in, group_far_in, top_far_in, parents_in,
+    coupling_in, noise_in, group_in, observed_in, top_in,
+    leaf_far, select, own_pair, noise, coupling, group, observed,
+    far_list, far_count, parent, group_far, top_far, parents, coefs, sems,
+):
+    copies = fetch(
+        [
+            (parent_in, parent), (group_far_in, group_far), (top_far_in, top_far),
+            (parents_in, parents), (far_list_in, far_list), (far_count_in, far_count),
+            (coupling_in, coupling), (noise_in, noise), (group_in, group),
+            (observed_in, observed),
+        ],
+        sems,
+    )
+    for copy in copies[:4]:
+        copy.wait()
+    own_parent = parent[lax.axis_index("wide")]
+    top_copy = pltpu.make_async_copy(top_in.at[own_parent], own_pair, sems.at[0])
+    top_copy.start()
+    select[...] = selection(group_far, top_far, own_parent, parents)
+    for copy in copies[4:]:
+        copy.wait()
+    leaf_coupling(blocks, coupling, far_list, far_count, coefs, leaf_far)
+    top_copy.wait()
+
+
+def mid_apply(blocks, other):
+    bf16 = jnp.bfloat16
+    groups = other[2].shape[0]
+    return pl.pallas_call(
+        mid_kernel,
+        out_shape=[
+            shape(8, RANK),
+            shape(16, 2 * groups, dtype=bf16),
+            shape(FAR_TOP, RANK, RANK, dtype=bf16),
+            shape(LEAVES, POINTS),
+            shape(LEAVES, FAR, RANK, RANK, dtype=bf16),
+            shape(FAR_GROUP, RANK, RANK, dtype=bf16),
+            shape(LEAVES, POINTS),
+        ],
+        in_specs=[VMEM] + [HBM] * len(other),
+        out_specs=[VMEM] * 7,
+        scratch_shapes=[
+            pltpu.SMEM((LEAVES, FAR), jnp.int32),
+            pltpu.SMEM((LEAVES,), jnp.int32),
+            pltpu.SMEM((groups,), jnp.int32),
+            pltpu.SMEM((1, FAR_GROUP), jnp.int32),
+            pltpu.SMEM(other[4].shape, jnp.int32),
+            pltpu.VMEM((1, groups), jnp.int32),
+            pltpu.VMEM((16, LANES), f32),
+            pltpu.SemaphoreType.DMA((10,)),
+        ],
+        cost_estimate=cost(10**7, 2 * 10**6),
+        compiler_params=pltpu.CompilerParams(vmem_limit_bytes=8 << 20),
+    )(blocks, *in_hbm(*other))
+
+
+def near_kernel(evaluate, *refs):
+    if evaluate:
+        (near_list_in, near_count_in, blocks, extra, values, own_near, noise, coords_in, tiles,
+         base, near_list, near_count, sems, window, sources, coords, columns, scratch, near,
+         spread, totals, kept, tile_sems) = refs
+    else:
+        (near_list_in, near_count_in, blocks, extra, values, own_near, noise, tiles, base,
+         near_list, near_count, sems, window, scratch, near, spread, totals, kept,
+         tile_sems) = refs
+    slots = NEAR - 1
+    pairs = [(near_list_in, near_list), (near_count_in, near_count)]
+    copies = fetch(pairs + ([(coords_in, coords)] if evaluate else []), sems)
+    if not evaluate:
+        begin_tiles(slots, kept, tiles, tile_sems)
+    wide = lax.axis_index("wide")
+    first_group = wide - lax.rem(wide, 2)
+    for device in range(PAIR + NARROW):
+        held, index = (blocks, device) if device < PAIR else (extra, device - PAIR)
+        more = PACK if device < PAIR else FIELD
+        for leaf in range(LEAVES):
+            at = device * LEAVES + leaf
+            window[at] = held[index, leaf * PIECES : (leaf + 1) * PIECES, :]
+            if evaluate:
+                rows = more + leaf * FIELD
+                sources[at] = held[index, rows : rows + FIELD, :]
     local_part = padded(noise, scratch) * values[...] + own_near[...]
+    for copy in copies:
+        copy.wait()
+    if evaluate:
+        for leaf in range(LEAVES):
+            columns[leaf] = jnp.transpose(padded(coords.at[leaf], scratch))
 
     def fill(leaf, slot):
         listed = near_list[leaf, slot + 1]
@@ -371,7 +422,6 @@
     )
     base[...] = local_part + near[...]
     if evaluate:
-        top_copy.wait()
         end_tiles(slots, kept, tiles, tile_sems)
 
 
@@ -388,73 +438,57 @@
     return [pltpu.VMEM((LEAVES, 3, POINTS), f32), pltpu.VMEM((LEAVES, POINTS, 8), f32)]
 
 
-def own_apply(evaluate, values, other):
-    out_shape, out_specs, scratch = [shape(8, POINTS)], [VMEM], []
+def own_apply(evaluate, values, other, later=(), lists=()):
+    out_shape, out_specs = [shape(8, POINTS)], [VMEM]
     if evaluate:
         out_shape = [pltpu.HBM((LEAVES, POINTS, POINTS), f32)] + out_shape
         out_specs = [HBM] + out_specs
         scratch = column_scratch() + [
             pltpu.VMEM((8, POINTS), f32), pltpu.SemaphoreType.DMA((1,))
         ]
+    else:
+        out_shape.append(shape(8, RANK))
+        out_specs.append(VMEM)
+        scratch = [
+            pltpu.SMEM((LEAVES, FAR), jnp.int32),
+            pltpu.SMEM((LEAVES,), jnp.int32),
+            pltpu.VMEM((16, LANES), f32),
+            pltpu.SemaphoreType.DMA((2,)),
+        ]
     return pl.pallas_call(
         functools.partial(own_kernel, evaluate),
         out_shape=out_shape,
-        in_specs=[VMEM, HBM],
+        in_specs=[VMEM, HBM] + [VMEM] * len(later) + [HBM] * len(lists),
         out_specs=out_specs,
         scratch_shapes=scratch + loop_scratch(1),
         cost_estimate=cost(10**8, 4 * 10**6),
         compiler_params=pltpu.CompilerParams(vmem_limit_bytes=16 << 20),
-    )(values, *in_hbm(other))
+    )(values, *in_hbm(other), *later, *in_hbm(*lists))
 
 
 def near_apply(evaluate, lists, near_data, other):
-    bf16 = jnp.bfloat16
     slots = NEAR - 1
-    smem = [
+    out_shape, out_specs = [shape(8, POINTS)], [VMEM]
+    scratch = [
         pltpu.SMEM((LEAVES, NEAR), jnp.int32),
         pltpu.SMEM((LEAVES,), jnp.int32),
-        pltpu.SMEM((LEAVES, FAR), jnp.int32),
-        pltpu.SMEM((LEAVES,), jnp.int32),
-    ]
-    out_shape = [shape(8, POINTS), shape(8, RANK)]
-    out_specs = [VMEM] * 2
-    scratch = smem + [
-        pltpu.SemaphoreType.DMA((13 if evaluate else 4,)),
+        pltpu.SemaphoreType.DMA((3,)),
         pltpu.VMEM((WINDOW, PIECES, LANES), f32),
     ]
     if evaluate:
-        groups = other[5].shape[0]
-        out_shape = [pltpu.HBM((slots * LEAVES, POINTS, POINTS), f32)] + out_shape + [
-            shape(16, 2 * groups, dtype=bf16),
-            shape(FAR_TOP, RANK, RANK, dtype=bf16),
-            shape(LEAVES, POINTS),
-            shape(LEAVES, FAR, RANK, RANK, dtype=bf16),
-            shape(FAR_GROUP, RANK, RANK, dtype=bf16),
-            shape(LEAVES, POINTS),
-        ]
-        out_specs = [HBM] + [VMEM] * 8
-        scratch += [pltpu.VMEM((WINDOW, FIELD, LANES), f32)] + column_scratch() + [
-            pltpu.SMEM((groups,), jnp.int32),
-            pltpu.VMEM((1, groups), jnp.int32),
-            pltpu.SMEM((1, FAR_GROUP), jnp.int32),
-            pltpu.SMEM(other[8].shape, jnp.int32),
-        ]
-    scratch += [
-        pltpu.VMEM((8, POINTS), f32),
-        pltpu.VMEM((8, POINTS), f32),
-        pltpu.VMEM((16, LANES), f32),
-    ] + loop_scratch(slots)
-    places = [HBM] * 10 if evaluate else [VMEM, VMEM, HBM]
-    other = in_hbm(*other) if evaluate else other[:2] + in_hbm(*other[2:])
+        out_shape = [pltpu.HBM((slots * LEAVES, POINTS, POINTS), f32)] + out_shape
+        out_specs = [HBM] + out_specs
+        scratch += [pltpu.VMEM((WINDOW, FIELD, LANES), f32)] + column_scratch()
+    scratch += [pltpu.VMEM((8, POINTS), f32)] * 2 + loop_scratch(slots)
     return pl.pallas_call(
         functools.partial(near_kernel, evaluate),
         out_shape=out_shape,
-        in_specs=[HBM] * 4 + [VMEM] * 4 + places,
+        in_specs=[HBM] * 2 + [VMEM] * 5 + [HBM],
         out_specs=out_specs,
         scratch_shapes=scratch,
         cost_estimate=cost(3 * 10**8, 2 * 10**7),
         compiler_params=pltpu.CompilerParams(vmem_limit_bytes=24 << 20),
-    )(*in_hbm(*lists), *near_data, *other)
+    )(*in_hbm(*lists), *near_data, *in_hbm(other))
 
 
 def far_field(rows, base, leaf_far, select, group_coupling, own_pair, top_transfer, transfer,
@@ -594,7 +628,7 @@
     warm_start,
     leaf_basis,
     leaf_transfer,
-    leaf_coupling,
+    leaf_coupling_matrices,
     group_coupling,
     top_transfer,
     top_coupling,
@@ -609,24 +643,29 @@
     groups = parent.shape[0]
     pairs = groups // 2
     wide = lax.axis_index("wide")
-    lists = (near_list, near_count, far_list, far_count)
     tops = lax.dynamic_slice_in_dim(top_transfer, wide // 2 * 2, 2, 0)
     field, scalar = shape(8, POINTS), shape(8, LANES)
     packed_shape = shape(PAIR, PACK, LANES)
     scratch = [pltpu.VMEM((8, POINTS), f32)]
 
-    def gather(packed, values, own_other, other, evaluate):
-        blocks = exchange(packed, 1)
-        *own_tiles, own_near = own_apply(evaluate, values, own_other)
+    def wide_gather(blocks, *first):
         copies, fields = simple(
             fold_kernel,
-            [shape(pairs, 4, LANES), shape(NARROW, packed.shape[1] - 4, LANES)],
-            [VMEM] * 2,
-        )(blocks, tops)
+            [shape(pairs, 4, LANES), shape(NARROW, blocks.shape[1] - 4, LANES)],
+            [VMEM] * (2 + len(first)),
+        )(blocks, tops, *first)
         extra = neighbours(fields)
-        rows = exchange(copies, PAIR).reshape(4 * pairs, LANES)
-        near = near_apply(evaluate, lists, (blocks, extra, values, own_near), other)
-        return rows, near, own_tiles
+        return extra, exchange(copies, PAIR).reshape(4 * pairs, LANES)
+
+    def gather(packed, values):
+        blocks = exchange(packed, 1)
+        extra, rows = wide_gather(blocks)
+        own_near, leaf_far = own_apply(
+            False, values, own_tiles, (blocks, coupling), (far_list, far_count)
+        )
+        near = (blocks, extra, values, own_near, noise)
+        (base,) = near_apply(False, (near_list, near_count), near, tiles)
+        return rows, base, leaf_far
 
     packed, values, basis, transfer = simple(
         begin_kernel,
@@ -641,36 +680,37 @@
         + scratch
         + [pltpu.SemaphoreType.DMA((4,))],
     )(*in_hbm(warm_start, coords, jnp.transpose(leaf_basis, (0, 2, 1)), leaf_transfer))
-    rows, near, (own_tiles,) = gather(
-        packed,
-        values,
-        coords,
+    blocks = exchange(packed, 1)
+    own_tiles, own_near = own_apply(True, values, coords)
+    extra, rows = wide_gather(blocks, own_near)
+    leaf_far, select, own_pair, noise, coupling, group, observed = mid_apply(
+        blocks,
         (
-            coords, noise_var, leaf_coupling, group_coupling[0], observed,
-            parent, parent.reshape(1, groups), group_far, top_far.T, top_coupling,
+            far_list, far_count, parent, group_far, top_far.T, parent.reshape(1, groups),
+            leaf_coupling_matrices, noise_var, group_coupling[0], observed, top_coupling,
         ),
-        True,
-    )
-    tiles, base, leaf_far, select, own_pair, noise, coupling, group, observed = near
+    )
+    near = (blocks, extra, values, own_near, noise)
+    tiles, base = near_apply(True, (near_list, near_count), near, coords)
     far_data = (select, group, own_pair, tops, transfer, basis)
     packed, residual = simple(
         residual_kernel, [packed_shape, field], [VMEM] * 10, scratch
     )(rows, base, leaf_far, *far_data, observed)
 
-    rows, near, _ = gather(packed, residual, own_tiles, (noise, coupling, tiles), False)
+    rows, *near = gather(packed, residual)
     packed, first, unit, norm = simple(
         second_kernel, [packed_shape, field, field, scalar], [VMEM] * 10
     )(rows, *near, *far_data, residual)
 
-    rows, near, _ = gather(packed, unit, own_tiles, (noise, coupling, tiles), False)
+    rows, *near = gather(packed, unit)
     sums, lower, lower_mapped, step, curve = simple(
         third_kernel,
-        [shape(2 * PAIR, 8, LANES), field, field, scalar, scalar],
+        [shape(PAIR, 8, LANES), field, field, scalar, scalar],
         [VMEM] * 12,
     )(rows, *near, *far_data, residual, first, norm)
     blocks = exchange(sums, 1)
-    (copies,) = simple(total_kernel, [shape(pairs // 2, 2, LANES)], [VMEM])(blocks)
-    blocks = exchange(copies, 2 * PAIR)
+    (copies,) = simple(total_kernel, [shape(pairs, 2, LANES)], [VMEM])(blocks)
+    blocks = exchange(copies, PAIR)
     (moved,) = simple(step_kernel, [field], [VMEM] * 3)(values, residual, step)
     own = shape(LEAVES, POINTS)
     return tuple(

time: 153 us -> 153 us (level)
  waiting for transfers between devices: 19.4 us -> 16.4 us
    all_to_all x5, waiting for transfers between devices: 19 us -> 14 us  [exchange(): lax.all_to_all(copies, ('wide', 'narrow'), 0, 0, tiled=True, axis_index_g...]
    ppermute x3, waiting for transfers between devices: 0.34 us -> 2.4 us  [neighbours(): return lax.ppermute(fields, 'wide', across)]
    all_to_all x5, starting transfers between devices: 53.2 us -> 55 us  [exchange(): lax.all_to_all(copies, ('wide', 'narrow'), 0, 0, tiled=True, axis_index_g...]
    pallas_call x5 -> x6, Pallas kernels: 4.31 us -> 5.99 us  [the longest x3 2.64 us: wide_gather(): simple(fold_kernel, [shape(pairs, 4, LANES), shape(NARROW, blocks.shape[1...]
  transfers between devices with their start and end apart: 8 -> 8, of which waited for: 6 -> 6; matrix products, arithmetic and copies ran while one was open for 1% -> 1% of each run, Pallas kernels for 19% -> 20%
where the time goes in v4:
time: 153 us; the launch traced here: 152 us
  starting transfers between devices  65.9 us (43%)
  Pallas kernels  40 us (26%)
  blocking collectives  28.1 us (18%)
  waiting for transfers between devices  16.4 us (11%)
    all_to_all x5, starting transfers between devices, exchange(): lax.all_to_all(copies, ('wide', 'narrow'), 0, 0, tiled=True, axis_index_g...  55 us
    all_to_all x3, blocking collectives, exchange(): lax.all_to_all(copies, ('wide', 'narrow'), 0, 0, tiled=True, axis_index_g...  28.1 us
    pallas_call x3, Pallas kernels, near_apply(): pl.pallas_call(functools.partial(near_kernel, evaluate), out_shape=out_sh...  18.2 us
    all_to_all x5, waiting for transfers between devices, exchange(): lax.all_to_all(copies, ('wide', 'narrow'), 0, 0, tiled=True, axis_index_g...  14 us
    ppermute x3, starting transfers between devices, neighbours(): return lax.ppermute(fields, 'wide', across)  10.9 us
    pallas_call x3, Pallas kernels, own_apply(): pl.pallas_call(functools.partial(own_kernel, evaluate), out_shape=out_sha...  10.4 us
  transfers between devices with their start and end apart: 8, of which 6 were waited for; matrix products, arithmetic and copies ran while one was open for 1% of the time, Pallas kernels for 20%

profile of v4, /device:TPU:1, one launch (start us, length us, event | category | flops | bytes accessed | tf_op | source)
XLA Modules:
  0.0 152.2 jit_solution(13018185252362488889)
XLA Ops:
  0.6 0.0 copy-start
  0.6 2.1 %shard_map.176 = (f32[8,52,128]{2,1,0:T(8,128)}, f32[8,512]{1,0:T(8,128)S(1)}, bf16[3,64,512]{2,1,0:T(8,128)(2,1)S(1)}, bf16[3,64,64]{2,1,0:T(8,128)(2,1)S(1)}) custom-call(f32[3,512]{1,0:T(4,128)} %warm_in.1, f32[3,3,512]{2,1,0:T(4,128)} %refs_7_.1, bf16[3,64,512]{2,1,0:T(8,128)(2,1)} %bitcast.10, bf16[3,64,64]{2,1,0:T(8,128)(2,1)} %transfer_in.1), custom_call_target="tpu_custom_call" | custom-call | flops 1000000 | bytes 1000000 | tf_op jit(solution)/shard_map/pallas_call | solution.py:670
  2.8 10.2 %all-to-all-start = ((f32[8,52,128]{2,1,0:T(8,128)}), f32[8,52,128]{2,1,0:T(8,128)S(1)}, u32[]{:S(2)}, u32[]{:S(2)}) async-start(f32[8,52,128]{2,1,0:T(8,128)} %get-tuple-element.38), calls=%async_computation | async-start | bytes 458752 | tf_op jit(solution)/shard_map/all_to_all | solution.py:611
  13.0 0.0 copy-done
  13.0 0.4 constant_dynamic-slice_fusion
  13.4 0.5 copy.20.top_transfer.refs_6_
  13.9 6.0 %shard_map.177 = (f32[3,512,512]{2,1,0:T(8,128)}, f32[8,512]{1,0:T(8,128)S(1)}) custom-call(f32[8,512]{1,0:T(8,128)S(1)} %get-tuple-element.39.refs_0_.refs_4_.warm, f32[3,3,512]{2,1,0:T(4,128)} %refs_7_.1), custom_call_target="tpu_custom_call" | custom-call | flops 100000000 | bytes 4000000 | tf_op jit(solution)/shard_map/pallas_call | solution.py:458
  19.9 0.0 all-to-all-done.blocks.refs_2_
  19.9 0.9 shard_map.178
  20.8 11.9 %all-to-all-start.1 = ((f32[64,4,128]{2,1,0:T(4,128)}), f32[64,4,128]{2,1,0:T(4,128)S(1)}, u32[]{:S(2)}, u32[]{:S(2)}) async-start(f32[64,4,128]{2,1,0:T(4,128)} %get-tuple-element.41), calls=%async_computation.1 | async-start | bytes 262144 | tf_op jit(solution)/shard_map/all_to_all | solution.py:611
  32.7 3.4 %collective-permute-start = (f32[4,48,128]{2,1,0:T(8,128)S(1)}, f32[4,48,128]{2,1,0:T(8,128)S(1)}, u32[]{:S(2)}, u32[]{:S(2)}) collective-permute-start(f32[4,48,128]{2,1,0:T(8,128)S(1)} %get-tuple-element.42), channel_id=1, source_target_pairs={{4,8},{8,4},{12,16},{16,12},{20,24},{24,20},{28,32},{32,28},{36,40... | collective-permute-start | bytes 294920 | tf_op jit(solution)/shard_map/ppermute | solution.py:621
  36.1 1.7 %shard_map.179 = (f32[8,64]{1,0:T(8,128)S(1)}, bf16[16,256]{1,0:T(8,128)(2,1)S(1)}, bf16[4,64,64]{2,1,0:T(8,128)(2,1)S(1)}, f32[3,512]{1,0:T(4,128)S(1)}, bf16[3...) custom-call(f32[8,52,128]{2,1,0:T(8,128)S(1)} %all-to-all-done.blocks.refs_2_, ...), custom_call_target="tpu_custom_call" | custom-call | flops 10000000 | bytes 2000000 | tf_op jit(solution)/shard_map/pallas_call | solution.py:348
  37.8 2.3 %collective-permute-done.refs_3_ = f32[4,48,128]{2,1,0:T(8,128)S(1)} collective-permute-done((f32[4,48,128]{2,1,0:T(8,128)S(1)}, f32[4,48,128]{2,1,0:T(8,128)S(1)}, u32[]{:S(2)}, u32[]{:S(2)}) %collective-permute-start) | collective-permute-done | bytes 98336 | tf_op jit(solution)/shard_map/ppermute | solution.py:621
  40.0 10.1 %shard_map.180 = (f32[9,512,512]{2,1,0:T(8,128)}, f32[8,512]{1,0:T(8,128)S(1)}) custom-call(s32[3,4]{1,0:T(4,128)} %refs_0_.5, s32[3]{0:T(128)} %refs_1_.7, f32[8,52,128]{2,1,0:T(8,128)S(1)} %all-to-all-done.blocks.refs_2_, f32[4,48,128]{2,1,0:T(8,128)S(1)} %collective-permute-done.refs_3_, f32[8,512]{1,0:T(8,128)S(1)} %get-tuple-element.39.refs_0_.refs_4_.warm, ...), custom_call_target="tpu_custom_call" | custom-call | flops 300000000 | bytes 20000000 | tf_op jit(solution)/shard_map/pallas_call | solution.py:483
  50.2 0.0 all-to-all-done.1
  50.2 1.2 shard_map.181
  51.4 9.4 %all_to_all.40.blocks.refs_2_ = f32[8,16,128]{2,1,0:T(8,128)S(1)} all-to-all(f32[8,16,128]{2,1,0:T(8,128)S(1)} %get-tuple-element.52), channel_id=1, replica_groups={{0,1,2,3,4,5,6,7},{8,9,10,11,12,13,14,15},{16,17,18,19,20,21,22,23},{24..., dimensions={0} | all-to-all | bytes 131072 | tf_op jit(solution)/shard_map/all_to_all | solution.py:611
  60.7 0.9 shard_map.182
  61.6 12.7 %all-to-all-start.3 = ((f32[64,4,128]{2,1,0:T(4,128)}), f32[64,4,128]{2,1,0:T(4,128)S(1)}, u32[]{:S(2)}, u32[]{:S(2)}) async-start(f32[64,4,128]{2,1,0:T(4,128)} %get-tuple-element.53), calls=%async_computation.3 | async-start | bytes 262144 | tf_op jit(solution)/shard_map/all_to_all | solution.py:611
  74.3 3.8 %collective-permute-start.1 = (f32[4,12,128]{2,1,0:T(8,128)S(1)}, f32[4,12,128]{2,1,0:T(8,128)S(1)}, u32[]{:S(2)}, u32[]{:S(2)}) collective-permute-start(f32[4,12,128]{2,1,0:T(8,128)S(1)} %get-tuple-element.54), channel_id=1, source_target_pairs={{4,8},{8,4},{12,16},{16,12},{20,24},{24,20},{28,32},{32,28},{36,40... | collective-permute-start | bytes 73736 | tf_op jit(solution)/shard_map/ppermute | solution.py:621
  78.1 2.2 %shard_map.183 = (f32[8,512]{1,0:T(8,128)S(1)}, f32[8,64]{1,0:T(8,128)S(1)}) custom-call(f32[8,512]{1,0:T(8,128)S(1)} %get-tuple-element.55.refs_0_.refs_4_.refs_9_.residual, f32[3,512,512]{2,1,0:T(8,128)} %get-tuple-element.56.refs_1_, f32[8,16,128]{2,1,0:T(8,128)S(1)} %all_to_all.40.blocks.refs_2_, bf16[3,8,64,64]{3,2,1,0:T(8,128)(2,1)S(1)} %get-tuple-element.57.refs_3_, ...), custom_call_target="tpu_custom_call" | custom-call | flops 100000000 | bytes 4000000 | tf_op jit(solution)/shard_map/pallas_call | solution.py:458
  80.3 0.1 collective-permute-done.1.refs_3_
  80.4 4.1 %shard_map.184.refs_1_ = f32[8,512]{1,0:T(8,128)S(1)} custom-call(s32[3,4]{1,0:T(4,128)} %refs_0_.5, s32[3]{0:T(128)} %refs_1_.7, f32[8,16,128]{2,1,0:T(8,128)S(1)} %all_to_all.40.blocks.refs_2_, f32[4,12,128]{2,1,0:T(8,128)S(1)} %collective-permute-done.1.refs_3_, f32[8,512]{1,0:T(8,128)S(1)} %get-tuple-element.55.refs_0_.refs_4_.refs_9_.residual, ...), custom_call_target="tpu_custom_call" | custom-call | flops 300000000 | bytes 20000000 | tf_op jit(solution)/shard_map/pallas_call | solution.py:483
  84.4 1.5 all-to-all-done.3
  85.9 1.2 shard_map.185
  87.1 9.4 %all_to_all.41.blocks.refs_2_ = f32[8,16,128]{2,1,0:T(8,128)S(1)} all-to-all(f32[8,16,128]{2,1,0:T(8,128)S(1)} %get-tuple-element.61), channel_id=1, replica_groups={{0,1,2,3,4,5,6,7},{8,9,10,11,12,13,14,15},{16,17,18,19,20,21,22,23},{24..., dimensions={0} | all-to-all | bytes 131072 | tf_op jit(solution)/shard_map/all_to_all | solution.py:611
  96.5 0.9 shard_map.186
  97.4 10.1 %all-to-all-start.5 = ((f32[64,4,128]{2,1,0:T(4,128)}), f32[64,4,128]{2,1,0:T(4,128)S(1)}, u32[]{:S(2)}, u32[]{:S(2)}) async-start(f32[64,4,128]{2,1,0:T(4,128)} %get-tuple-element.62), calls=%async_computation.5 | async-start | bytes 262144 | tf_op jit(solution)/shard_map/all_to_all | solution.py:611
  107.5 3.8 %collective-permute-start.2 = (f32[4,12,128]{2,1,0:T(8,128)S(1)}, f32[4,12,128]{2,1,0:T(8,128)S(1)}, u32[]{:S(2)}, u32[]{:S(2)}) collective-permute-start(f32[4,12,128]{2,1,0:T(8,128)S(1)} %get-tuple-element.63), channel_id=1, source_target_pairs={{4,8},{8,4},{12,16},{16,12},{20,24},{24,20},{28,32},{32,28},{36,40... | collective-permute-start | bytes 73736 | tf_op jit(solution)/shard_map/ppermute | solution.py:621
  111.3 2.2 %shard_map.187 = (f32[8,512]{1,0:T(8,128)S(1)}, f32[8,64]{1,0:T(8,128)S(1)}) custom-call(f32[8,512]{1,0:T(8,128)S(1)} %get-tuple-element.64.refs_0_.refs_4_, f32[3,512,512]{2,1,0:T(8,128)} %get-tuple-element.56.refs_1_, f32[8,16,128]{2,1,0:T(8,128)S(1)} %all_to_all.41.blocks.refs_2_, bf16[3,8,64,64]{3,2,1,0:T(8,128)(2,1)S(1)} %get-tuple-element.57.refs_3_, ...), custom_call_target="tpu_custom_call" | custom-call | flops 100000000 | bytes 4000000 | tf_op jit(solution)/shard_map/pallas_call | solution.py:458
  113.5 0.1 collective-permute-done.2.refs_3_
  113.5 4.1 %shard_map.188.refs_1_ = f32[8,512]{1,0:T(8,128)S(1)} custom-call(s32[3,4]{1,0:T(4,128)} %refs_0_.5, s32[3]{0:T(128)} %refs_1_.7, f32[8,16,128]{2,1,0:T(8,128)S(1)} %all_to_all.41.blocks.refs_2_, f32[4,12,128]{2,1,0:T(8,128)S(1)} %collective-permute-done.2.refs_3_, f32[8,512]{1,0:T(8,128)S(1)} %get-tuple-element.64.refs_0_.refs_4_, ...), custom_call_target="tpu_custom_call" | custom-call | flops 300000000 | bytes 20000000 | tf_op jit(solution)/shard_map/pallas_call | solution.py:483
  117.6 1.5 all-to-all-done.5
  119.1 1.0 shard_map.189
  120.1 9.4 %all_to_all.42.blocks = f32[8,8,128]{2,1,0:T(8,128)S(1)} all-to-all(f32[8,8,128]{2,1,0:T(8,128)S(1)} %get-tuple-element.69), channel_id=1, replica_groups={{0,1,2,3,4,5,6,7},{8,9,10,11,12,13,14,15},{16,17,18,19,20,21,22,23},{24..., dimensions={0} | all-to-all | bytes 65536 | tf_op jit(solution)/shard_map/all_to_all | solution.py:611
  129.5 0.6 shard_map.190
  130.1 10.1 %all-to-all-start.7 = ((f32[64,2,128]{2,1,0:T(2,128)}), f32[64,2,128]{2,1,0:T(2,128)S(1)}, u32[]{:S(2)}, u32[]{:S(2)}) async-start(f32[64,2,128]{2,1,0:T(2,128)} %shard_map.190), calls=%async_computation.7 | async-start | bytes 131072 | tf_op jit(solution)/shard_map/all_to_all | solution.py:611
  140.2 11.1 %all-to-all-done.7.blocks = f32[64,2,128]{2,1,0:T(2,128)S(1)} async-done(((f32[64,2,128]{2,1,0:T(2,128)}), f32[64,2,128]{2,1,0:T(2,128)S(1)}, u32[]{:S(2)}, u32[]{:S(2)}) %all-to-all-start.7) | async-done | bytes 65568 | tf_op jit(solution)/shard_map/all_to_all | solution.py:611
  151.3 0.9 shard_map.192
  (1 shorter events, 0.0 us)
Async XLA Ops:
  0.6 12.4 %copy-start = (bf16[128,64,64]{0,2,1:T(8,128)(2,1)S(1)}, bf16[128,64,64]{0,2,1:T(8,128)(2,1)}, u32[]{:S(2)}) copy-start(bf16[128,64,64]{0,2,1:T(8,128)(2,1)} %param.25) | copy-start | bytes 3145732
  2.8 17.1 %all-to-all-start = ((f32[8,52,128]{2,1,0:T(8,128)}), f32[8,52,128]{2,1,0:T(8,128)S(1)}, u32[]{:S(2)}, u32[]{:S(2)}) async-start(f32[8,52,128]{2,1,0:T(8,128)} %get-tuple-element.38), calls=%async_computation | async-start | bytes 458752 | tf_op jit(solution)/shard_map/all_to_all | solution.py:611
  20.8 29.4 %all-to-all-start.1 = ((f32[64,4,128]{2,1,0:T(4,128)}), f32[64,4,128]{2,1,0:T(4,128)S(1)}, u32[]{:S(2)}, u32[]{:S(2)}) async-start(f32[64,4,128]{2,1,0:T(4,128)} %get-tuple-element.41), calls=%async_computation.1 | async-start | bytes 262144 | tf_op jit(solution)/shard_map/all_to_all | solution.py:611
  32.7 7.3 %collective-permute-start = (f32[4,48,128]{2,1,0:T(8,128)S(1)}, f32[4,48,128]{2,1,0:T(8,128)S(1)}, u32[]{:S(2)}, u32[]{:S(2)}) collective-permute-start(f32[4,48,128]{2,1,0:T(8,128)S(1)} %get-tuple-element.42), channel_id=1, source_target_pairs={{4,8},{8,4},{12,16},{16,12},{20,24},{24,20},{28,32},{32,28},{36,40... | collective-permute-start | bytes 294920 | tf_op jit(solution)/shard_map/ppermute | solution.py:621
  61.6 24.3 %all-to-all-start.3 = ((f32[64,4,128]{2,1,0:T(4,128)}), f32[64,4,128]{2,1,0:T(4,128)S(1)}, u32[]{:S(2)}, u32[]{:S(2)}) async-start(f32[64,4,128]{2,1,0:T(4,128)} %get-tuple-element.53), calls=%async_computation.3 | async-start | bytes 262144 | tf_op jit(solution)/shard_map/all_to_all | solution.py:611
  74.3 6.0 %collective-permute-start.1 = (f32[4,12,128]{2,1,0:T(8,128)S(1)}, f32[4,12,128]{2,1,0:T(8,128)S(1)}, u32[]{:S(2)}, u32[]{:S(2)}) collective-permute-start(f32[4,12,128]{2,1,0:T(8,128)S(1)} %get-tuple-element.54), channel_id=1, source_target_pairs={{4,8},{8,4},{12,16},{16,12},{20,24},{24,20},{28,32},{32,28},{36,40... | collective-permute-start | bytes 73736 | tf_op jit(solution)/shard_map/ppermute | solution.py:621
  97.4 21.7 %all-to-all-start.5 = ((f32[64,4,128]{2,1,0:T(4,128)}), f32[64,4,128]{2,1,0:T(4,128)S(1)}, u32[]{:S(2)}, u32[]{:S(2)}) async-start(f32[64,4,128]{2,1,0:T(4,128)} %get-tuple-element.62), calls=%async_computation.5 | async-start | bytes 262144 | tf_op jit(solution)/shard_map/all_to_all | solution.py:611
  107.5 6.0 %collective-permute-start.2 = (f32[4,12,128]{2,1,0:T(8,128)S(1)}, f32[4,12,128]{2,1,0:T(8,128)S(1)}, u32[]{:S(2)}, u32[]{:S(2)}) collective-permute-start(f32[4,12,128]{2,1,0:T(8,128)S(1)} %get-tuple-element.63), channel_id=1, source_target_pairs={{4,8},{8,4},{12,16},{16,12},{20,24},{24,20},{28,32},{32,28},{36,40... | collective-permute-start | bytes 73736 | tf_op jit(solution)/shard_map/ppermute | solution.py:621
  130.1 21.2 %all-to-all-start.7 = ((f32[64,2,128]{2,1,0:T(2,128)}), f32[64,2,128]{2,1,0:T(2,128)S(1)}, u32[]{:S(2)}, u32[]{:S(2)}) async-start(f32[64,2,128]{2,1,0:T(2,128)} %shard_map.190), calls=%async_computation.7 | async-start | bytes 131072 | tf_op jit(solution)/shard_map/all_to_all | solution.py:611

commit v5 on v4

--- a/solution.py
+++ b/solution.py
@@ -60,6 +60,32 @@
     return out[:count] + (out[count : 2 * count] + out[2 * count :])
 
 
+def three_parts(vectors):
+    high = vectors.astype(jnp.bfloat16).astype(f32)
+    rest = vectors - high
+    middle = rest.astype(jnp.bfloat16).astype(f32)
+    return high, middle, rest - middle
+
+
+def with_rows(vectors, third, fourth):
+    row = rows_of(vectors)
+    return jnp.where(row == 3, third, jnp.where(row == 4, fourth, vectors))
+
+
+def target_factor(points):
+    norm = three_parts(jnp.sum(points * points, axis=0, keepdims=True))
+    high, middle, low = three_parts(points)
+    first = [with_rows(one, 1.0, part) for one, part in zip((high, high, middle), norm)]
+    return jnp.concatenate(first + [middle, high, low], axis=0)
+
+
+def source_factor(points):
+    norm = three_parts(jnp.sum(points * points, axis=0, keepdims=True))
+    high, middle, low = three_parts(-2.0 * points)
+    first = [with_rows(one, part, 1.0) for one, part in zip((high, middle, high), norm)]
+    return jnp.concatenate(first + [middle, low, high], axis=0)
+
+
 def row_by_leaf(terms):
     out = jnp.zeros_like(terms[0])
     for leaf, term in enumerate(terms):
@@ -182,13 +208,17 @@
             tile_copy(False, slots, kept, tiles, sems, leaf, quarter).start()
 
 
-def tile_products(evaluate, slots, fill, near, columns, spread, totals, kept, tiles, sems):
+def tile_products(
+    evaluate, slots, fill, near, columns, spread, totals, kept, tiles, sems, factors=None
+):
+    rows_at_once = CHUNK if factors is None else QUARTER
+
     def leaf_step(leaf, _):
         for slot in range(slots):
             field, point = fill(leaf, slot)
             for piece in range(PIECES):
                 spread[slot, piece] = jnp.broadcast_to(field(piece), (8, LANES))
-            if evaluate:
+            if evaluate and factors is None:
                 for at in range(FIELD):
                     spread[slot, PIECES + at] = jnp.broadcast_to(point(at), (8, LANES))
 
@@ -197,21 +227,31 @@
                 tile_copy(False, slots, kept, tiles, sems, leaf, quarter).wait()
 
             def step(chunk, _):
-                start = pl.multiple_of(quarter * QUARTER + chunk * CHUNK, CHUNK)
-                acc = jnp.zeros((CHUNK // 8, 8, LANES), f32)
+                start = pl.multiple_of(quarter * QUARTER + chunk * rows_at_once, rows_at_once)
+                acc = jnp.zeros((rows_at_once // 8, 8, LANES), f32)
                 if evaluate:
-                    column = columns[leaf, pl.ds(start, CHUNK), :]
+                    column = columns[leaf, pl.ds(start, rows_at_once), :]
+                if evaluate and factors is None:
                     target = [
-                        jnp.broadcast_to(column[:, axis : axis + 1], (CHUNK, LANES)).reshape(
-                            CHUNK // 8, 8, LANES
+                        jnp.broadcast_to(column[:, axis : axis + 1], (rows_at_once, LANES)).reshape(
+                            rows_at_once // 8, 8, LANES
                         )
                         for axis in range(3)
                     ]
                 for slot in range(slots):
+                    if factors is not None:
+                        distances = jnp.dot(column, factors[slot], preferred_element_type=f32)
                     for piece in range(PIECES):
                         cut = slice(piece * LANES, (piece + 1) * LANES)
-                        where = (leaf * slots + slot, pl.ds(start, CHUNK), cut)
-                        if evaluate:
+                        where = (leaf * slots + slot, pl.ds(start, rows_at_once), cut)
+                        if factors is not None:
+                            squared = distances[:, cut].reshape(rows_at_once // 8, 8, LANES)
+                            squared = jnp.maximum(squared, 1e-30)
+                            distance = squared * lax.rsqrt(squared)
+                            decay = jnp.exp2(distance * -log2_e)
+                            tile = (distance * amplitude + amplitude) * decay
+                            kept[where] = tile.reshape(rows_at_once, LANES)
+                        elif evaluate:
                             squared = None
                             for axis in range(3):
                                 source = spread[slot, PIECES + axis * PIECES + piece]
@@ -222,14 +262,14 @@
                             distance = squared * lax.rsqrt(squared)
                             decay = jnp.exp2(distance * (-rate * log2_e))
                             tile = (distance * (amplitude * rate) + amplitude) * decay
-                            kept[where] = tile.reshape(CHUNK, LANES)
+                            kept[where] = tile.reshape(rows_at_once, LANES)
                         else:
-                            tile = kept[where].reshape(CHUNK // 8, 8, LANES)
+                            tile = kept[where].reshape(rows_at_once // 8, 8, LANES)
                         acc = acc + tile * spread[slot, piece][None]
-                totals[pl.ds(start, CHUNK), :] = acc.reshape(CHUNK, LANES)
+                totals[pl.ds(start, rows_at_once), :] = acc.reshape(rows_at_once, LANES)
                 return 0
 
-            lax.fori_loop(0, QUARTER // CHUNK, step, 0)
+            lax.fori_loop(0, QUARTER // rows_at_once, step, 0)
             if evaluate:
                 tile_copy(True, slots, kept, tiles, sems, leaf, quarter).start()
             return 0
@@ -376,8 +416,8 @@
 def near_kernel(evaluate, *refs):
     if evaluate:
         (near_list_in, near_count_in, blocks, extra, values, own_near, noise, coords_in, tiles,
-         base, near_list, near_count, sems, window, sources, coords, columns, scratch, near,
-         spread, totals, kept, tile_sems) = refs
+         base, near_list, near_count, sems, window, sources, coords, columns, factors, centres,
+         scratch, near, spread, totals, kept, tile_sems) = refs
     else:
         (near_list_in, near_count_in, blocks, extra, values, own_near, noise, tiles, base,
          near_list, near_count, sems, window, scratch, near, spread, totals, kept,
@@ -403,7 +443,18 @@
         copy.wait()
     if evaluate:
         for leaf in range(LEAVES):
-            columns[leaf] = jnp.transpose(padded(coords.at[leaf], scratch))
+            points = padded(coords.at[leaf], scratch)
+            centre = jnp.broadcast_to(points[:, :1], (8, POINTS))
+            centres[leaf] = centre
+            factor = target_factor((points - centre) * rate)
+            columns[leaf] = jnp.transpose(factor).astype(jnp.bfloat16)
+
+    def source(leaf, points):
+        lines = jnp.zeros((8, POINTS), f32)
+        for axis in range(3):
+            line = [points[axis * PIECES + i : axis * PIECES + i + 1] for i in range(PIECES)]
+            lines = jnp.where(rows_of(lines) == axis, jnp.concatenate(line, axis=1), lines)
+        return source_factor((lines - centres[leaf]) * rate).astype(jnp.bfloat16)
 
     def fill(leaf, slot):
         listed = near_list[leaf, slot + 1]
@@ -413,12 +464,13 @@
         turn = jnp.where((turn >= 0) & (turn < 2), turn, 2)
         place = jnp.where(used, turn * GROUP + listed - of_group * GROUP, 0)
         field = window[place] * jnp.where(used, 1.0, 0.0).astype(f32)
-        points = sources[place] if evaluate else None
-        return lambda piece: field[piece : piece + 1], lambda at: points[at : at + 1]
+        if evaluate:
+            factors[slot] = source(leaf, sources[place])
+        return lambda piece: field[piece : piece + 1], None
 
     tile_products(
         evaluate, slots, fill, near, columns if evaluate else None, spread, totals, kept, tiles,
-        tile_sems,
+        tile_sems, factors if evaluate else None,
     )
     base[...] = local_part + near[...]
     if evaluate:
@@ -478,7 +530,13 @@
     if evaluate:
         out_shape = [pltpu.HBM((slots * LEAVES, POINTS, POINTS), f32)] + out_shape
         out_specs = [HBM] + out_specs
-        scratch += [pltpu.VMEM((WINDOW, FIELD, LANES), f32)] + column_scratch()
+        scratch += [
+            pltpu.VMEM((WINDOW, FIELD, LANES), f32),
+            pltpu.VMEM((LEAVES, 3, POINTS), f32),
+            pltpu.VMEM((LEAVES, POINTS, 48), jnp.bfloat16),
+            pltpu.VMEM((slots, 48, POINTS), jnp.bfloat16),
+            pltpu.VMEM((LEAVES, 8, POINTS), f32),
+        ]
     scratch += [pltpu.VMEM((8, POINTS), f32)] * 2 + loop_scratch(slots)
     return pl.pallas_call(
         functools.partial(near_kernel, evaluate),

time: 153 us -> 150 us (0.980)
  Pallas kernels: 40 us -> 37.6 us
    pallas_call x3, Pallas kernels: 18.2 us -> 15.8 us  [near_apply(): pl.pallas_call(functools.partial(near_kernel, evaluate), out_shape=out_sh...]
  transfers between devices with their start and end apart: 8 -> 8, of which waited for: 6 -> 6; matrix products, arithmetic and copies ran while one was open for 1% -> 1% of each run, Pallas kernels for 20% -> 19%
where the time goes in v5:
time: 150 us
  starting transfers between devices  65.9 us (44%)
  Pallas kernels  37.6 us (25%)
  blocking collectives  28.1 us (19%)
  waiting for transfers between devices  16.4 us (11%)
    all_to_all x5, starting transfers between devices, exchange(): lax.all_to_all(copies, ('wide', 'narrow'), 0, 0, tiled=True, axis_index_g...  55 us
    all_to_all x3, blocking collectives, exchange(): lax.all_to_all(copies, ('wide', 'narrow'), 0, 0, tiled=True, axis_index_g...  28.1 us
    pallas_call x3, Pallas kernels, near_apply(): pl.pallas_call(functools.partial(near_kernel, evaluate), out_shape=out_sh...  15.8 us
    all_to_all x5, waiting for transfers between devices, exchange(): lax.all_to_all(copies, ('wide', 'narrow'), 0, 0, tiled=True, axis_index_g...  14 us
    ppermute x3, starting transfers between devices, neighbours(): return lax.ppermute(fields, 'wide', across)  10.9 us
    pallas_call x3, Pallas kernels, own_apply(): pl.pallas_call(functools.partial(own_kernel, evaluate), out_shape=out_sha...  10.4 us
  transfers between devices with their start and end apart: 8, of which 6 were waited for; matrix products, arithmetic and copies ran while one was open for 1% of the time, Pallas kernels for 19%

profile of v5, /device:TPU:1, one launch (start us, length us, event | category | flops | bytes accessed | tf_op | source)
XLA Modules:
  0.0 149.7 jit_solution(11914807931500254569)
XLA Ops:
  0.6 0.0 copy-start
  0.6 2.1 %shard_map.176 = (f32[8,52,128]{2,1,0:T(8,128)}, f32[8,512]{1,0:T(8,128)S(1)}, bf16[3,64,512]{2,1,0:T(8,128)(2,1)S(1)}, bf16[3,64,64]{2,1,0:T(8,128)(2,1)S(1)}) custom-call(f32[3,512]{1,0:T(4,128)} %warm_in.1, f32[3,3,512]{2,1,0:T(4,128)} %refs_7_.1, bf16[3,64,512]{2,1,0:T(8,128)(2,1)} %bitcast.10, bf16[3,64,64]{2,1,0:T(8,128)(2,1)} %transfer_in.1), custom_call_target="tpu_custom_call" | custom-call | flops 1000000 | bytes 1000000 | tf_op jit(solution)/shard_map/pallas_call | solution.py:728
  2.8 10.2 %all-to-all-start = ((f32[8,52,128]{2,1,0:T(8,128)}), f32[8,52,128]{2,1,0:T(8,128)S(1)}, u32[]{:S(2)}, u32[]{:S(2)}) async-start(f32[8,52,128]{2,1,0:T(8,128)} %get-tuple-element.38), calls=%async_computation | async-start | bytes 458752 | tf_op jit(solution)/shard_map/all_to_all | solution.py:669
  13.0 0.0 copy-done
  13.0 0.4 constant_dynamic-slice_fusion
  13.4 0.5 copy.20.top_transfer.refs_6_
  13.9 6.0 %shard_map.177 = (f32[3,512,512]{2,1,0:T(8,128)}, f32[8,512]{1,0:T(8,128)S(1)}) custom-call(f32[8,512]{1,0:T(8,128)S(1)} %get-tuple-element.39.refs_0_.refs_4_.warm, f32[3,3,512]{2,1,0:T(4,128)} %refs_7_.1), custom_call_target="tpu_custom_call" | custom-call | flops 100000000 | bytes 4000000 | tf_op jit(solution)/shard_map/pallas_call | solution.py:510
  19.9 0.0 all-to-all-done.blocks.refs_2_
  19.9 0.9 shard_map.178
  20.8 11.9 %all-to-all-start.1 = ((f32[64,4,128]{2,1,0:T(4,128)}), f32[64,4,128]{2,1,0:T(4,128)S(1)}, u32[]{:S(2)}, u32[]{:S(2)}) async-start(f32[64,4,128]{2,1,0:T(4,128)} %get-tuple-element.41), calls=%async_computation.1 | async-start | bytes 262144 | tf_op jit(solution)/shard_map/all_to_all | solution.py:669
  32.7 3.4 %collective-permute-start = (f32[4,48,128]{2,1,0:T(8,128)S(1)}, f32[4,48,128]{2,1,0:T(8,128)S(1)}, u32[]{:S(2)}, u32[]{:S(2)}) collective-permute-start(f32[4,48,128]{2,1,0:T(8,128)S(1)} %get-tuple-element.42), channel_id=1, source_target_pairs={{4,8},{8,4},{12,16},{16,12},{20,24},{24,20},{28,32},{32,28},{36,40... | collective-permute-start | bytes 294920 | tf_op jit(solution)/shard_map/ppermute | solution.py:679
  36.1 1.7 %shard_map.179 = (f32[8,64]{1,0:T(8,128)S(1)}, bf16[16,256]{1,0:T(8,128)(2,1)S(1)}, bf16[4,64,64]{2,1,0:T(8,128)(2,1)S(1)}, f32[3,512]{1,0:T(4,128)S(1)}, bf16[3...) custom-call(f32[8,52,128]{2,1,0:T(8,128)S(1)} %all-to-all-done.blocks.refs_2_, ...), custom_call_target="tpu_custom_call" | custom-call | flops 10000000 | bytes 2000000 | tf_op jit(solution)/shard_map/pallas_call | solution.py:388
  37.8 2.3 %collective-permute-done.refs_3_ = f32[4,48,128]{2,1,0:T(8,128)S(1)} collective-permute-done((f32[4,48,128]{2,1,0:T(8,128)S(1)}, f32[4,48,128]{2,1,0:T(8,128)S(1)}, u32[]{:S(2)}, u32[]{:S(2)}) %collective-permute-start) | collective-permute-done | bytes 98336 | tf_op jit(solution)/shard_map/ppermute | solution.py:679
  40.0 7.7 %shard_map.180 = (f32[9,512,512]{2,1,0:T(8,128)}, f32[8,512]{1,0:T(8,128)S(1)}) custom-call(s32[3,4]{1,0:T(4,128)} %refs_0_.5, s32[3]{0:T(128)} %refs_1_.7, f32[8,52,128]{2,1,0:T(8,128)S(1)} %all-to-all-done.blocks.refs_2_, f32[4,48,128]{2,1,0:T(8,128)S(1)} %collective-permute-done.refs_3_, f32[8,512]{1,0:T(8,128)S(1)} %get-tuple-element.39.refs_0_.refs_4_.warm, ...), custom_call_target="tpu_custom_call" | custom-call | flops 300000000 | bytes 20000000 | tf_op jit(solution)/shard_map/pallas_call | solution.py:541
  47.7 0.0 all-to-all-done.1
  47.7 1.2 shard_map.181
  48.9 9.4 %all_to_all.40.blocks.refs_2_ = f32[8,16,128]{2,1,0:T(8,128)S(1)} all-to-all(f32[8,16,128]{2,1,0:T(8,128)S(1)} %get-tuple-element.52), channel_id=1, replica_groups={{0,1,2,3,4,5,6,7},{8,9,10,11,12,13,14,15},{16,17,18,19,20,21,22,23},{24..., dimensions={0} | all-to-all | bytes 131072 | tf_op jit(solution)/shard_map/all_to_all | solution.py:669
  58.3 0.9 shard_map.182
  59.1 12.7 %all-to-all-start.3 = ((f32[64,4,128]{2,1,0:T(4,128)}), f32[64,4,128]{2,1,0:T(4,128)S(1)}, u32[]{:S(2)}, u32[]{:S(2)}) async-start(f32[64,4,128]{2,1,0:T(4,128)} %get-tuple-element.53), calls=%async_computation.3 | async-start | bytes 262144 | tf_op jit(solution)/shard_map/all_to_all | solution.py:669
  71.9 3.8 %collective-permute-start.1 = (f32[4,12,128]{2,1,0:T(8,128)S(1)}, f32[4,12,128]{2,1,0:T(8,128)S(1)}, u32[]{:S(2)}, u32[]{:S(2)}) collective-permute-start(f32[4,12,128]{2,1,0:T(8,128)S(1)} %get-tuple-element.54), channel_id=1, source_target_pairs={{4,8},{8,4},{12,16},{16,12},{20,24},{24,20},{28,32},{32,28},{36,40... | collective-permute-start | bytes 73736 | tf_op jit(solution)/shard_map/ppermute | solution.py:679
  75.6 2.2 %shard_map.183 = (f32[8,512]{1,0:T(8,128)S(1)}, f32[8,64]{1,0:T(8,128)S(1)}) custom-call(f32[8,512]{1,0:T(8,128)S(1)} %get-tuple-element.55.refs_0_.refs_4_.refs_9_.residual, f32[3,512,512]{2,1,0:T(8,128)} %get-tuple-element.56.refs_1_, f32[8,16,128]{2,1,0:T(8,128)S(1)} %all_to_all.40.blocks.refs_2_, bf16[3,8,64,64]{3,2,1,0:T(8,128)(2,1)S(1)} %get-tuple-element.57.refs_3_, ...), custom_call_target="tpu_custom_call" | custom-call | flops 100000000 | bytes 4000000 | tf_op jit(solution)/shard_map/pallas_call | solution.py:510
  77.8 0.1 collective-permute-done.1.refs_3_
  77.9 4.1 %shard_map.184.refs_1_ = f32[8,512]{1,0:T(8,128)S(1)} custom-call(s32[3,4]{1,0:T(4,128)} %refs_0_.5, s32[3]{0:T(128)} %refs_1_.7, f32[8,16,128]{2,1,0:T(8,128)S(1)} %all_to_all.40.blocks.refs_2_, f32[4,12,128]{2,1,0:T(8,128)S(1)} %collective-permute-done.1.refs_3_, f32[8,512]{1,0:T(8,128)S(1)} %get-tuple-element.55.refs_0_.refs_4_.refs_9_.residual, ...), custom_call_target="tpu_custom_call" | custom-call | flops 300000000 | bytes 20000000 | tf_op jit(solution)/shard_map/pallas_call | solution.py:541
  82.0 1.5 all-to-all-done.3
  83.4 1.2 shard_map.185
  84.6 9.4 %all_to_all.41.blocks.refs_2_ = f32[8,16,128]{2,1,0:T(8,128)S(1)} all-to-all(f32[8,16,128]{2,1,0:T(8,128)S(1)} %get-tuple-element.61), channel_id=1, replica_groups={{0,1,2,3,4,5,6,7},{8,9,10,11,12,13,14,15},{16,17,18,19,20,21,22,23},{24..., dimensions={0} | all-to-all | bytes 131072 | tf_op jit(solution)/shard_map/all_to_all | solution.py:669
  94.1 0.9 shard_map.186
  94.9 10.1 %all-to-all-start.5 = ((f32[64,4,128]{2,1,0:T(4,128)}), f32[64,4,128]{2,1,0:T(4,128)S(1)}, u32[]{:S(2)}, u32[]{:S(2)}) async-start(f32[64,4,128]{2,1,0:T(4,128)} %get-tuple-element.62), calls=%async_computation.5 | async-start | bytes 262144 | tf_op jit(solution)/shard_map/all_to_all | solution.py:669
  105.0 3.8 %collective-permute-start.2 = (f32[4,12,128]{2,1,0:T(8,128)S(1)}, f32[4,12,128]{2,1,0:T(8,128)S(1)}, u32[]{:S(2)}, u32[]{:S(2)}) collective-permute-start(f32[4,12,128]{2,1,0:T(8,128)S(1)} %get-tuple-element.63), channel_id=1, source_target_pairs={{4,8},{8,4},{12,16},{16,12},{20,24},{24,20},{28,32},{32,28},{36,40... | collective-permute-start | bytes 73736 | tf_op jit(solution)/shard_map/ppermute | solution.py:679
  108.8 2.2 %shard_map.187 = (f32[8,512]{1,0:T(8,128)S(1)}, f32[8,64]{1,0:T(8,128)S(1)}) custom-call(f32[8,512]{1,0:T(8,128)S(1)} %get-tuple-element.64.refs_0_.refs_4_, f32[3,512,512]{2,1,0:T(8,128)} %get-tuple-element.56.refs_1_, f32[8,16,128]{2,1,0:T(8,128)S(1)} %all_to_all.41.blocks.refs_2_, bf16[3,8,64,64]{3,2,1,0:T(8,128)(2,1)S(1)} %get-tuple-element.57.refs_3_, ...), custom_call_target="tpu_custom_call" | custom-call | flops 100000000 | bytes 4000000 | tf_op jit(solution)/shard_map/pallas_call | solution.py:510
  111.0 0.1 collective-permute-done.2.refs_3_
  111.1 4.1 %shard_map.188.refs_1_ = f32[8,512]{1,0:T(8,128)S(1)} custom-call(s32[3,4]{1,0:T(4,128)} %refs_0_.5, s32[3]{0:T(128)} %refs_1_.7, f32[8,16,128]{2,1,0:T(8,128)S(1)} %all_to_all.41.blocks.refs_2_, f32[4,12,128]{2,1,0:T(8,128)S(1)} %collective-permute-done.2.refs_3_, f32[8,512]{1,0:T(8,128)S(1)} %get-tuple-element.64.refs_0_.refs_4_, ...), custom_call_target="tpu_custom_call" | custom-call | flops 300000000 | bytes 20000000 | tf_op jit(solution)/shard_map/pallas_call | solution.py:541
  115.1 1.5 all-to-all-done.5
  116.6 1.0 shard_map.189
  117.6 9.4 %all_to_all.42.blocks = f32[8,8,128]{2,1,0:T(8,128)S(1)} all-to-all(f32[8,8,128]{2,1,0:T(8,128)S(1)} %get-tuple-element.69), channel_id=1, replica_groups={{0,1,2,3,4,5,6,7},{8,9,10,11,12,13,14,15},{16,17,18,19,20,21,22,23},{24..., dimensions={0} | all-to-all | bytes 65536 | tf_op jit(solution)/shard_map/all_to_all | solution.py:669
  127.0 0.6 shard_map.190
  127.6 10.1 %all-to-all-start.7 = ((f32[64,2,128]{2,1,0:T(2,128)}), f32[64,2,128]{2,1,0:T(2,128)S(1)}, u32[]{:S(2)}, u32[]{:S(2)}) async-start(f32[64,2,128]{2,1,0:T(2,128)} %shard_map.190), calls=%async_computation.7 | async-start | bytes 131072 | tf_op jit(solution)/shard_map/all_to_all | solution.py:669
  137.8 11.1 %all-to-all-done.7.blocks = f32[64,2,128]{2,1,0:T(2,128)S(1)} async-done(((f32[64,2,128]{2,1,0:T(2,128)}), f32[64,2,128]{2,1,0:T(2,128)S(1)}, u32[]{:S(2)}, u32[]{:S(2)}) %all-to-all-start.7) | async-done | bytes 65568 | tf_op jit(solution)/shard_map/all_to_all | solution.py:669
  148.8 0.9 shard_map.192
  (1 shorter events, 0.0 us)
Async XLA Ops:
  0.6 12.4 %copy-start = (bf16[128,64,64]{0,2,1:T(8,128)(2,1)S(1)}, bf16[128,64,64]{0,2,1:T(8,128)(2,1)}, u32[]{:S(2)}) copy-start(bf16[128,64,64]{0,2,1:T(8,128)(2,1)} %param.25) | copy-start | bytes 3145732
  2.8 17.1 %all-to-all-start = ((f32[8,52,128]{2,1,0:T(8,128)}), f32[8,52,128]{2,1,0:T(8,128)S(1)}, u32[]{:S(2)}, u32[]{:S(2)}) async-start(f32[8,52,128]{2,1,0:T(8,128)} %get-tuple-element.38), calls=%async_computation | async-start | bytes 458752 | tf_op jit(solution)/shard_map/all_to_all | solution.py:669
  20.8 26.9 %all-to-all-start.1 = ((f32[64,4,128]{2,1,0:T(4,128)}), f32[64,4,128]{2,1,0:T(4,128)S(1)}, u32[]{:S(2)}, u32[]{:S(2)}) async-start(f32[64,4,128]{2,1,0:T(4,128)} %get-tuple-element.41), calls=%async_computation.1 | async-start | bytes 262144 | tf_op jit(solution)/shard_map/all_to_all | solution.py:669
  32.7 7.3 %collective-permute-start = (f32[4,48,128]{2,1,0:T(8,128)S(1)}, f32[4,48,128]{2,1,0:T(8,128)S(1)}, u32[]{:S(2)}, u32[]{:S(2)}) collective-permute-start(f32[4,48,128]{2,1,0:T(8,128)S(1)} %get-tuple-element.42), channel_id=1, source_target_pairs={{4,8},{8,4},{12,16},{16,12},{20,24},{24,20},{28,32},{32,28},{36,40... | collective-permute-start | bytes 294920 | tf_op jit(solution)/shard_map/ppermute | solution.py:679
  59.1 24.3 %all-to-all-start.3 = ((f32[64,4,128]{2,1,0:T(4,128)}), f32[64,4,128]{2,1,0:T(4,128)S(1)}, u32[]{:S(2)}, u32[]{:S(2)}) async-start(f32[64,4,128]{2,1,0:T(4,128)} %get-tuple-element.53), calls=%async_computation.3 | async-start | bytes 262144 | tf_op jit(solution)/shard_map/all_to_all | solution.py:669
  71.9 6.0 %collective-permute-start.1 = (f32[4,12,128]{2,1,0:T(8,128)S(1)}, f32[4,12,128]{2,1,0:T(8,128)S(1)}, u32[]{:S(2)}, u32[]{:S(2)}) collective-permute-start(f32[4,12,128]{2,1,0:T(8,128)S(1)} %get-tuple-element.54), channel_id=1, source_target_pairs={{4,8},{8,4},{12,16},{16,12},{20,24},{24,20},{28,32},{32,28},{36,40... | collective-permute-start | bytes 73736 | tf_op jit(solution)/shard_map/ppermute | solution.py:679
  94.9 21.7 %all-to-all-start.5 = ((f32[64,4,128]{2,1,0:T(4,128)}), f32[64,4,128]{2,1,0:T(4,128)S(1)}, u32[]{:S(2)}, u32[]{:S(2)}) async-start(f32[64,4,128]{2,1,0:T(4,128)} %get-tuple-element.62), calls=%async_computation.5 | async-start | bytes 262144 | tf_op jit(solution)/shard_map/all_to_all | solution.py:669
  105.0 6.0 %collective-permute-start.2 = (f32[4,12,128]{2,1,0:T(8,128)S(1)}, f32[4,12,128]{2,1,0:T(8,128)S(1)}, u32[]{:S(2)}, u32[]{:S(2)}) collective-permute-start(f32[4,12,128]{2,1,0:T(8,128)S(1)} %get-tuple-element.63), channel_id=1, source_target_pairs={{4,8},{8,4},{12,16},{16,12},{20,24},{24,20},{28,32},{32,28},{36,40... | collective-permute-start | bytes 73736 | tf_op jit(solution)/shard_map/ppermute | solution.py:679
  127.6 21.2 %all-to-all-start.7 = ((f32[64,2,128]{2,1,0:T(2,128)}), f32[64,2,128]{2,1,0:T(2,128)S(1)}, u32[]{:S(2)}, u32[]{:S(2)}) async-start(f32[64,2,128]{2,1,0:T(2,128)} %shard_map.190), calls=%async_computation.7 | async-start | bytes 131072 | tf_op jit(solution)/shard_map/all_to_all | solution.py:669

commit v6 on v5

--- a/solution.py
+++ b/solution.py
@@ -202,14 +202,15 @@
     return pltpu.make_async_copy(source.at[part], target.at[part], sems.at[leaf * PIECES + quarter])
 
 
-def begin_tiles(slots, kept, tiles, sems):
-    for leaf in range(LEAVES):
+def begin_tiles(slots, kept, tiles, sems, first=0):
+    for leaf in range(first, LEAVES):
         for quarter in range(PIECES):
             tile_copy(False, slots, kept, tiles, sems, leaf, quarter).start()
 
 
 def tile_products(
-    evaluate, slots, fill, near, columns, spread, totals, kept, tiles, sems, factors=None
+    evaluate, slots, fill, near, columns, spread, totals, kept, tiles, sems, factors=None,
+    leaves=(0, LEAVES), held=False,
 ):
     rows_at_once = CHUNK if factors is None else QUARTER
 
@@ -223,7 +224,7 @@
                     spread[slot, PIECES + at] = jnp.broadcast_to(point(at), (8, LANES))
 
         def quarter_step(quarter, _):
-            if not evaluate:
+            if not evaluate and not held:
                 tile_copy(False, slots, kept, tiles, sems, leaf, quarter).wait()
 
             def step(chunk, _):
@@ -285,8 +286,9 @@
         near[pl.ds(leaf, 1), :] = jnp.concatenate(pieces, axis=1)
         return 0
 
-    near[...] = jnp.zeros(near.shape, f32)
-    lax.fori_loop(0, LEAVES, leaf_step, 0)
+    if leaves[0] == 0:
+        near[...] = jnp.zeros(near.shape, f32)
+    lax.fori_loop(*leaves, leaf_step, 0)
 
 
 def end_tiles(slots, kept, tiles, sems):
@@ -328,13 +330,15 @@
         for leaf in range(LEAVES):
             columns[leaf] = jnp.transpose(padded(coords.at[leaf], scratch))
     else:
-        (values, tiles, blocks, coupling, far_list_in, far_count_in, own_near, leaf_far, far_list,
-         far_count, coefs, sem, *loop) = refs
+        (values, tiles, blocks, coupling, far_list_in, far_count_in, others, own_near, leaf_far,
+         early, far_list, far_count, coefs, sem, *loop) = refs
         coords = columns = None
     spread, totals, kept, sems = loop
     if not evaluate:
         copies = fetch([(far_list_in, far_list), (far_count_in, far_count)], sem)
         begin_tiles(1, kept, tiles, sems)
+        early_copy = pltpu.make_async_copy(others.at[pl.ds(0, NEAR - 1)], early, sem.at[2])
+        early_copy.start()
         for copy in copies:
             copy.wait()
         leaf_coupling(blocks, coupling, far_list, far_count, coefs, leaf_far)
@@ -353,6 +357,8 @@
     tile_products(evaluate, 1, fill, own_near, columns, spread, totals, kept, tiles, sems)
     if evaluate:
         end_tiles(1, kept, tiles, sems)
+    else:
+        early_copy.wait()
 
 
 def mid_kernel(
@@ -419,14 +425,14 @@
          base, near_list, near_count, sems, window, sources, coords, columns, factors, centres,
          scratch, near, spread, totals, kept, tile_sems) = refs
     else:
-        (near_list_in, near_count_in, blocks, extra, values, own_near, noise, tiles, base,
+        (near_list_in, near_count_in, blocks, extra, values, own_near, noise, early, tiles, base,
          near_list, near_count, sems, window, scratch, near, spread, totals, kept,
          tile_sems) = refs
     slots = NEAR - 1
     pairs = [(near_list_in, near_list), (near_count_in, near_count)]
     copies = fetch(pairs + ([(coords_in, coords)] if evaluate else []), sems)
     if not evaluate:
-        begin_tiles(slots, kept, tiles, tile_sems)
+        begin_tiles(slots, kept, tiles, tile_sems, 1)
     wide = lax.axis_index("wide")
     first_group = wide - lax.rem(wide, 2)
     for device in range(PAIR + NARROW):
@@ -468,10 +474,16 @@
             factors[slot] = source(leaf, sources[place])
         return lambda piece: field[piece : piece + 1], None
 
-    tile_products(
-        evaluate, slots, fill, near, columns if evaluate else None, spread, totals, kept, tiles,
-        tile_sems, factors if evaluate else None,
-    )
+    if evaluate:
+        tile_products(
+            True, slots, fill, near, columns, spread, totals, kept, tiles, tile_sems, factors
+        )
+    else:
+        rest = (tiles, tile_sems, None)
+        tile_products(
+            False, slots, fill, near, None, spread, totals, early, *rest, (0, 1), True
+        )
+        tile_products(False, slots, fill, near, None, spread, totals, kept, *rest, (1, LEAVES))
     base[...] = local_part + near[...]
     if evaluate:
         end_tiles(slots, kept, tiles, tile_sems)
@@ -499,13 +511,13 @@
             pltpu.VMEM((8, POINTS), f32), pltpu.SemaphoreType.DMA((1,))
         ]
     else:
-        out_shape.append(shape(8, RANK))
-        out_specs.append(VMEM)
+        out_shape += [shape(8, RANK), shape(NEAR - 1, POINTS, POINTS)]
+        out_specs += [VMEM] * 2
         scratch = [
             pltpu.SMEM((LEAVES, FAR), jnp.int32),
             pltpu.SMEM((LEAVES,), jnp.int32),
             pltpu.VMEM((16, LANES), f32),
-            pltpu.SemaphoreType.DMA((2,)),
+            pltpu.SemaphoreType.DMA((3,)),
         ]
     return pl.pallas_call(
         functools.partial(own_kernel, evaluate),
@@ -541,7 +553,7 @@
     return pl.pallas_call(
         functools.partial(near_kernel, evaluate),
         out_shape=out_shape,
-        in_specs=[HBM] * 2 + [VMEM] * 5 + [HBM],
+        in_specs=[HBM] * 2 + [VMEM] * len(near_data) + [HBM],
         out_specs=out_specs,
         scratch_shapes=scratch,
         cost_estimate=cost(3 * 10**8, 2 * 10**7),
@@ -718,10 +730,10 @@
     def gather(packed, values):
         blocks = exchange(packed, 1)
         extra, rows = wide_gather(blocks)
-        own_near, leaf_far = own_apply(
-            False, values, own_tiles, (blocks, coupling), (far_list, far_count)
+        own_near, leaf_far, early = own_apply(
+            False, values, own_tiles, (blocks, coupling), (far_list, far_count, tiles)
         )
-        near = (blocks, extra, values, own_near, noise)
+        near = (blocks, extra, values, own_near, noise, early)
         (base,) = near_apply(False, (near_list, near_count), near, tiles)
         return rows, base, leaf_far
 

time: 150 us -> 149 us (level)
  starting transfers between devices: 65.9 us -> 64.1 us
    all_to_all x5, starting transfers between devices: 55 us -> 53.2 us  [exchange(): lax.all_to_all(copies, ('wide', 'narrow'), 0, 0, tiled=True, axis_index_g...]
    pallas_call x3, Pallas kernels: 15.8 us -> 14 us  [near_apply(): pl.pallas_call(functools.partial(near_kernel, evaluate), out_shape=out_sh...]
    pallas_call x3, Pallas kernels: 10.4 us -> 12 us  [own_apply(): pl.pallas_call(functools.partial(own_kernel, evaluate), out_shape=out_sha...]
  transfers between devices with their start and end apart: 8 -> 8, of which waited for: 6 -> 4; matrix products, arithmetic and copies ran while one was open for 1% -> 1% of each run, Pallas kernels for 19% -> 19%
where the time goes in v6:
time: 149 us; the launch traced here: 148 us
  starting transfers between devices  64.1 us (43%)
  Pallas kernels  37.4 us (25%)
  blocking collectives  28.1 us (19%)
  waiting for transfers between devices  16.6 us (11%)
    all_to_all x5, starting transfers between devices, exchange(): lax.all_to_all(copies, ('wide', 'narrow'), 0, 0, tiled=True, axis_index_g...  53.2 us
    all_to_all x3, blocking collectives, exchange(): lax.all_to_all(copies, ('wide', 'narrow'), 0, 0, tiled=True, axis_index_g...  28.1 us
    all_to_all x5, waiting for transfers between devices, exchange(): lax.all_to_all(copies, ('wide', 'narrow'), 0, 0, tiled=True, axis_index_g...  14.3 us
    pallas_call x3, Pallas kernels, near_apply(): pl.pallas_call(functools.partial(near_kernel, evaluate), out_shape=out_sh...  14 us
    pallas_call x3, Pallas kernels, own_apply(): pl.pallas_call(functools.partial(own_kernel, evaluate), out_shape=out_sha...  12 us
    ppermute x3, starting transfers between devices, neighbours(): return lax.ppermute(fields, 'wide', across)  10.9 us
  transfers between devices with their start and end apart: 8, of which 4 were waited for; matrix products, arithmetic and copies ran while one was open for 1% of the time, Pallas kernels for 19%

profile of v6, /device:TPU:1, one launch (start us, length us, event | category | flops | bytes accessed | tf_op | source)
XLA Modules:
  0.0 147.9 jit_solution(7242848564837227446)
XLA Ops:
  0.6 0.0 copy-start
  0.6 2.1 %shard_map.176 = (f32[8,52,128]{2,1,0:T(8,128)}, f32[8,512]{1,0:T(8,128)S(1)}, bf16[3,64,512]{2,1,0:T(8,128)(2,1)S(1)}, bf16[3,64,64]{2,1,0:T(8,128)(2,1)S(1)}) custom-call(f32[3,512]{1,0:T(4,128)} %warm_in.1, f32[3,3,512]{2,1,0:T(4,128)} %refs_7_.1, bf16[3,64,512]{2,1,0:T(8,128)(2,1)} %bitcast.10, bf16[3,64,64]{2,1,0:T(8,128)(2,1)} %transfer_in.1), custom_call_target="tpu_custom_call" | custom-call | flops 1000000 | bytes 1000000 | tf_op jit(solution)/shard_map/pallas_call | solution.py:740
  2.8 10.2 %all-to-all-start = ((f32[8,52,128]{2,1,0:T(8,128)}), f32[8,52,128]{2,1,0:T(8,128)S(1)}, u32[]{:S(2)}, u32[]{:S(2)}) async-start(f32[8,52,128]{2,1,0:T(8,128)} %get-tuple-element.40), calls=%async_computation | async-start | bytes 458752 | tf_op jit(solution)/shard_map/all_to_all | solution.py:681
  13.0 0.0 copy-done
  13.0 0.4 constant_dynamic-slice_fusion
  13.4 0.5 copy.20.top_transfer.refs_6_
  13.9 6.0 %shard_map.177 = (f32[3,512,512]{2,1,0:T(8,128)}, f32[8,512]{1,0:T(8,128)S(1)}) custom-call(f32[8,512]{1,0:T(8,128)S(1)} %get-tuple-element.41.refs_0_.refs_4_.warm, f32[3,3,512]{2,1,0:T(4,128)} %refs_7_.1), custom_call_target="tpu_custom_call" | custom-call | flops 100000000 | bytes 4000000 | tf_op jit(solution)/shard_map/pallas_call | solution.py:522
  19.9 0.0 all-to-all-done.blocks.refs_2_
  19.9 0.9 shard_map.178
  20.8 11.9 %all-to-all-start.1 = ((f32[64,4,128]{2,1,0:T(4,128)}), f32[64,4,128]{2,1,0:T(4,128)S(1)}, u32[]{:S(2)}, u32[]{:S(2)}) async-start(f32[64,4,128]{2,1,0:T(4,128)} %get-tuple-element.43), calls=%async_computation.1 | async-start | bytes 262144 | tf_op jit(solution)/shard_map/all_to_all | solution.py:681
  32.7 3.4 %collective-permute-start = (f32[4,48,128]{2,1,0:T(8,128)S(1)}, f32[4,48,128]{2,1,0:T(8,128)S(1)}, u32[]{:S(2)}, u32[]{:S(2)}) collective-permute-start(f32[4,48,128]{2,1,0:T(8,128)S(1)} %get-tuple-element.44), channel_id=1, source_target_pairs={{4,8},{8,4},{12,16},{16,12},{20,24},{24,20},{28,32},{32,28},{36,40... | collective-permute-start | bytes 294920 | tf_op jit(solution)/shard_map/ppermute | solution.py:691
  36.1 1.7 %shard_map.179 = (f32[8,64]{1,0:T(8,128)S(1)}, bf16[16,256]{1,0:T(8,128)(2,1)S(1)}, bf16[4,64,64]{2,1,0:T(8,128)(2,1)S(1)}, f32[3,512]{1,0:T(4,128)S(1)}, bf16[3...) custom-call(f32[8,52,128]{2,1,0:T(8,128)S(1)} %all-to-all-done.blocks.refs_2_, ...), custom_call_target="tpu_custom_call" | custom-call | flops 10000000 | bytes 2000000 | tf_op jit(solution)/shard_map/pallas_call | solution.py:394
  37.8 2.3 %collective-permute-done.refs_3_ = f32[4,48,128]{2,1,0:T(8,128)S(1)} collective-permute-done((f32[4,48,128]{2,1,0:T(8,128)S(1)}, f32[4,48,128]{2,1,0:T(8,128)S(1)}, u32[]{:S(2)}, u32[]{:S(2)}) %collective-permute-start) | collective-permute-done | bytes 98336 | tf_op jit(solution)/shard_map/ppermute | solution.py:691
  40.0 7.7 %shard_map.180 = (f32[9,512,512]{2,1,0:T(8,128)}, f32[8,512]{1,0:T(8,128)S(1)}) custom-call(s32[3,4]{1,0:T(4,128)} %refs_0_.5, s32[3]{0:T(128)} %refs_1_.7, f32[8,52,128]{2,1,0:T(8,128)S(1)} %all-to-all-done.blocks.refs_2_, f32[4,48,128]{2,1,0:T(8,128)S(1)} %collective-permute-done.refs_3_, f32[8,512]{1,0:T(8,128)S(1)} %get-tuple-element.41.refs_0_.refs_4_.warm, ...), custom_call_target="tpu_custom_call" | custom-call | flops 300000000 | bytes 20000000 | tf_op jit(solution)/shard_map/pallas_call | solution.py:553
  47.7 0.0 all-to-all-done.1
  47.7 1.2 shard_map.181
  48.9 9.4 %all_to_all.40.blocks.refs_2_ = f32[8,16,128]{2,1,0:T(8,128)S(1)} all-to-all(f32[8,16,128]{2,1,0:T(8,128)S(1)} %get-tuple-element.54), channel_id=1, replica_groups={{0,1,2,3,4,5,6,7},{8,9,10,11,12,13,14,15},{16,17,18,19,20,21,22,23},{24..., dimensions={0} | all-to-all | bytes 131072 | tf_op jit(solution)/shard_map/all_to_all | solution.py:681
  58.3 0.9 shard_map.182
  59.1 12.7 %all-to-all-start.3 = ((f32[64,4,128]{2,1,0:T(4,128)}), f32[64,4,128]{2,1,0:T(4,128)S(1)}, u32[]{:S(2)}, u32[]{:S(2)}) async-start(f32[64,4,128]{2,1,0:T(4,128)} %get-tuple-element.55), calls=%async_computation.3 | async-start | bytes 262144 | tf_op jit(solution)/shard_map/all_to_all | solution.py:681
  71.9 3.8 %collective-permute-start.1 = (f32[4,12,128]{2,1,0:T(8,128)S(1)}, f32[4,12,128]{2,1,0:T(8,128)S(1)}, u32[]{:S(2)}, u32[]{:S(2)}) collective-permute-start(f32[4,12,128]{2,1,0:T(8,128)S(1)} %get-tuple-element.56), channel_id=1, source_target_pairs={{4,8},{8,4},{12,16},{16,12},{20,24},{24,20},{28,32},{32,28},{36,40... | collective-permute-start | bytes 73736 | tf_op jit(solution)/shard_map/ppermute | solution.py:691
  75.6 3.0 %shard_map.183 = (f32[8,512]{1,0:T(8,128)S(1)}, f32[8,64]{1,0:T(8,128)S(1)}, f32[3,512,512]{2,1,0:T(8,128)S(1)}) custom-call(f32[8,512]{1,0:T(8,128)S(1)} %get-tuple-element.57.refs_0_.refs_4_.refs_9_.residual, f32[3,512,512]{2,1,0:T(8,128)} %get-tuple-element.58.refs_1_, f32[8,16,128]{2,1,0:T(8,128)S(1)} %all_to_all.40.blocks.refs_2_, ...), custom_call_target="tpu_custom_call" | custom-call | flops 100000000 | bytes 4000000 | tf_op jit(solution)/shard_map/pallas_call | solution.py:522
  78.6 0.0 collective-permute-done.1.refs_3_
  78.6 3.2 %shard_map.184.refs_1_ = f32[8,512]{1,0:T(8,128)S(1)} custom-call(s32[3,4]{1,0:T(4,128)} %refs_0_.5, s32[3]{0:T(128)} %refs_1_.7, f32[8,16,128]{2,1,0:T(8,128)S(1)} %all_to_all.40.blocks.refs_2_, f32[4,12,128]{2,1,0:T(8,128)S(1)} %collective-permute-done.1.refs_3_, f32[8,512]{1,0:T(8,128)S(1)} %get-tuple-element.57.refs_0_.refs_4_.refs_9_.residual, ...), custom_call_target="tpu_custom_call" | custom-call | flops 300000000 | bytes 20000000 | tf_op jit(solution)/shard_map/pallas_call | solution.py:553
  81.8 1.6 %all-to-all-done.3 = f32[64,4,128]{2,1,0:T(4,128)S(1)} async-done(((f32[64,4,128]{2,1,0:T(4,128)}), f32[64,4,128]{2,1,0:T(4,128)S(1)}, u32[]{:S(2)}, u32[]{:S(2)}) %all-to-all-start.3) | async-done | bytes 131104 | tf_op jit(solution)/shard_map/all_to_all | solution.py:681
  83.4 1.2 shard_map.185
  84.6 9.4 %all_to_all.41.blocks.refs_2_ = f32[8,16,128]{2,1,0:T(8,128)S(1)} all-to-all(f32[8,16,128]{2,1,0:T(8,128)S(1)} %get-tuple-element.64), channel_id=1, replica_groups={{0,1,2,3,4,5,6,7},{8,9,10,11,12,13,14,15},{16,17,18,19,20,21,22,23},{24..., dimensions={0} | all-to-all | bytes 131072 | tf_op jit(solution)/shard_map/all_to_all | solution.py:681
  94.1 0.9 shard_map.186
  94.9 9.2 %all-to-all-start.5 = ((f32[64,4,128]{2,1,0:T(4,128)}), f32[64,4,128]{2,1,0:T(4,128)S(1)}, u32[]{:S(2)}, u32[]{:S(2)}) async-start(f32[64,4,128]{2,1,0:T(4,128)} %get-tuple-element.65), calls=%async_computation.5 | async-start | bytes 262144 | tf_op jit(solution)/shard_map/all_to_all | solution.py:681
  104.2 3.8 %collective-permute-start.2 = (f32[4,12,128]{2,1,0:T(8,128)S(1)}, f32[4,12,128]{2,1,0:T(8,128)S(1)}, u32[]{:S(2)}, u32[]{:S(2)}) collective-permute-start(f32[4,12,128]{2,1,0:T(8,128)S(1)} %get-tuple-element.66), channel_id=1, source_target_pairs={{4,8},{8,4},{12,16},{16,12},{20,24},{24,20},{28,32},{32,28},{36,40... | collective-permute-start | bytes 73736 | tf_op jit(solution)/shard_map/ppermute | solution.py:691
  107.9 3.0 %shard_map.187 = (f32[8,512]{1,0:T(8,128)S(1)}, f32[8,64]{1,0:T(8,128)S(1)}, f32[3,512,512]{2,1,0:T(8,128)S(1)}) custom-call(f32[8,512]{1,0:T(8,128)S(1)} %get-tuple-element.67.refs_0_.refs_4_, f32[3,512,512]{2,1,0:T(8,128)} %get-tuple-element.58.refs_1_, f32[8,16,128]{2,1,0:T(8,128)S(1)} %all_to_all.41.blocks.refs_2_, ...), custom_call_target="tpu_custom_call" | custom-call | flops 100000000 | bytes 4000000 | tf_op jit(solution)/shard_map/pallas_call | solution.py:522
  110.9 0.0 collective-permute-done.2.refs_3_
  110.9 3.2 %shard_map.188.refs_1_ = f32[8,512]{1,0:T(8,128)S(1)} custom-call(s32[3,4]{1,0:T(4,128)} %refs_0_.5, s32[3]{0:T(128)} %refs_1_.7, f32[8,16,128]{2,1,0:T(8,128)S(1)} %all_to_all.41.blocks.refs_2_, f32[4,12,128]{2,1,0:T(8,128)S(1)} %collective-permute-done.2.refs_3_, f32[8,512]{1,0:T(8,128)S(1)} %get-tuple-element.67.refs_0_.refs_4_, ...), custom_call_target="tpu_custom_call" | custom-call | flops 300000000 | bytes 20000000 | tf_op jit(solution)/shard_map/pallas_call | solution.py:553
  114.1 1.6 %all-to-all-done.5 = f32[64,4,128]{2,1,0:T(4,128)S(1)} async-done(((f32[64,4,128]{2,1,0:T(4,128)}), f32[64,4,128]{2,1,0:T(4,128)S(1)}, u32[]{:S(2)}, u32[]{:S(2)}) %all-to-all-start.5) | async-done | bytes 131104 | tf_op jit(solution)/shard_map/all_to_all | solution.py:681
  115.7 1.0 shard_map.189
  116.7 9.4 %all_to_all.42.blocks = f32[8,8,128]{2,1,0:T(8,128)S(1)} all-to-all(f32[8,8,128]{2,1,0:T(8,128)S(1)} %get-tuple-element.73), channel_id=1, replica_groups={{0,1,2,3,4,5,6,7},{8,9,10,11,12,13,14,15},{16,17,18,19,20,21,22,23},{24..., dimensions={0} | all-to-all | bytes 65536 | tf_op jit(solution)/shard_map/all_to_all | solution.py:681
  126.1 0.6 shard_map.190
  126.8 9.2 %all-to-all-start.7 = ((f32[64,2,128]{2,1,0:T(2,128)}), f32[64,2,128]{2,1,0:T(2,128)S(1)}, u32[]{:S(2)}, u32[]{:S(2)}) async-start(f32[64,2,128]{2,1,0:T(2,128)} %shard_map.190), calls=%async_computation.7 | async-start | bytes 131072 | tf_op jit(solution)/shard_map/all_to_all | solution.py:681
  136.0 11.1 %all-to-all-done.7.blocks = f32[64,2,128]{2,1,0:T(2,128)S(1)} async-done(((f32[64,2,128]{2,1,0:T(2,128)}), f32[64,2,128]{2,1,0:T(2,128)S(1)}, u32[]{:S(2)}, u32[]{:S(2)}) %all-to-all-start.7) | async-done | bytes 65568 | tf_op jit(solution)/shard_map/all_to_all | solution.py:681
  147.1 0.9 shard_map.192
  (1 shorter events, 0.0 us)
Async XLA Ops:
  0.6 12.4 %copy-start = (bf16[128,64,64]{0,2,1:T(8,128)(2,1)S(1)}, bf16[128,64,64]{0,2,1:T(8,128)(2,1)}, u32[]{:S(2)}) copy-start(bf16[128,64,64]{0,2,1:T(8,128)(2,1)} %param.25) | copy-start | bytes 3145732
  2.8 17.1 %all-to-all-start = ((f32[8,52,128]{2,1,0:T(8,128)}), f32[8,52,128]{2,1,0:T(8,128)S(1)}, u32[]{:S(2)}, u32[]{:S(2)}) async-start(f32[8,52,128]{2,1,0:T(8,128)} %get-tuple-element.40), calls=%async_computation | async-start | bytes 458752 | tf_op jit(solution)/shard_map/all_to_all | solution.py:681
  20.8 26.9 %all-to-all-start.1 = ((f32[64,4,128]{2,1,0:T(4,128)}), f32[64,4,128]{2,1,0:T(4,128)S(1)}, u32[]{:S(2)}, u32[]{:S(2)}) async-start(f32[64,4,128]{2,1,0:T(4,128)} %get-tuple-element.43), calls=%async_computation.1 | async-start | bytes 262144 | tf_op jit(solution)/shard_map/all_to_all | solution.py:681
  32.7 7.3 %collective-permute-start = (f32[4,48,128]{2,1,0:T(8,128)S(1)}, f32[4,48,128]{2,1,0:T(8,128)S(1)}, u32[]{:S(2)}, u32[]{:S(2)}) collective-permute-start(f32[4,48,128]{2,1,0:T(8,128)S(1)} %get-tuple-element.44), channel_id=1, source_target_pairs={{4,8},{8,4},{12,16},{16,12},{20,24},{24,20},{28,32},{32,28},{36,40... | collective-permute-start | bytes 294920 | tf_op jit(solution)/shard_map/ppermute | solution.py:691
  59.1 24.3 %all-to-all-start.3 = ((f32[64,4,128]{2,1,0:T(4,128)}), f32[64,4,128]{2,1,0:T(4,128)S(1)}, u32[]{:S(2)}, u32[]{:S(2)}) async-start(f32[64,4,128]{2,1,0:T(4,128)} %get-tuple-element.55), calls=%async_computation.3 | async-start | bytes 262144 | tf_op jit(solution)/shard_map/all_to_all | solution.py:681
  71.9 6.8 %collective-permute-start.1 = (f32[4,12,128]{2,1,0:T(8,128)S(1)}, f32[4,12,128]{2,1,0:T(8,128)S(1)}, u32[]{:S(2)}, u32[]{:S(2)}) collective-permute-start(f32[4,12,128]{2,1,0:T(8,128)S(1)} %get-tuple-element.56), channel_id=1, source_target_pairs={{4,8},{8,4},{12,16},{16,12},{20,24},{24,20},{28,32},{32,28},{36,40... | collective-permute-start | bytes 73736 | tf_op jit(solution)/shard_map/ppermute | solution.py:691
  94.9 20.8 %all-to-all-start.5 = ((f32[64,4,128]{2,1,0:T(4,128)}), f32[64,4,128]{2,1,0:T(4,128)S(1)}, u32[]{:S(2)}, u32[]{:S(2)}) async-start(f32[64,4,128]{2,1,0:T(4,128)} %get-tuple-element.65), calls=%async_computation.5 | async-start | bytes 262144 | tf_op jit(solution)/shard_map/all_to_all | solution.py:681
  104.2 6.8 %collective-permute-start.2 = (f32[4,12,128]{2,1,0:T(8,128)S(1)}, f32[4,12,128]{2,1,0:T(8,128)S(1)}, u32[]{:S(2)}, u32[]{:S(2)}) collective-permute-start(f32[4,12,128]{2,1,0:T(8,128)S(1)} %get-tuple-element.66), channel_id=1, source_target_pairs={{4,8},{8,4},{12,16},{16,12},{20,24},{24,20},{28,32},{32,28},{36,40... | collective-permute-start | bytes 73736 | tf_op jit(solution)/shard_map/ppermute | solution.py:691
  126.8 20.3 %all-to-all-start.7 = ((f32[64,2,128]{2,1,0:T(2,128)}), f32[64,2,128]{2,1,0:T(2,128)S(1)}, u32[]{:S(2)}, u32[]{:S(2)}) async-start(f32[64,2,128]{2,1,0:T(2,128)} %shard_map.190), calls=%async_computation.7 | async-start | bytes 131072 | tf_op jit(solution)/shard_map/all_to_all | solution.py:681
